TPU v7x, 256 devices: a whole 4x4x8 slice. The times are simulated.
256 devices in a mesh: win: 4 (over y), pair: 64 (over x, z, core).
Axes of the slice: x: 4, y: 4, z: 8, core: 2. Of those that a mesh axis runs over, the one named last changes fastest.
Arguments:
- spectra: bfloat16 [512, 4, 2, 32, 1024], P('pair', 'win')
- send_blocks: int32 [64, 64, 2], P('pair'), may hold values from 0 to 7, as said below
- tile_slots: int32 [256, 2], P('pair'), may hold values from 0 to 127, as said below
Outputs:
- correlations: bfloat16 [32, 256, 32, 1024], P('win', 'pair')
Inputs may be any that keep to these rules, and one draw needn't show every extreme that they name: `send_blocks`: entry [s, d, k] names the block, counted within pair index s, that s sends to owner d in slot k; the 2 slots of one s and d name different blocks. `tile_slots`: row t belongs to owner t // 4; an entry r stands for slot r % 2 of what pair index r // 2 sends to that owner. The second entry of a row lies 1 to 2 slots after or before the first, so the two blocks of a tile are different and lie on the same or neighbouring pair indices.
All inputs are finite; a program needn't handle non-finite values.
Results may differ from a plain program's by a relative error of at most 0.0068.
Values may be sent and summed in bfloat16 or wider, within the bound.
No kernel may reach another device: no remote copies, remote signals or barrier semaphores. Data moves between devices by JAX's collectives and lax.ppermute only.
A program may use at most 320 MiB of HBM per device.

v0:
```python
import math

import jax
import jax.numpy as jnp
from jax import lax
from jax.sharding import PartitionSpec as P

LAGS = 1024
NS = 4096
F0 = 64
BAND = 64


def whiten(spectral):
    whole_shape = spectral.shape
    band_count = whole_shape[-1] // BAND
    widened = spectral.astype(jnp.float32).reshape(whole_shape[:-1] + (band_count, BAND))
    band_power = jnp.mean(widened * widened, axis=(-4, -1), keepdims=True)
    return (widened * lax.rsqrt(band_power + 1e-06)).reshape(whole_shape).astype(jnp.bfloat16)


def lag_rows_table(bin_total):
    bin_index = jnp.arange(bin_total, dtype=jnp.int32) + F0
    lag_index = jnp.arange(LAGS, dtype=jnp.int32) - LAGS // 2
    wrapped = bin_index[:, None] * lag_index[None, :] % NS
    phases = wrapped.astype(jnp.float32) * (2.0 * math.pi / NS)
    return jnp.concatenate([jnp.cos(phases), -jnp.sin(phases)], axis=0).astype(jnp.bfloat16)


def cross_stack(first_rows, second_rows):
    swapped = jnp.stack([first_rows[:, :, 1], -first_rows[:, :, 0]], axis=2)
    paired = jnp.stack([first_rows, swapped], axis=0)
    return jnp.einsum(
        "stwcif,twcjf->itjsf", paired, second_rows, preferred_element_type=jnp.float32
    )


def local(spectra, send_blocks, tile_slots):
    pair_count = lax.axis_size("pair")
    capacity = send_blocks.shape[2]
    panel_shape = spectra.shape[1:]
    outgoing = whiten(spectra)
    picked_blocks = jnp.take(outgoing, send_blocks[0].reshape(-1), axis=0)
    parcels = picked_blocks.reshape((pair_count, capacity) + panel_shape)
    arrived = lax.all_to_all(parcels, "pair", split_axis=0, concat_axis=0, tiled=True)
    arrived = arrived.reshape((pair_count * capacity,) + panel_shape)
    first_panels = jnp.take(arrived, tile_slots[:, 0], axis=0)
    second_panels = jnp.take(arrived, tile_slots[:, 1], axis=0)
    row_quarters = lax.all_to_all(first_panels, "win", split_axis=3, concat_axis=1, tiled=True)
    all_windows = lax.all_gather(second_panels, "win", axis=1, tiled=True)
    cross_terms = cross_stack(row_quarters, all_windows)
    stacked = cross_terms.astype(jnp.bfloat16)
    bin_total = spectra.shape[-1]
    windows_all = spectra.shape[1] * lax.axis_size("win")
    flattened = stacked.reshape(-1, 2 * bin_total)
    lagged = jnp.dot(flattened, lag_rows_table(bin_total), preferred_element_type=jnp.float32)
    lagged = lagged * (1.0 / math.sqrt(windows_all * bin_total))
    return lagged.reshape(stacked.shape[:3] + (LAGS,)).astype(jnp.bfloat16)


def solution(mesh):
    in_specs = (P("pair", "win", None, None, None), P("pair", None, None), P("pair", None))
    out_specs = P("win", "pair", None, None)
    return jax.shard_map(local, mesh=mesh, in_specs=in_specs, out_specs=out_specs, check_vma=False)
```

profile of v0, /device:TPU:1, one launch (start us, length us, event | category | flops | bytes accessed | tf_op | source)
XLA Modules:
  0.0 556.1 jit_solution(5962070551640169722)
XLA Ops:
  6.5 0.8 copy.34
  7.3 0.7 compare_and_fusion.2
  8.0 1.6 fusion.16
  9.6 0.6 reduce_sum.14
  10.1 0.6 reduce_sum.18
  10.8 0.6 mul.56
  11.4 0.6 mul.57
  12.0 1.5 fusion.18
  13.5 0.1 reshape_squeeze.6
  13.7 0.1 copy.33
  13.8 8.2 %gather_fusion = bf16[128,2,32,1024]{3,2,1,0:T(8,128)(2,1)} fusion(bf16[8,2,32,1024]{3,2,1,0:T(8,128)(2,1)S(1)} %fusion.18, s32[1024]{0:T(1024)S(1)} %pad_clamp_fusion.2), kind=kCustom, calls=%fused_computation.2 | custom fusion | bytes 33554944 | tf_op jit(solution)/shard_map/jit(_take)/gather | solution.py:43
  22.0 14.1 %broadcast_select_fusion = bf16[64,2,1,2,32,1024]{5,4,3,1,2,0:T(8,128)(2,1)} fusion(bf16[64,2,1,2,32,1024]{5,4,3,1,2,0:T(8,128)(2,1)} %bitcast.50, pred[64,2]{1,0:T(8,128)(4,1)S(1)} %copy.33), kind=kLoop, calls=%fused_computation.9 | loop fusion | flops 8388608 | bytes 33554560 | tf_op jit(solution)/shard_map/jit(_take)/select_n | solution.py:43
  36.2 0.0 copy-start.1
  36.2 13.3 %all-to-all-start = ((bf16[64,2,1,2,32,1024]{5,4,3,1,2,0:T(8,128)(2,1)}), bf16[64,2,1,2,32,1024]{5,4,3,1,2,0:T(8,128)(2,1)}, u32[]{:S(2)}, u32[]{:S(2)}) async-start(bf16[64,2,1,2,32,1024]{5,4,3,1,2,0:T(8,128)(2,1)} %broadcast_select_fusion), calls=%async_computation | async-start | bytes 33554432 | tf_op jit(solution)/shard_map/all_to_all | solution.py:45
  49.5 0.0 all-gather.2.cloned.1.call-start
  49.5 0.0 copy-done.1
  49.6 365.4 %all-to-all-done = bf16[64,2,1,2,32,1024]{5,4,3,1,2,0:T(8,128)(2,1)} async-done(((bf16[64,2,1,2,32,1024]{5,4,3,1,2,0:T(8,128)(2,1)}), bf16[64,2,1,2,32,1024]{5,4,3,1,2,0:T(8,128)(2,1)}, u32[]{:S(2)}, u32[]{:S(2)}) %all-to-all-start) | async-done | bytes 16777248 | tf_op jit(solution)/shard_map/all_to_all | solution.py:45
  415.0 6.3 %gather_fusion.1 = bf16[4,2,32,1024]{3,2,1,0:T(8,128)(2,1)S(1)} fusion(bf16[128,2,32,1024]{3,2,1,0:T(8,128)(2,1)} %bitcast.6, s32[1024]{0:T(1024)S(1)} %pad_clamp_fusion.1), kind=kCustom, calls=%fused_computation.clone | custom fusion | bytes 1048592 | tf_op jit(solution)/shard_map/jit(_take)/gather | solution.py:48
  421.4 0.9 bitcast_select_fusion.1
  422.3 0.0 all-gather.2.cloned.1.call-update
  422.3 6.3 %gather_fusion.2 = bf16[4,2,32,1024]{3,2,1,0:T(8,128)(2,1)S(1)} fusion(bf16[128,2,32,1024]{3,2,1,0:T(8,128)(2,1)} %bitcast.6, s32[1024]{0:T(1024)S(1)} %pad_clamp_fusion), kind=kCustom, calls=%fused_computation.1.clone | custom fusion | bytes 1048592 | tf_op jit(solution)/shard_map/jit(_take)/gather | solution.py:47
  428.7 0.1 bitcast_select_fusion
  428.8 1.4 copy.35
  430.2 4.2 all-to-all-start.1
  434.4 18.8 %cosine_convert_fusion = (bf16[1024,1024]{1,0:T(8,128)(2,1)S(1)}, bf16[1024,1024]{1,0:T(8,128)(2,1)}) fusion(s32[1024]{0:T(1024)S(1)} %get-tuple-element.16, s32[1024]{0:T(1024)S(1)} %get-tuple-element.17), kind=kLoop, calls=%fused_computation.26 | loop fusion | flops 17825792 | bytes 4202496 | tf_op jit(solution)/shard_map/convert
  453.2 0.0 all-to-all-done.1
  453.2 9.2 %copy.37 = bf16[4,1,2,4,8,1024]{4,3,2,5,0,1:T(4,128)(2,1)} copy(bf16[4,1,2,4,8,1024]{5,2,0,4,3,1:T(2,128)(2,1)S(1)} %bitcast.56) | data formatting | bytes 1048576 | tf_op jit(solution)/shard_map/all_to_all | solution.py:49
  462.3 5.7 %fusion.22 = (bf16[4,4,1,8,1024]{3,1,2,4,0:T(4,128)(2,1)S(1)}, bf16[4,4,1,8,1024]{3,1,2,4,0:T(4,128)(2,1)S(1)}) fusion(bf16[4,4,2,8,1024]{3,1,2,4,0:T(4,128)(2,1)} %bitcast.51), kind=kLoop, calls=%fused_computation.50 | loop fusion | flops 131072 | bytes 1048576 | tf_op jit(solution)/shard_map/slice | solution.py:31
  468.0 8.2 %maximum_bitcast_fusion = bf16[1,4,4,2,8,1024]{4,2,3,0,5,1:T(4,128)(2,1)} fusion(bf16[4,4,1,8,1024]{3,1,2,4,0:T(4,128)(2,1)S(1)} %get-tuple-element.11, bf16[4,4,1,8,1024]{3,1,2,4,0:T(4,128)(2,1)S(1)} %get-tuple-element.10), kind=kLoop, calls=%fused_computation.10 | loop fusion | flops 262144 | bytes 1048576 | tf_op jit(solution)/shard_map/stack | solution.py:32
  476.2 0.0 all-gather.2.cloned.1.call-done
  476.3 12.4 %copy.41 = bf16[4,4,2,32,1024,1]{3,1,2,5,4,0:T(4,128)(2,1)} copy(bf16[4,4,2,32,1024,1]{4,3,2,0,1,5:T(8,128)(2,1)} %bitcast.55) | data formatting | bytes 4194304 | tf_op jit(solution)/shard_map/all_gather | solution.py:50
  488.7 24.5 %fusion = bf16[8,4,32,2,1024]{2,0,3,4,1:T(8,128)(2,1)} fusion(bf16[4,4,2,32,1024,1]{3,1,2,5,4,0:T(4,128)(2,1)} %copy.41, bf16[1,4,4,2,8,1024]{4,2,3,0,5,1:T(4,128)(2,1)} %maximum_bitcast_fusion, bf16[1,4,4,2,8,1024]{4,2,3,0,5,1:T(4,128)(2,1)} %bitcast.52), kind=kOutput, calls=%fused_computation.4 | convolution fusion | flops 37748736 | bytes 7340032 | tf_op jit(solution)/shard_map/stwcif,twcjf->itjsf/dot_general | solution.py:33
  513.2 26.6 %copy.40 = bf16[8,4,32,2,1024]{4,3,2,1,0:T(2,128)(2,1)} copy(bf16[8,4,32,2,1024]{2,0,3,4,1:T(8,128)(2,1)} %fusion) | data formatting | bytes 8388608 | tf_op jit(solution)/shard_map/convert_element_type | solution.py:52
  539.8 0.0 copy-start
  539.8 3.8 copy.47
  543.5 0.0 copy-done
  543.5 5.7 %multiply_convert_fusion = bf16[1024,1024]{1,0:T(8,128)(2,1)} fusion(bf16[1024,2048]{1,0:T(8,128)(2,1)S(1)} %bitcast.54, bf16[1024,1024]{1,0:T(8,128)(2,1)S(1)} %copy-done, bf16[1024,1024]{1,0:T(8,128)(2,1)S(1)} %get-tuple-element.12), kind=kOutput, calls=%fused_computation.24 | convolution fusion | flops 4305453056 | bytes 10485760 | tf_op jit(solution)/shard_map/dot_general | solution.py:56
  (7 shorter events, 0.1 us)
Async XLA Ops:
  36.2 13.4 %copy-start.1 = (s32[4,2]{0,1:T(2,128)S(1)}, s32[4,2]{0,1:T(2,128)}, u32[]{:S(2)}) copy-start(s32[4,2]{0,1:T(2,128)} %param.7) | copy-start | bytes 100
  36.2 378.9 %all-to-all-start = ((bf16[64,2,1,2,32,1024]{5,4,3,1,2,0:T(8,128)(2,1)}), bf16[64,2,1,2,32,1024]{5,4,3,1,2,0:T(8,128)(2,1)}, u32[]{:S(2)}, u32[]{:S(2)}) async-start(bf16[64,2,1,2,32,1024]{5,4,3,1,2,0:T(8,128)(2,1)} %broadcast_select_fusion), calls=%async_computation | async-start | bytes 33554432 | tf_op jit(solution)/shard_map/all_to_all | solution.py:45
  49.5 426.8 %all-gather.2.cloned.1.call-start = ((), (), s32[]{:S(2)}) async-start(), calls=%async_computation.2 | async-start | bytes 2621440 | tf_op jit(solution)/shard_map/all_gather | solution.py:50
  430.2 23.0 %all-to-all-start.1 = ((bf16[4,1,2,32,1024]{4,2,0,1,3:T(2,128)(2,1)}), bf16[4,1,2,32,1024]{4,2,0,1,3:T(2,128)(2,1)S(1)}, u32[]{:S(2)}, u32[]{:S(2)}) async-start(bf16[4,1,2,32,1024]{4,2,0,1,3:T(2,128)(2,1)} %copy.35), calls=%async_computation.1 | async-start | bytes 1048576 | tf_op jit(solution)/shard_map/all_to_all | solution.py:49
  539.8 3.8 copy-start
Sparse Core Ops, SparseCore 0:
  422.4 35.9 all-gather.1
where the time goes:
time: 557 us; the launch traced here: 556 us
  waiting for transfers between devices  365 us (66%)
  local copies, waits for them, and re-layouts  77 us (14%)
  other arithmetic  52.3 us (9%)
  matrix products  30.2 us (5%)
  starting transfers between devices  17.5 us (3%)
  between operations  13.5 us (2%)
    all_to_all x1, waiting for transfers between devices, local(): lax.all_to_all(parcels, 'pair', split_axis=0, concat_axis=0, tiled=True)  365 us
    convert_element_type x1, local copies, waits for them, and re-layouts, local(): stacked = cross_terms.astype(jnp.bfloat16)  26.6 us
    dot_general x1, matrix products, cross_stack(): jnp.einsum('stwcif,twcjf->itjsf', paired, second_rows, preferred_element_...  24.5 us
    another operation x1, other arithmetic  18.8 us
    select_n x2, other arithmetic, local(): picked_blocks = jnp.take(outgoing, send_blocks[0].reshape(-1), axis=0)  14.1 us
    all_to_all x1, starting transfers between devices, local(): lax.all_to_all(parcels, 'pair', split_axis=0, concat_axis=0, tiled=True)  13.3 us
    all_gather x1, local copies, waits for them, and re-layouts, local(): all_windows = lax.all_gather(second_panels, 'win', axis=1, tiled=True)  12.4 us
  transfers between devices with their start and end apart: 3, of which 1 were waited for; matrix products, arithmetic and copies ran while one was open for 9% of the time, Pallas kernels for 0%

commit v1 on v0

v1 whole, which is shorter than its diff:
```python
import functools
import math

import jax
import jax.numpy as jnp
from jax import lax
from jax.experimental import pallas as pl
from jax.experimental.pallas import tpu as pltpu
from jax.sharding import PartitionSpec as P

LAGS = 1024
NS = 4096
F0 = 64
BAND = 64
LANES = 128
GROUP = 8


def whiten_kernel(x_ref, out_ref):
    blocks, bins = x_ref.shape[0], x_ref.shape[-1]
    lane_groups = bins // LANES
    row_band = lax.broadcasted_iota(jnp.int32, (LANES, LANES), 0) // BAND
    column_band = lax.broadcasted_iota(jnp.int32, (LANES, LANES), 1) // BAND
    ones = jnp.where(row_band == column_band, 1.0 / (2 * BAND), 0.0).astype(jnp.float32)
    for block in range(blocks):
        for lane_group in range(lane_groups):
            lanes = slice(lane_group * LANES, (lane_group + 1) * LANES)
            real = x_ref[block, 0, 0, :, lanes].astype(jnp.float32)
            imag = x_ref[block, 0, 1, :, lanes].astype(jnp.float32)
            power = jnp.dot(
                real * real + imag * imag,
                ones,
                precision=lax.Precision.HIGHEST,
                preferred_element_type=jnp.float32,
            )
            scale = lax.rsqrt(power + 1e-06)
            for part, rows in enumerate((real * scale, imag * scale)):
                for half in range(2):
                    piece = rows[half * GROUP : (half + 1) * GROUP].astype(jnp.bfloat16)
                    out_ref[(half * 2 + part) * lane_groups + lane_group, block] = piece


def whiten_spread(spectra):
    blocks, _, parts, channels, bins = spectra.shape
    pieces = parts * channels * bins // (GROUP * LANES)
    steps = channels // 16
    return pl.pallas_call(
        whiten_kernel,
        grid=(steps,),
        in_specs=[pl.BlockSpec((blocks, 1, parts, 16, bins), lambda g: (0, 0, 0, g, 0))],
        out_specs=pl.BlockSpec((pieces // steps, blocks, GROUP, LANES), lambda g: (g, 0, 0, 0)),
        out_shape=jax.ShapeDtypeStruct((pieces, blocks, GROUP, LANES), jnp.bfloat16),
        compiler_params=pltpu.CompilerParams(vmem_limit_bytes=24 * 2**20),
        name="whiten_spread",
    )(spectra)


def pick_kernel(index_ref, x_ref, first_ref, second_ref):
    owners, tiles = first_ref.shape[:2]

    def one_owner(owner, carry):
        for tile in range(tiles):
            base = (owner * tiles + tile) * 2
            first_ref[owner, tile] = x_ref[index_ref[base]]
            second_ref[owner, tile] = x_ref[index_ref[base + 1]]
        return carry

    lax.fori_loop(0, owners, one_owner, 0)


def pick(index, spread, owners, tiles):
    shape = jax.ShapeDtypeStruct((owners, tiles, GROUP, LANES), jnp.bfloat16)
    return pl.pallas_call(
        pick_kernel,
        in_specs=[
            pl.BlockSpec(memory_space=pltpu.SMEM),
            pl.BlockSpec(memory_space=pltpu.VMEM),
        ],
        out_specs=[pl.BlockSpec(memory_space=pltpu.VMEM)] * 2,
        out_shape=[shape, shape],
        compiler_params=pltpu.CompilerParams(vmem_limit_bytes=24 * 2**20),
        name="pick_blocks",
    )(index, spread)


def correlate_kernel(scaling, a_ref, b_ref, table_ref, out_ref, stack_ref):
    tile = pl.program_id(0)
    windows, _, lane_groups = a_ref.shape[:3]
    groups = b_ref.shape[1]
    bins = lane_groups * LANES
    channels = groups * GROUP

    def one_lane_group(lane_group, carry):
        lanes = pl.multiple_of(lane_group * LANES, LANES)
        a = [
            [a_ref[w, part, lane_group, tile].astype(jnp.float32) for part in range(2)]
            for w in range(windows)
        ]
        for pair in range(groups // 2):
            b = [
                [
                    [
                        b_ref[w, pair * 2 + half, part, lane_group, tile].astype(jnp.float32)
                        for part in range(2)
                    ]
                    for w in range(windows)
                ]
                for half in range(2)
            ]
            for i in range(GROUP):
                rows = [[None, None], [None, None]]
                for w in range(windows):
                    a0 = jnp.broadcast_to(a[w][0][i : i + 1], (GROUP, LANES))
                    a1 = jnp.broadcast_to(a[w][1][i : i + 1], (GROUP, LANES))
                    for half in range(2):
                        b0, b1 = b[half][w]
                        real = a0 * b0 + a1 * b1
                        imag = a1 * b0 - a0 * b1
                        if w:
                            real += rows[half][0]
                            imag += rows[half][1]
                        rows[half] = [real, imag]
                start = i * channels + pair * 2 * GROUP
                for part in range(2):
                    joined = jnp.concatenate([rows[0][part], rows[1][part]], axis=0)
                    stack_ref[
                        start : start + 2 * GROUP, pl.ds(part * bins + lanes, LANES)
                    ] = joined.astype(jnp.bfloat16)
        return carry

    lax.fori_loop(0, lane_groups, one_lane_group, 0)
    lagged = jnp.dot(stack_ref[...], table_ref[...], preferred_element_type=jnp.float32)
    lagged = (lagged * scaling).astype(jnp.bfloat16)
    out_ref[...] = lagged.reshape(out_ref.shape)


def correlate(a, b, table):
    windows, _, lane_groups, tiles = a.shape[:4]
    channels = b.shape[1] * GROUP
    bins = lane_groups * LANES
    lags = table.shape[1]
    scaling = 1.0 / math.sqrt(windows * bins)
    return pl.pallas_call(
        functools.partial(correlate_kernel, scaling),
        grid=(tiles,),
        in_specs=[
            pl.BlockSpec(a.shape, lambda t: (0,) * 6),
            pl.BlockSpec(b.shape, lambda t: (0,) * 7),
            pl.BlockSpec(table.shape, lambda t: (0, 0)),
        ],
        out_specs=pl.BlockSpec((GROUP, 1, channels, lags), lambda t: (0, t, 0, 0)),
        out_shape=jax.ShapeDtypeStruct((GROUP, tiles, channels, lags), jnp.bfloat16),
        scratch_shapes=[pltpu.VMEM((GROUP * channels, 2 * bins), jnp.bfloat16)],
        compiler_params=pltpu.CompilerParams(vmem_limit_bytes=48 * 2**20),
        name="correlate",
    )(a, b, table)


def lag_rows_table(bin_total):
    bin_index = jnp.arange(bin_total, dtype=jnp.int32) + F0
    lag_index = jnp.arange(LAGS, dtype=jnp.int32) - LAGS // 2
    wrapped = bin_index[:, None] * lag_index[None, :] % NS
    phases = wrapped.astype(jnp.float32) * (2.0 * math.pi / NS)
    return jnp.concatenate([jnp.cos(phases), -jnp.sin(phases)], axis=0).astype(jnp.bfloat16)


def block_index(send_blocks, tile_slots, blocks):
    owners, capacity = send_blocks.shape[1:]
    tiles = tile_slots.shape[0]
    mine = jnp.concatenate([send_blocks.reshape(-1), tile_slots.reshape(-1)])
    tables = lax.all_gather(mine, "pair", axis=0, tiled=False)
    sent = tables[:, : owners * capacity].reshape(owners, owners, capacity)
    slots = tables[:, owners * capacity :]
    sent = sent + blocks * jnp.arange(owners, dtype=jnp.int32)[:, None, None]
    by_owner = jnp.transpose(sent, (1, 0, 2)).reshape(owners, 1, owners * capacity)
    chosen = slots[:, :, None] == jnp.arange(owners * capacity, dtype=jnp.int32)
    return jnp.sum(jnp.where(chosen, by_owner, 0), axis=-1).reshape(owners * tiles * 2)


def local(spectra, send_blocks, tile_slots):
    owners = lax.axis_size("pair")
    windows = lax.axis_size("win")
    blocks, _, parts, channels, bins = spectra.shape
    tiles = tile_slots.shape[0]
    lane_groups = bins // LANES
    index = block_index(send_blocks, tile_slots, blocks)
    outgoing = whiten_spread(spectra)
    spread = lax.all_to_all(outgoing, "pair", split_axis=0, concat_axis=0, tiled=True)
    spread = spread.reshape(owners * blocks, GROUP, LANES)
    first, second = pick(index, spread, owners, tiles)
    second = lax.all_to_all(second, "pair", split_axis=0, concat_axis=0, tiled=True)
    all_second = lax.all_gather(second, "win", axis=0, tiled=False)
    first = lax.all_to_all(first, "pair", split_axis=0, concat_axis=0, tiled=True)
    all_first = lax.all_to_all(first, "win", split_axis=0, concat_axis=0, tiled=True)
    a = all_first.reshape(windows, parts, lane_groups, tiles, GROUP, LANES)
    b = all_second.reshape(windows, channels // GROUP, parts, lane_groups, tiles, GROUP, LANES)
    return correlate(a, b, lag_rows_table(bins))


def solution(mesh):
    in_specs = (P("pair", "win", None, None, None), P("pair", None, None), P("pair", None))
    out_specs = P("win", "pair", None, None)
    return jax.shard_map(local, mesh=mesh, in_specs=in_specs, out_specs=out_specs, check_vma=False)
```

time: 557 us -> 389 us (0.70)
  waiting for transfers between devices: 365 us -> 17.3 us
  blocking collectives: 0 us -> 285 us
  local copies, waits for them, and re-layouts: 77 us -> 4.36 us
  other arithmetic: 52.3 us -> 21.2 us
  matrix products: 30.2 us -> 0 us
  Pallas kernels: 0 us -> 23.3 us
  starting transfers between devices: 17.5 us -> 23.8 us
    all_to_all x2 -> x3, waiting for transfers between devices: 365 us -> 17.2 us  [the longest x1 17.2 us: local(): lax.all_to_all(first, 'pair', split_axis=0, concat_axis=0, tiled=True)]
    unnamed x0 -> x1, blocking collectives: none -> 258 us
    dot_general x2 -> x0, matrix products: 30.2 us -> none  [the longest x1 24.5 us: cross_stack(): jnp.einsum('stwcif,twcjf->itjsf', paired, second_rows, preferred_element_...]
    all_to_all x0 -> x1, blocking collectives: none -> 26.9 us  [local(): lax.all_to_all(second, 'pair', split_axis=0, concat_axis=0, tiled=True)]
    convert_element_type x1 -> x0, local copies, waits for them, and re-layouts: 26.6 us -> none  [local(): stacked = cross_terms.astype(jnp.bfloat16)]
    pallas_call x0 -> x3, Pallas kernels: none -> 23.3 us  [the longest x1 13.4 us: correlate(): pl.pallas_call(functools.partial(correlate_kernel, scaling), grid=(tiles,...]
    gather x3 -> x0, local copies, waits for them, and re-layouts: 20.9 us -> none  [the longest x1 8.24 us: local(): picked_blocks = jnp.take(outgoing, send_blocks[0].reshape(-1), axis=0)]
    select_n x4 -> x0, other arithmetic: 15.2 us -> none  [the longest x2 14.1 us: local(): picked_blocks = jnp.take(outgoing, send_blocks[0].reshape(-1), axis=0)]
  transfers between devices with their start and end apart: 3 -> 4, of which waited for: 1 -> 1; matrix products, arithmetic and copies ran while one was open for 9% -> 6% of each run, Pallas kernels for 0% -> 0%
where the time goes in v1:
time: 389 us
  blocking collectives  285 us (73%)
  starting transfers between devices  23.8 us (6%)
  Pallas kernels  23.3 us (6%)
  other arithmetic  21.2 us (5%)
  waiting for transfers between devices  17.3 us (4%)
  between operations  14.2 us (4%)
  local copies, waits for them, and re-layouts  4.36 us (1%)
    unnamed x1, blocking collectives  258 us
    all_to_all x1, blocking collectives, local(): lax.all_to_all(second, 'pair', split_axis=0, concat_axis=0, tiled=True)  26.9 us
    another operation x1, other arithmetic  17.4 us
    all_to_all x1, waiting for transfers between devices, local(): lax.all_to_all(first, 'pair', split_axis=0, concat_axis=0, tiled=True)  17.2 us
    pallas_call x1, Pallas kernels, correlate(): pl.pallas_call(functools.partial(correlate_kernel, scaling), grid=(tiles,...  13.4 us
    all_to_all x1, starting transfers between devices, local(): lax.all_to_all(outgoing, 'pair', split_axis=0, concat_axis=0, tiled=True)  13 us
  transfers between devices with their start and end apart: 4, of which 1 were waited for; matrix products, arithmetic and copies ran while one was open for 6% of the time, Pallas kernels for 0%

profile of v1, /device:TPU:1, one launch (start us, length us, event | category | flops | bytes accessed | tf_op | source)
XLA Modules:
  0.0 388.5 jit_solution(3007404862953349159)
XLA Ops:
  6.5 0.0 copy-start.4
  6.5 0.0 copy-start.1
  6.5 1.2 copy-done.1
  7.8 0.0 copy-start.2
  7.8 0.0 copy-start.3
  7.8 7.6 %whiten_spread.1 = bf16[64,8,8,128]{3,2,1,0:T(8,128)(2,1)} custom-call(bf16[8,1,2,32,1024]{4,3,2,1,0:T(8,128)(2,1)S(1)} %copy-done.1), custom_call_target="tpu_custom_call" | custom-call | tf_op jit(solution)/shard_map/whiten_spread/pallas_call | solution.py:47
  15.4 13.0 %all-to-all-start = ((bf16[64,8,8,128]{3,2,1,0:T(8,128)(2,1)}), bf16[64,8,8,128]{3,2,1,0:T(8,128)(2,1)S(1)}, u32[]{:S(2)}, u32[]{:S(2)}) async-start(bf16[64,8,8,128]{3,2,1,0:T(8,128)(2,1)} %whiten_spread.1), calls=%async_computation | async-start | bytes 2097152 | tf_op jit(solution)/shard_map/all_to_all | solution.py:188
  28.4 0.0 all-gather.4.cloned.1.call-start
  28.5 0.0 copy-done.2
  28.5 0.1 copy.21
  28.6 0.1 reshape.37
  28.7 0.0 copy-done.3
  28.7 0.1 copy.22
  28.8 0.1 reshape.38
  28.9 0.0 copy-done.4
  28.9 0.6 dynamic-slice
  30.2 0.1 add_dynamic-update-slice_fusion
  30.3 257.6 %all-reduce = s32[8704]{0:T(1024)S(1)} all-reduce(s32[8704]{0:T(1024)S(1)} %add_dynamic-update-slice_fusion), channel_id=2, replica_groups=mesh['win'=4,'pair'=64] {'pair'}, use_global_device_ids=true, to_apply=%add | all-reduce | flops 8704 | bytes 69632
  287.9 0.1 reshape.44
  288.0 0.1 copy.23
  288.2 0.1 copy.24
  288.3 0.1 copy.25
  288.3 1.3 select_reduce_fusion
  289.6 0.1 reshape.40.index_ref
  289.7 0.0 all-to-all-done
  289.7 2.3 pick_blocks.1
  292.0 26.9 %all_to_all.20 = bf16[64,4,8,128]{3,2,1,0:T(8,128)(2,1)} all-to-all(bf16[64,4,8,128]{3,2,1,0:T(8,128)(2,1)S(1)} %get-tuple-element.8), channel_id=1, replica_groups=mesh['win'=4,'pair'=64] {'pair'}, dimensions={0} | all-to-all | bytes 1048576 | tf_op jit(solution)/shard_map/all_to_all | solution.py:191
  318.9 0.0 all-gather.4.cloned.1.call-update
  318.9 6.6 %all-to-all-start.1 = ((bf16[64,4,8,128]{3,2,1,0:T(8,128)(2,1)}), bf16[64,4,8,128]{3,2,1,0:T(8,128)(2,1)}, u32[]{:S(2)}, u32[]{:S(2)}) async-start(bf16[64,4,8,128]{3,2,1,0:T(8,128)(2,1)} %get-tuple-element.7), calls=%async_computation.1 | async-start | bytes 1048576 | tf_op jit(solution)/shard_map/all_to_all | solution.py:193
  325.5 17.2 %all-to-all-done.1 = bf16[64,4,8,128]{3,2,1,0:T(8,128)(2,1)} async-done(((bf16[64,4,8,128]{3,2,1,0:T(8,128)(2,1)}), bf16[64,4,8,128]{3,2,1,0:T(8,128)(2,1)}, u32[]{:S(2)}, u32[]{:S(2)}) %all-to-all-start.1) | async-done | bytes 524320 | tf_op jit(solution)/shard_map/all_to_all | solution.py:193
  342.7 4.2 %all-to-all-start.2 = ((bf16[64,4,8,128]{3,2,1,0:T(8,128)(2,1)}), bf16[64,4,8,128]{3,2,1,0:T(8,128)(2,1)S(1)}, u32[]{:S(2)}, u32[]{:S(2)}) async-start(bf16[64,4,8,128]{3,2,1,0:T(8,128)(2,1)} %all-to-all-done.1), calls=%async_computation.2 | async-start | bytes 1048576 | tf_op jit(solution)/shard_map/all_to_all | solution.py:194
  346.9 17.4 %cosine_convert_fusion = (bf16[1024,1024]{1,0:T(8,128)(2,1)S(1)}, bf16[1024,1024]{1,0:T(8,128)(2,1)S(1)}) fusion(s32[1024]{0:T(1024)S(1)} %get-tuple-element.11, s32[1024]{0:T(1024)S(1)} %get-tuple-element.12), kind=kLoop, calls=%fused_computation.10 | loop fusion | flops 17825792 | bytes 4202496 | tf_op jit(solution)/shard_map/convert
  364.3 2.4 pad_maximum_fusion.table_ref
  366.7 0.0 all-to-all-done.2
  366.7 0.0 all-gather.4.cloned.1.call-done
  366.7 0.0 copy-start
  366.7 1.6 copy-done
  368.3 13.4 %correlate.1 = bf16[8,4,32,1024]{3,2,1,0:T(8,128)(2,1)} custom-call(bf16[4,2,8,4,8,128]{5,4,3,2,1,0:T(8,128)(2,1)S(1)} %bitcast.10, bf16[4,4,2,8,4,8,128]{6,5,4,3,2,1,0:T(8,128)(2,1)S(1)} %bitcast.9, bf16[2048,1024]{1,0:T(8,128)(2,1)} %pad_maximum_fusion.table_ref), custom_call_target="tpu_custom_call" | custom-call | tf_op jit(solution)/shard_map/correlate/pallas_call | solution.py:143
  (6 shorter events, 0.0 us)
Async XLA Ops:
  6.5 22.4 %copy-start.4 = (u32[256]{0:T(256)S(1)}, u32[256]{0:T(256)}, u32[]{:S(2)}) copy-start(u32[256]{0:T(256)} %constant.30) | copy-start | bytes 3076
  6.5 1.2 copy-start.1
  7.8 20.7 %copy-start.2 = (s32[1,64,2]{1,2,0:T(2,128)S(1)}, s32[1,64,2]{1,2,0:T(2,128)}, u32[]{:S(2)}) copy-start(s32[1,64,2]{1,2,0:T(2,128)} %param.4) | copy-start | bytes 1540
  7.8 20.9 %copy-start.3 = (s32[4,2]{0,1:T(2,128)S(1)}, s32[4,2]{0,1:T(2,128)}, u32[]{:S(2)}) copy-start(s32[4,2]{0,1:T(2,128)} %param.5) | copy-start | bytes 100
  15.4 274.3 %all-to-all-start = ((bf16[64,8,8,128]{3,2,1,0:T(8,128)(2,1)}), bf16[64,8,8,128]{3,2,1,0:T(8,128)(2,1)S(1)}, u32[]{:S(2)}, u32[]{:S(2)}) async-start(bf16[64,8,8,128]{3,2,1,0:T(8,128)(2,1)} %whiten_spread.1), calls=%async_computation | async-start | bytes 2097152 | tf_op jit(solution)/shard_map/all_to_all | solution.py:188
  28.4 338.3 %all-gather.4.cloned.1.call-start = ((), (), s32[]{:S(2)}) async-start(), calls=%async_computation.4 | async-start | bytes 2621440 | tf_op jit(solution)/shard_map/all_gather | solution.py:192
  318.9 23.8 %all-to-all-start.1 = ((bf16[64,4,8,128]{3,2,1,0:T(8,128)(2,1)}), bf16[64,4,8,128]{3,2,1,0:T(8,128)(2,1)}, u32[]{:S(2)}, u32[]{:S(2)}) async-start(bf16[64,4,8,128]{3,2,1,0:T(8,128)(2,1)} %get-tuple-element.7), calls=%async_computation.1 | async-start | bytes 1048576 | tf_op jit(solution)/shard_map/all_to_all | solution.py:193
  342.7 24.0 %all-to-all-start.2 = ((bf16[64,4,8,128]{3,2,1,0:T(8,128)(2,1)}), bf16[64,4,8,128]{3,2,1,0:T(8,128)(2,1)S(1)}, u32[]{:S(2)}, u32[]{:S(2)}) async-start(bf16[64,4,8,128]{3,2,1,0:T(8,128)(2,1)} %all-to-all-done.1), calls=%async_computation.2 | async-start | bytes 1048576 | tf_op jit(solution)/shard_map/all_to_all | solution.py:194
  366.7 1.6 copy-start
Sparse Core Ops, SparseCore 0:
  319.1 30.5 all-gather.3

commit v2 on v1

v2 whole, which is shorter than its diff:
```python
import functools
import math

import jax
import jax.numpy as jnp
from jax import lax
from jax.experimental import pallas as pl
from jax.experimental.pallas import tpu as pltpu
from jax.sharding import PartitionSpec as P

LAGS = 1024
NS = 4096
F0 = 64
BAND = 64
LANES = 128
GROUP = 8
HALF = 64


def whiten_kernel(x_ref, sent_ref, slots_ref, out_ref, table_ref):
    blocks, bins = x_ref.shape[0], x_ref.shape[-1]
    lane_groups = bins // LANES
    row_band = lax.broadcasted_iota(jnp.int32, (LANES, LANES), 0) // BAND
    column_band = lax.broadcasted_iota(jnp.int32, (LANES, LANES), 1) // BAND
    ones = jnp.where(row_band == column_band, 1.0, 0.0).astype(jnp.bfloat16)
    ones = jnp.concatenate([ones, ones, ones], axis=0)
    for lane_group in range(lane_groups):
        lanes = slice(lane_group * LANES, (lane_group + 1) * LANES)
        real = x_ref[:, 0, 0, :, lanes].astype(jnp.float32).reshape(blocks * 16, LANES)
        imag = x_ref[:, 0, 1, :, lanes].astype(jnp.float32).reshape(blocks * 16, LANES)
        rest = real * real + imag * imag
        terms = []
        for _ in range(3):
            terms.append(rest.astype(jnp.bfloat16))
            rest = rest - terms[-1].astype(jnp.float32)
        power = jnp.dot(jnp.concatenate(terms, axis=1), ones, preferred_element_type=jnp.float32)
        scale = lax.rsqrt(power * (1.0 / (2 * BAND)) + 1e-06)
        for part, rows in enumerate((real * scale, imag * scale)):
            rows = rows.reshape(blocks, 2, GROUP, LANES)
            for half in range(2):
                place = (half * 2 + part) * lane_groups + lane_group
                out_ref[place, :blocks] = rows[:, half].astype(jnp.bfloat16)
    table_ref[...] = jnp.zeros_like(table_ref)
    table_ref[0:2, : sent_ref.shape[1]] = sent_ref[...].astype(jnp.float32)
    table_ref[2:4, : slots_ref.shape[1]] = slots_ref[...].astype(jnp.float32)
    piece = table_ref[...].astype(jnp.bfloat16)
    out_ref[:, blocks] = jnp.broadcast_to(piece, (out_ref.shape[0],) + piece.shape)


def whiten_spread(spectra, sent, slots):
    blocks, _, parts, channels, bins = spectra.shape
    pieces = parts * channels * bins // (GROUP * LANES)
    steps = channels // 16
    return pl.pallas_call(
        whiten_kernel,
        grid=(steps,),
        in_specs=[
            pl.BlockSpec((blocks, 1, parts, 16, bins), lambda g: (0, 0, 0, g, 0)),
            pl.BlockSpec(sent.shape, lambda g: (0, 0)),
            pl.BlockSpec(slots.shape, lambda g: (0, 0)),
        ],
        out_specs=pl.BlockSpec((pieces // steps, blocks + 1, GROUP, LANES), lambda g: (g, 0, 0, 0)),
        out_shape=jax.ShapeDtypeStruct((pieces, blocks + 1, GROUP, LANES), jnp.bfloat16),
        scratch_shapes=[pltpu.VMEM((GROUP, LANES), jnp.float32)],
        compiler_params=pltpu.CompilerParams(vmem_limit_bytes=24 * 2**20),
        name="whiten_spread",
    )(spectra, sent, slots)


def pick_kernel(x_ref, *refs):
    out_refs, (table_ref, index_ref, place_ref, sem) = refs[:-4], refs[-4:]
    owners, stride = x_ref.shape[:2]
    table_ref[...] = x_ref[:, stride - 1].astype(jnp.float32).reshape(table_ref.shape)
    sent = [table_ref[pl.ds(k, owners, stride=GROUP), :] for k in range(2)]
    lane = lax.broadcasted_iota(jnp.int32, (owners, LANES), 1)
    by_owner = jnp.concatenate(sent, axis=0).T[:owners].astype(jnp.int32)
    by_owner = by_owner + stride * (lane % HALF)
    places = jnp.zeros((owners, LANES), jnp.int32)
    tiles = sum(ref.shape[1] for ref in out_refs) // 2
    for part in range(2):
        slots = table_ref[pl.ds(2 + part, owners, stride=GROUP), :].astype(jnp.int32)
        for tile in range(tiles):
            slot = slots[:, tile : tile + 1]
            hit = lane == (slot % 2) * HALF + slot // 2
            place = jnp.sum(jnp.where(hit, by_owner, 0), axis=1, keepdims=True)
            places = jnp.where(lane == part * tiles + tile, place, places)
    index_ref[...] = places
    copy = pltpu.make_async_copy(index_ref, place_ref, sem)
    copy.start()
    copy.wait()
    flat = x_ref.reshape(owners * stride, GROUP, LANES)

    def one_owner(owner, carry):
        start = 0
        for out_ref in out_refs:
            count = out_ref.shape[1] // 2
            for part in range(2):
                for tile in range(count):
                    place = place_ref[owner, part * tiles + start + tile]
                    out_ref[owner, part * count + tile] = flat[place]
            start += count
        return carry

    lax.fori_loop(0, owners, one_owner, 0, unroll=2)


def pick(spread, shares):
    owners = spread.shape[0]
    shapes = [
        jax.ShapeDtypeStruct((owners, 2 * count, GROUP, LANES), jnp.bfloat16) for count in shares
    ]
    return pl.pallas_call(
        pick_kernel,
        in_specs=[pl.BlockSpec(memory_space=pltpu.VMEM)],
        out_specs=[pl.BlockSpec(memory_space=pltpu.VMEM)] * len(shapes),
        out_shape=shapes,
        scratch_shapes=[
            pltpu.VMEM((owners * GROUP, LANES), jnp.float32),
            pltpu.VMEM((owners, LANES), jnp.int32),
            pltpu.SMEM((owners, LANES), jnp.int32),
            pltpu.SemaphoreType.DMA,
        ],
        compiler_params=pltpu.CompilerParams(vmem_limit_bytes=24 * 2**20),
        name="pick_blocks",
    )(spread)


def correlate_kernel(scaling, windows, win_ref, a_ref, *refs):
    b_refs, table_ref = refs[:windows], refs[windows]
    out_ref, stack_ref = refs[-2:]
    step = pl.program_id(0)
    last = pl.num_programs(0) - 1
    lane_groups = a_ref.shape[2]
    groups = b_refs[0].shape[0]
    bins = lane_groups * LANES
    channels = groups * GROUP
    source = [lax.rem(win_ref[0] + windows - w, windows) for w in range(windows)]

    def cross(lane_group, slot):
        lanes = pl.multiple_of(lane_group * LANES, LANES)
        a = [
            [a_ref[source[w], part, lane_group, step].astype(jnp.float32) for part in range(2)]
            for w in range(windows)
        ]
        for pair in range(groups // 2):
            b = [
                [
                    [
                        b_refs[w][pair * 2 + half, part, lane_group, step].astype(jnp.float32)
                        for part in range(2)
                    ]
                    for w in range(windows)
                ]
                for half in range(2)
            ]
            for i in range(GROUP):
                rows = [[None, None], [None, None]]
                for w in range(windows):
                    a0 = jnp.broadcast_to(a[w][0][i : i + 1], (GROUP, LANES))
                    a1 = jnp.broadcast_to(a[w][1][i : i + 1], (GROUP, LANES))
                    for half in range(2):
                        b0, b1 = b[half][w]
                        real = a0 * b0 + a1 * b1
                        imag = a1 * b0 - a0 * b1
                        if w:
                            real += rows[half][0]
                            imag += rows[half][1]
                        rows[half] = [real, imag]
                start = i * channels + pair * 2 * GROUP
                for part in range(2):
                    joined = jnp.concatenate([rows[0][part], rows[1][part]], axis=0)
                    stack_ref[
                        slot, start : start + 2 * GROUP, pl.ds(part * bins + lanes, LANES)
                    ] = joined.astype(jnp.bfloat16)

    def lagged(chunk, slot):
        columns = pl.ds(pl.multiple_of(chunk * 2 * LANES, 2 * LANES), 2 * LANES)
        rows = jnp.dot(stack_ref[slot], table_ref[:, columns], preferred_element_type=jnp.float32)
        rows = (rows * scaling).astype(jnp.bfloat16)
        out_ref[:, 0, :, columns] = rows.reshape(GROUP, channels, 2 * LANES)

    def run(with_cross, with_lagged):
        def body(chunk, carry):
            if with_lagged:
                lagged(chunk, lax.rem(step + 1, 2))
            if with_cross:
                cross(chunk * 2, lax.rem(step, 2))
                cross(chunk * 2 + 1, lax.rem(step, 2))
            return carry

        lax.fori_loop(0, lane_groups // 2, body, 0)

    @pl.when(step == 0)
    def _():
        run(True, False)

    @pl.when(jnp.logical_and(step > 0, step < last))
    def _():
        run(True, True)

    @pl.when(step == last)
    def _():
        run(False, True)


def correlate(a, b, table, start, tiles, result):
    windows, _, lane_groups, count = a.shape[:4]
    channels = b[0].shape[0] * GROUP
    bins = lane_groups * LANES
    lags = table.shape[1]
    scaling = 1.0 / math.sqrt(windows * bins)
    win = lax.axis_index("win").astype(jnp.int32).reshape(1)
    whole = lambda x: pl.BlockSpec(x.shape, lambda t: (0,) * len(x.shape))
    operands = [win, a, *b, table]
    in_specs = [pl.BlockSpec(memory_space=pltpu.SMEM)] + [whole(x) for x in operands[1:]]
    aliases = {}
    if result is not None:
        aliases = {len(operands): 0}
        operands.append(result)
        in_specs.append(pl.BlockSpec(memory_space=pl.ANY))
    place = lambda t: (0, start + jnp.maximum(t - 1, 0), 0, 0)
    return pl.pallas_call(
        functools.partial(correlate_kernel, scaling, windows),
        grid=(count + 1,),
        in_specs=in_specs,
        out_specs=pl.BlockSpec((GROUP, 1, channels, lags), place),
        out_shape=jax.ShapeDtypeStruct((GROUP, tiles, channels, lags), jnp.bfloat16),
        scratch_shapes=[pltpu.VMEM((2, GROUP * channels, 2 * bins), jnp.bfloat16)],
        input_output_aliases=aliases,
        compiler_params=pltpu.CompilerParams(vmem_limit_bytes=40 * 2**20),
        cost_estimate=pl.CostEstimate(
            flops=4 * count * GROUP * channels * bins * lags,
            bytes_accessed=8 * 2**20,
            transcendentals=0,
        ),
        name="correlate",
    )(*operands)


def lag_rows_table(bin_total):
    bin_index = jnp.arange(bin_total, dtype=jnp.int32) + F0
    lag_index = jnp.arange(LAGS, dtype=jnp.int32) - LAGS // 2
    wrapped = bin_index[:, None] * lag_index[None, :] % NS
    phases = wrapped.astype(jnp.float32) * (2.0 * math.pi / NS)
    return jnp.concatenate([jnp.cos(phases), -jnp.sin(phases)], axis=0).astype(jnp.bfloat16)


def local(spectra, send_blocks, tile_slots):
    windows = lax.axis_size("win")
    blocks, _, parts, channels, bins = spectra.shape
    tiles = tile_slots.shape[0]
    lane_groups = bins // LANES
    shares = (tiles // 2, tiles - tiles // 2)
    exchange = lambda x, axis: lax.all_to_all(x, axis, split_axis=0, concat_axis=0, tiled=True)

    outgoing = whiten_spread(spectra, send_blocks[0].T, tile_slots.T)
    spread = exchange(outgoing, "pair")
    spread, table = lax.optimization_barrier((spread, lag_rows_table(bins)))
    picked = pick(spread, shares)
    result, start = None, 0
    for share, count in enumerate(shares):
        both = exchange(picked[share], "pair")
        first, second = both[:, :count], both[:, count:]
        a = exchange(first, "win").reshape(windows, parts, lane_groups, count, GROUP, LANES)
        b = [second]
        for distance in range(1, windows):
            turn = [(w, (w + distance) % windows) for w in range(windows)]
            b.append(lax.ppermute(second, "win", turn))
        b = [x.reshape(channels // GROUP, parts, lane_groups, count, GROUP, LANES) for x in b]
        result = correlate(a, b, table, start, tiles, result)
        start += count
    return result


def solution(mesh):
    in_specs = (P("pair", "win", None, None, None), P("pair", None, None), P("pair", None))
    out_specs = P("win", "pair", None, None)
    return jax.shard_map(local, mesh=mesh, in_specs=in_specs, out_specs=out_specs, check_vma=False)
```

time: 389 us -> 134 us (0.34)
  blocking collectives: 285 us -> 23.3 us
  between operations: 14.2 us -> 0.1 us
  starting transfers between devices: 23.8 us -> 34.6 us
  waiting for transfers between devices: 17.3 us -> 27.9 us
  Pallas kernels: 23.3 us -> 19 us
  local copies, waits for them, and re-layouts: 4.36 us -> 8.45 us
    unnamed x1 -> x0, blocking collectives: 258 us -> none
    all_to_all x3 -> x4, waiting for transfers between devices: 17.2 us -> 27.9 us  [local(): lax.all_to_all(x, axis, split_axis=0, concat_axis=0, tiled=True)]
    ppermute x0 -> x6, starting transfers between devices: none -> 7.6 us  [local(): b.append(lax.ppermute(second, 'win', turn))]
    pallas_call x1, Pallas kernels: 7.63 us -> 1.73 us  [whiten_spread(): pl.pallas_call(whiten_kernel, grid=(steps,), in_specs=[pl.BlockSpec((bloc...]
    all_to_all x3 -> x4, starting transfers between devices: 23.7 us -> 27 us  [local(): lax.all_to_all(x, axis, split_axis=0, concat_axis=0, tiled=True)]
    pallas_call x2 -> x3, Pallas kernels: 15.6 us -> 17.2 us  [the longest x2 13.9 us: correlate(): pl.pallas_call(functools.partial(correlate_kernel, scaling, windows), gri...]
  transfers between devices with their start and end apart: 4 -> 10, of which waited for: 1 -> 4; matrix products, arithmetic and copies ran while one was open for 6% -> 16% of each run, Pallas kernels for 0% -> 5%
where the time goes in v2:
time: 134 us; the launch traced here: 133 us
  starting transfers between devices  34.6 us (26%)
  waiting for transfers between devices  27.9 us (21%)
  blocking collectives  23.3 us (17%)
  other arithmetic  19.8 us (15%)
  Pallas kernels  19 us (14%)
  local copies, waits for them, and re-layouts  8.45 us (6%)
    all_to_all x4, waiting for transfers between devices, local(): lax.all_to_all(x, axis, split_axis=0, concat_axis=0, tiled=True)  27.9 us
    all_to_all x4, starting transfers between devices, local(): lax.all_to_all(x, axis, split_axis=0, concat_axis=0, tiled=True)  27 us
    all_to_all x1, blocking collectives, local(): lax.all_to_all(x, axis, split_axis=0, concat_axis=0, tiled=True)  23.3 us
    another operation x1, other arithmetic  17.4 us
    pallas_call x2, Pallas kernels, correlate(): pl.pallas_call(functools.partial(correlate_kernel, scaling, windows), gri...  13.9 us
    ppermute x6, starting transfers between devices, local(): b.append(lax.ppermute(second, 'win', turn))  7.6 us
    unnamed x10, local copies, waits for them, and re-layouts  6.94 us
    pallas_call x1, Pallas kernels, pick(): pl.pallas_call(pick_kernel, in_specs=[pl.BlockSpec(memory_space=pltpu.VME...  3.29 us
  transfers between devices with their start and end apart: 10, of which 4 were waited for; matrix products, arithmetic and copies ran while one was open for 16% of the time, Pallas kernels for 5%

profile of v2, /device:TPU:1, one launch (start us, length us, event | category | flops | bytes accessed | tf_op | source)
XLA Modules:
  0.0 133.2 jit_solution(12800436777290911986)
XLA Ops:
  0.0 0.0 copy-start.2
  0.0 1.2 copy-done.2
  1.2 0.0 copy-start.3
  1.2 0.7 copy-done.3
  1.9 0.0 copy-start.4
  1.9 0.7 copy-done.4
  2.6 1.7 %whiten_spread.1 = bf16[64,9,8,128]{3,2,1,0:T(8,128)(2,1)} custom-call(bf16[8,1,2,32,1024]{4,3,2,1,0:T(8,128)(2,1)S(1)} %copy-done.2, s32[2,64]{1,0:T(2,128)S(1)} %bitcast.22, s32[2,4]{1,0:T(2,128)S(1)} %bitcast.23), custom_call_target="tpu_custom_call" | custom-call | tf_op jit(solution)/shard_map/whiten_spread/pallas_call | solution.py:54
  4.3 13.0 %all-to-all-start = ((bf16[64,9,8,128]{3,2,1,0:T(8,128)(2,1)}), bf16[64,9,8,128]{3,2,1,0:T(8,128)(2,1)S(1)}, u32[]{:S(2)}, u32[]{:S(2)}) async-start(bf16[64,9,8,128]{3,2,1,0:T(8,128)(2,1)} %whiten_spread.1), calls=%async_computation | async-start | bytes 2359296 | tf_op jit(solution)/shard_map/all_to_all | solution.py:254
  17.3 17.4 %cosine_convert_fusion = (bf16[1024,1024]{1,0:T(8,128)(2,1)S(1)}, bf16[1024,1024]{1,0:T(8,128)(2,1)S(1)}) fusion(s32[1024]{0:T(1024)S(1)} %get-tuple-element.19, s32[1024]{0:T(1024)S(1)} %get-tuple-element.20), kind=kLoop, calls=%fused_computation.10 | loop fusion | flops 17825792 | bytes 4202496 | tf_op jit(solution)/shard_map/convert
  34.7 2.4 %pad_maximum_fusion.refs_4_ = bf16[2048,1024]{1,0:T(8,128)(2,1)} fusion(bf16[1024,1024]{1,0:T(8,128)(2,1)S(1)} %get-tuple-element.18, bf16[1024,1024]{1,0:T(8,128)(2,1)S(1)} %get-tuple-element.17), kind=kLoop, calls=%fused_computation.8 | loop fusion | flops 8388608 | bytes 8388608 | tf_op jit(solution)/shard_map/concatenate | solution.py:245
  37.1 11.6 %all-to-all-done.x_ref = bf16[64,9,8,128]{3,2,1,0:T(8,128)(2,1)S(1)} async-done(((bf16[64,9,8,128]{3,2,1,0:T(8,128)(2,1)}), bf16[64,9,8,128]{3,2,1,0:T(8,128)(2,1)S(1)}, u32[]{:S(2)}, u32[]{:S(2)}) %all-to-all-start) | async-done | bytes 1179680 | tf_op jit(solution)/shard_map/all_to_all | solution.py:254
  48.7 3.3 %pick_blocks.1 = (bf16[64,4,8,128]{3,2,1,0:T(8,128)(2,1)S(1)}, bf16[64,4,8,128]{3,2,1,0:T(8,128)(2,1)}) custom-call(bf16[64,9,8,128]{3,2,1,0:T(8,128)(2,1)S(1)} %all-to-all-done.x_ref), custom_call_target="tpu_custom_call" | custom-call | tf_op jit(solution)/shard_map/pick_blocks/pallas_call | solution.py:112
  52.0 23.3 %all_to_all.25 = bf16[64,4,8,128]{3,2,1,0:T(8,128)(2,1)S(1)} all-to-all(bf16[64,4,8,128]{3,2,1,0:T(8,128)(2,1)S(1)} %get-tuple-element.12), channel_id=1, replica_groups=mesh['win'=4,'pair'=64] {'pair'}, dimensions={0} | all-to-all | bytes 1048576 | tf_op jit(solution)/shard_map/all_to_all | solution.py:254
  75.3 6.3 %all-to-all-start.1 = ((bf16[64,4,8,128]{3,2,1,0:T(8,128)(2,1)}), bf16[64,4,8,128]{3,2,1,0:T(8,128)(2,1)S(1)}, u32[]{:S(2)}, u32[]{:S(2)}) async-start(bf16[64,4,8,128]{3,2,1,0:T(8,128)(2,1)} %get-tuple-element.10), calls=%async_computation.1 | async-start | bytes 1048576 | tf_op jit(solution)/shard_map/all_to_all | solution.py:254
  81.6 0.8 fusion.3
  82.3 2.7 %collective-permute-start.5 = (bf16[64,2,8,128]{3,2,1,0:T(8,128)(2,1)S(1)}, bf16[64,2,8,128]{3,2,1,0:T(8,128)(2,1)S(1)}, u32[]{:S(2)}, u32[]{:S(2)}) collective-permute-start(bf16[64,2,8,128]{3,2,1,0:T(8,128)(2,1)S(1)} %get-tuple-element.13), channel_id=1, source_target_pairs={{0,192},{64,0},{128,64},{192,128},{1,193},{65,1},{129,65},{193,129... | collective-permute-start | bytes 786440 | tf_op jit(solution)/shard_map/ppermute | solution.py:268
  85.1 0.4 collective-permute-start.4
  85.4 0.7 collective-permute-start.3
  86.1 12.8 %all-to-all-done.1 = bf16[64,4,8,128]{3,2,1,0:T(8,128)(2,1)S(1)} async-done(((bf16[64,4,8,128]{3,2,1,0:T(8,128)(2,1)}), bf16[64,4,8,128]{3,2,1,0:T(8,128)(2,1)S(1)}, u32[]{:S(2)}, u32[]{:S(2)}) %all-to-all-start.1) | async-done | bytes 524320 | tf_op jit(solution)/shard_map/all_to_all | solution.py:254
  98.9 4.2 %all-to-all-start.4 = ((bf16[64,2,8,128]{3,2,1,0:T(8,128)(2,1)}), bf16[64,2,8,128]{3,2,1,0:T(8,128)(2,1)S(1)}, u32[]{:S(2)}, u32[]{:S(2)}) async-start(bf16[64,2,8,128]{3,2,1,0:T(8,128)(2,1)} %get-tuple-element.14), calls=%async_computation.4 | async-start | bytes 524288 | tf_op jit(solution)/shard_map/all_to_all | solution.py:254
  103.1 0.7 fusion.4
  103.8 2.7 %collective-permute-start.2 = (bf16[64,2,8,128]{3,2,1,0:T(8,128)(2,1)S(1)}, bf16[64,2,8,128]{3,2,1,0:T(8,128)(2,1)S(1)}, u32[]{:S(2)}, u32[]{:S(2)}) collective-permute-start(bf16[64,2,8,128]{3,2,1,0:T(8,128)(2,1)S(1)} %get-tuple-element.15), channel_id=1, source_target_pairs={{0,192},{64,0},{128,64},{192,128},{1,193},{65,1},{129,65},{193,129... | collective-permute-start | bytes 786440 | tf_op jit(solution)/shard_map/ppermute | solution.py:268
  106.5 0.6 collective-permute-start.1
  107.1 0.0 collective-permute-done.5
  107.1 0.6 collective-permute-start
  107.7 1.3 all-to-all-done.4
  108.9 3.6 %all-to-all-start.2 = ((bf16[64,2,8,128]{3,2,1,0:T(8,128)(2,1)}), bf16[64,2,8,128]{3,2,1,0:T(8,128)(2,1)S(1)}, u32[]{:S(2)}, u32[]{:S(2)}) async-start(bf16[64,2,8,128]{3,2,1,0:T(8,128)(2,1)} %get-tuple-element.16), calls=%async_computation.2 | async-start | bytes 524288 | tf_op jit(solution)/shard_map/all_to_all | solution.py:254
  112.5 0.0 collective-permute-done.4
  112.5 0.0 collective-permute-done.3
  112.6 0.0 copy-start
  112.6 2.2 %copy-done = bf16[2048,1024]{1,0:T(8,128)(2,1)S(1)} copy-done((bf16[2048,1024]{1,0:T(8,128)(2,1)S(1)}, bf16[2048,1024]{1,0:T(8,128)(2,1)}, u32[]{:S(2)}) %copy-start) | copy-done | bytes 4194328
  114.7 7.0 %correlate.2.refs_5_ = bf16[8,4,32,1024]{3,2,1,0:T(8,128)(2,1)} custom-call(s32[1]{0:T(128)} %bitcast.win_ref, bf16[4,2,8,2,8,128]{5,4,3,2,1,0:T(8,128)(2,1)S(1)} %bitcast.20, bf16[4,2,8,2,8,128]{5,4,3,2,1,0:T(8,128)(2,1)S(1)} %bitcast.21, bf16[4,2,8,2,8,128]{5,4,3,2,1,0:T(8,128)(2,1)S(1)} %bitcast.26, bf16[4,2,8,2,8,128]{5,4,3,2,1,0:T(8,128)(2,1)S(1)} %bitcast.25, ...), custom_call_target="tpu_custom_call" | custom-call | flops 2147483648 | bytes 8388608 | tf_op jit(solution)/shard_map/correlate/pallas_call | solution.py:222
  121.7 2.3 %all-to-all-done.2 = bf16[64,2,8,128]{3,2,1,0:T(8,128)(2,1)S(1)} async-done(((bf16[64,2,8,128]{3,2,1,0:T(8,128)(2,1)}), bf16[64,2,8,128]{3,2,1,0:T(8,128)(2,1)S(1)}, u32[]{:S(2)}, u32[]{:S(2)}) %all-to-all-start.2) | async-done | bytes 262176 | tf_op jit(solution)/shard_map/all_to_all | solution.py:254
  124.0 0.0 collective-permute-done.2
  124.0 0.0 collective-permute-done.1
  124.0 0.0 collective-permute-done
  124.0 0.0 copy-start.1
  124.0 2.2 %copy-done.1 = bf16[2048,1024]{1,0:T(8,128)(2,1)S(1)} copy-done((bf16[2048,1024]{1,0:T(8,128)(2,1)S(1)}, bf16[2048,1024]{1,0:T(8,128)(2,1)}, u32[]{:S(2)}) %copy-start.1) | copy-done | bytes 4194328
  126.2 7.0 %correlate.3 = bf16[8,4,32,1024]{3,2,1,0:T(8,128)(2,1)} custom-call(s32[1]{0:T(128)} %bitcast.win_ref, bf16[4,2,8,2,8,128]{5,4,3,2,1,0:T(8,128)(2,1)S(1)} %bitcast.15, bf16[4,2,8,2,8,128]{5,4,3,2,1,0:T(8,128)(2,1)S(1)} %bitcast.16, bf16[4,2,8,2,8,128]{5,4,3,2,1,0:T(8,128)(2,1)S(1)} %bitcast.19, ...), custom_call_target="tpu_custom_call", output_to_operand_aliasing={{}: (7, {})} | custom-call | flops 2147483648 | bytes 8388608 | tf_op jit(solution)/shard_map/correlate/pallas_call | solution.py:222
  (1 shorter events, 0.0 us)
Async XLA Ops:
  0.0 1.2 copy-start.2
  1.2 0.7 copy-start.3
  1.9 0.7 copy-start.4
  4.3 44.4 %all-to-all-start = ((bf16[64,9,8,128]{3,2,1,0:T(8,128)(2,1)}), bf16[64,9,8,128]{3,2,1,0:T(8,128)(2,1)S(1)}, u32[]{:S(2)}, u32[]{:S(2)}) async-start(bf16[64,9,8,128]{3,2,1,0:T(8,128)(2,1)} %whiten_spread.1), calls=%async_computation | async-start | bytes 2359296 | tf_op jit(solution)/shard_map/all_to_all | solution.py:254
  75.3 23.6 %all-to-all-start.1 = ((bf16[64,4,8,128]{3,2,1,0:T(8,128)(2,1)}), bf16[64,4,8,128]{3,2,1,0:T(8,128)(2,1)S(1)}, u32[]{:S(2)}, u32[]{:S(2)}) async-start(bf16[64,4,8,128]{3,2,1,0:T(8,128)(2,1)} %get-tuple-element.10), calls=%async_computation.1 | async-start | bytes 1048576 | tf_op jit(solution)/shard_map/all_to_all | solution.py:254
  82.3 24.7 %collective-permute-start.5 = (bf16[64,2,8,128]{3,2,1,0:T(8,128)(2,1)S(1)}, bf16[64,2,8,128]{3,2,1,0:T(8,128)(2,1)S(1)}, u32[]{:S(2)}, u32[]{:S(2)}) collective-permute-start(bf16[64,2,8,128]{3,2,1,0:T(8,128)(2,1)S(1)} %get-tuple-element.13), channel_id=1, source_target_pairs={{0,192},{64,0},{128,64},{192,128},{1,193},{65,1},{129,65},{193,129... | collective-permute-start | bytes 786440 | tf_op jit(solution)/shard_map/ppermute | solution.py:268
  85.1 27.5 %collective-permute-start.4 = (bf16[64,2,8,128]{3,2,1,0:T(8,128)(2,1)S(1)}, bf16[64,2,8,128]{3,2,1,0:T(8,128)(2,1)S(1)}, u32[]{:S(2)}, u32[]{:S(2)}) collective-permute-start(bf16[64,2,8,128]{3,2,1,0:T(8,128)(2,1)S(1)} %get-tuple-element.13), channel_id=1, source_target_pairs={{0,128},{64,192},{128,0},{192,64},{1,129},{65,193},{129,1},{193,65... | collective-permute-start | bytes 786440 | tf_op jit(solution)/shard_map/ppermute | solution.py:268
  85.4 27.1 %collective-permute-start.3 = (bf16[64,2,8,128]{3,2,1,0:T(8,128)(2,1)S(1)}, bf16[64,2,8,128]{3,2,1,0:T(8,128)(2,1)S(1)}, u32[]{:S(2)}, u32[]{:S(2)}) collective-permute-start(bf16[64,2,8,128]{3,2,1,0:T(8,128)(2,1)S(1)} %get-tuple-element.13), channel_id=1, source_target_pairs={{0,64},{64,128},{128,192},{192,0},{1,65},{65,129},{129,193},{193,1... | collective-permute-start | bytes 786440 | tf_op jit(solution)/shard_map/ppermute | solution.py:268
  98.9 10.0 %all-to-all-start.4 = ((bf16[64,2,8,128]{3,2,1,0:T(8,128)(2,1)}), bf16[64,2,8,128]{3,2,1,0:T(8,128)(2,1)S(1)}, u32[]{:S(2)}, u32[]{:S(2)}) async-start(bf16[64,2,8,128]{3,2,1,0:T(8,128)(2,1)} %get-tuple-element.14), calls=%async_computation.4 | async-start | bytes 524288 | tf_op jit(solution)/shard_map/all_to_all | solution.py:254
  103.8 20.2 %collective-permute-start.2 = (bf16[64,2,8,128]{3,2,1,0:T(8,128)(2,1)S(1)}, bf16[64,2,8,128]{3,2,1,0:T(8,128)(2,1)S(1)}, u32[]{:S(2)}, u32[]{:S(2)}) collective-permute-start(bf16[64,2,8,128]{3,2,1,0:T(8,128)(2,1)S(1)} %get-tuple-element.15), channel_id=1, source_target_pairs={{0,192},{64,0},{128,64},{192,128},{1,193},{65,1},{129,65},{193,129... | collective-permute-start | bytes 786440 | tf_op jit(solution)/shard_map/ppermute | solution.py:268
  106.5 17.5 %collective-permute-start.1 = (bf16[64,2,8,128]{3,2,1,0:T(8,128)(2,1)S(1)}, bf16[64,2,8,128]{3,2,1,0:T(8,128)(2,1)S(1)}, u32[]{:S(2)}, u32[]{:S(2)}) collective-permute-start(bf16[64,2,8,128]{3,2,1,0:T(8,128)(2,1)S(1)} %get-tuple-element.15), channel_id=1, source_target_pairs={{0,128},{64,192},{128,0},{192,64},{1,129},{65,193},{129,1},{193,65... | collective-permute-start | bytes 786440 | tf_op jit(solution)/shard_map/ppermute | solution.py:268
  107.1 16.9 %collective-permute-start = (bf16[64,2,8,128]{3,2,1,0:T(8,128)(2,1)S(1)}, bf16[64,2,8,128]{3,2,1,0:T(8,128)(2,1)S(1)}, u32[]{:S(2)}, u32[]{:S(2)}) collective-permute-start(bf16[64,2,8,128]{3,2,1,0:T(8,128)(2,1)S(1)} %get-tuple-element.15), channel_id=1, source_target_pairs={{0,64},{64,128},{128,192},{192,0},{1,65},{65,129},{129,193},{193,1... | collective-permute-start | bytes 786440 | tf_op jit(solution)/shard_map/ppermute | solution.py:268
  108.9 15.1 %all-to-all-start.2 = ((bf16[64,2,8,128]{3,2,1,0:T(8,128)(2,1)}), bf16[64,2,8,128]{3,2,1,0:T(8,128)(2,1)S(1)}, u32[]{:S(2)}, u32[]{:S(2)}) async-start(bf16[64,2,8,128]{3,2,1,0:T(8,128)(2,1)} %get-tuple-element.16), calls=%async_computation.2 | async-start | bytes 524288 | tf_op jit(solution)/shard_map/all_to_all | solution.py:254
  112.6 2.2 %copy-start = (bf16[2048,1024]{1,0:T(8,128)(2,1)S(1)}, bf16[2048,1024]{1,0:T(8,128)(2,1)}, u32[]{:S(2)}) copy-start(bf16[2048,1024]{1,0:T(8,128)(2,1)} %pad_maximum_fusion.refs_4_) | copy-start | bytes 12582916
  124.0 2.2 %copy-start.1 = (bf16[2048,1024]{1,0:T(8,128)(2,1)S(1)}, bf16[2048,1024]{1,0:T(8,128)(2,1)}, u32[]{:S(2)}) copy-start(bf16[2048,1024]{1,0:T(8,128)(2,1)} %pad_maximum_fusion.refs_4_) | copy-start | bytes 12582916

commit v3 on v2

v3 whole, which is shorter than its diff:
```python
import functools
import math

import jax
import jax.numpy as jnp
from jax import lax
from jax.experimental import pallas as pl
from jax.experimental.pallas import tpu as pltpu
from jax.sharding import PartitionSpec as P

LAGS = 1024
NS = 4096
F0 = 64
BAND = 64
LANES = 128
GROUP = 8
HALF = 64


def whiten_kernel(win_ref, x_ref, sent_ref, slots_ref, out_ref, table_ref):
    blocks = x_ref.shape[0]
    _, lane_groups, groups = out_ref.shape[:3]
    step = pl.program_id(0)
    row_band = lax.broadcasted_iota(jnp.int32, (LANES, LANES), 0) // BAND
    column_band = lax.broadcasted_iota(jnp.int32, (LANES, LANES), 1) // BAND
    ones = jnp.where(row_band == column_band, 1.0, 0.0).astype(jnp.bfloat16)
    ones = jnp.concatenate([ones, ones, ones], axis=0)
    for lane_group in range(lane_groups):
        lanes = slice(lane_group * LANES, (lane_group + 1) * LANES)
        real = x_ref[:, 0, 0, :, lanes].astype(jnp.float32).reshape(blocks * 16, LANES)
        imag = x_ref[:, 0, 1, :, lanes].astype(jnp.float32).reshape(blocks * 16, LANES)
        rest = real * real + imag * imag
        terms = []
        for _ in range(3):
            terms.append(rest.astype(jnp.bfloat16))
            rest = rest - terms[-1].astype(jnp.float32)
        power = jnp.dot(jnp.concatenate(terms, axis=1), ones, preferred_element_type=jnp.float32)
        scale = lax.rsqrt(power * (1.0 / (2 * BAND)) + 1e-06)
        for part, rows in enumerate((real * scale, imag * scale)):
            rows = rows.reshape(blocks, 2, GROUP, LANES)
            for half in range(2):
                place = lax.rem(2 * step + half + groups - win_ref[0], groups)
                out_ref[part, lane_group, place, :blocks] = rows[:, half].astype(jnp.bfloat16)

    @pl.when(step == 0)
    def _():
        table_ref[...] = jnp.zeros_like(table_ref)
        table_ref[0:2, : sent_ref.shape[1]] = sent_ref[...].astype(jnp.float32)
        table_ref[2:4, : slots_ref.shape[1]] = slots_ref[...].astype(jnp.float32)
        piece = table_ref[...].astype(jnp.bfloat16)
        shape = out_ref.shape
        out_ref[:, :, :, blocks] = jnp.broadcast_to(piece, shape[:3] + shape[4:])


def whiten_spread(win, spectra, sent, slots):
    blocks, _, parts, channels, bins = spectra.shape
    shape = (parts, bins // LANES, channels // GROUP, blocks + 1, GROUP, LANES)
    return pl.pallas_call(
        whiten_kernel,
        grid=(channels // 16,),
        in_specs=[
            pl.BlockSpec(memory_space=pltpu.SMEM),
            pl.BlockSpec((blocks, 1, parts, 16, bins), lambda g: (0, 0, 0, g, 0)),
            pl.BlockSpec(sent.shape, lambda g: (0, 0)),
            pl.BlockSpec(slots.shape, lambda g: (0, 0)),
        ],
        out_specs=pl.BlockSpec(shape, lambda g: (0,) * len(shape)),
        out_shape=jax.ShapeDtypeStruct(shape, jnp.bfloat16),
        scratch_shapes=[pltpu.VMEM((GROUP, LANES), jnp.float32)],
        compiler_params=pltpu.CompilerParams(vmem_limit_bytes=60 * 2**20),
        name="whiten_spread",
    )(win, spectra, sent, slots)


def copy_pieces(place_ref, x_ref, out_ref, start):
    flat = x_ref.reshape((x_ref.shape[0] * x_ref.shape[1],) + x_ref.shape[2:])

    def one_owner(owner, carry):
        for tile in range(out_ref.shape[1]):
            out_ref[owner, tile] = flat[place_ref[owner, start + tile]]
        return carry

    lax.fori_loop(0, out_ref.shape[0], one_owner, 0, unroll=4)


def pick_second_kernel(x_ref, out_ref, index_ref, table_ref, place_ref, sem):
    owners, stride = x_ref.shape[:2]
    tiles = out_ref.shape[1]
    table_ref[...] = x_ref[:, stride - 1].astype(jnp.float32).reshape(table_ref.shape)
    sent = [table_ref[pl.ds(k, owners, stride=GROUP), :] for k in range(2)]
    lane = lax.broadcasted_iota(jnp.int32, (owners, LANES), 1)
    by_owner = jnp.concatenate(sent, axis=0).T[:owners].astype(jnp.int32)
    by_owner = by_owner + stride * (lane % HALF)
    places = jnp.zeros((owners, LANES), jnp.int32)
    for part in range(2):
        slots = table_ref[pl.ds(2 + part, owners, stride=GROUP), :].astype(jnp.int32)
        for tile in range(tiles):
            slot = slots[:, tile : tile + 1]
            hit = lane == (slot % 2) * HALF + slot // 2
            place = jnp.sum(jnp.where(hit, by_owner, 0), axis=1, keepdims=True)
            places = jnp.where(lane == part * tiles + tile, place, places)
    index_ref[...] = places
    copy = pltpu.make_async_copy(index_ref, place_ref, sem)
    copy.start()
    copy.wait()
    copy_pieces(place_ref, x_ref, out_ref, tiles)


def pick_second(spread, tiles):
    owners = spread.shape[0]
    return pl.pallas_call(
        pick_second_kernel,
        in_specs=[pl.BlockSpec(memory_space=pltpu.VMEM)],
        out_specs=[pl.BlockSpec(memory_space=pltpu.VMEM)] * 2,
        out_shape=[
            jax.ShapeDtypeStruct((owners, tiles, GROUP, LANES), jnp.bfloat16),
            jax.ShapeDtypeStruct((owners, LANES), jnp.int32),
        ],
        scratch_shapes=[
            pltpu.VMEM((owners * GROUP, LANES), jnp.float32),
            pltpu.SMEM((owners, LANES), jnp.int32),
            pltpu.SemaphoreType.DMA,
        ],
        compiler_params=pltpu.CompilerParams(vmem_limit_bytes=24 * 2**20),
        name="pick_second",
    )(spread)


def pick_first(index, spread, tiles):
    owners = spread.shape[0]
    return pl.pallas_call(
        lambda place_ref, x_ref, out_ref: copy_pieces(place_ref, x_ref, out_ref, 0),
        in_specs=[
            pl.BlockSpec(memory_space=pltpu.SMEM),
            pl.BlockSpec(memory_space=pltpu.VMEM),
        ],
        out_specs=pl.BlockSpec(memory_space=pltpu.VMEM),
        out_shape=jax.ShapeDtypeStruct((owners, tiles, GROUP, LANES), jnp.bfloat16),
        compiler_params=pltpu.CompilerParams(vmem_limit_bytes=24 * 2**20),
        name="pick_first",
    )(index, spread)


def correlate_kernel(scaling, win_ref, a_ref, *refs):
    windows = a_ref.shape[2]
    b_refs, table_hbm = refs[:windows], refs[windows]
    out_ref, stack_ref, table_ref, sem = refs[windows + 1 :]
    step = pl.program_id(0)
    last = pl.num_programs(0) - 1
    _, lane_groups, groups = b_refs[0].shape[:3]
    bins = lane_groups * LANES
    channels = groups * GROUP
    places = [
        [lax.rem(group + distance + groups - win_ref[0], groups) for group in range(groups)]
        for distance in range(windows)
    ]
    table_copy = pltpu.make_async_copy(table_hbm, table_ref, sem)

    def cross(lane_group, slot):
        lanes = pl.multiple_of(lane_group * LANES, LANES)
        a = [
            [a_ref[part, lane_group, w, step].astype(jnp.float32) for part in range(2)]
            for w in range(windows)
        ]
        for pair in range(groups // 2):
            b = [
                [
                    [
                        b_refs[w][part, lane_group, places[w][pair * 2 + half], step].astype(
                            jnp.float32
                        )
                        for part in range(2)
                    ]
                    for w in range(windows)
                ]
                for half in range(2)
            ]
            for i in range(GROUP):
                rows = [[None, None], [None, None]]
                for w in range(windows):
                    a0 = jnp.broadcast_to(a[w][0][i : i + 1], (GROUP, LANES))
                    a1 = jnp.broadcast_to(a[w][1][i : i + 1], (GROUP, LANES))
                    for half in range(2):
                        b0, b1 = b[half][w]
                        real = a0 * b0 + a1 * b1
                        imag = a1 * b0 - a0 * b1
                        if w:
                            real += rows[half][0]
                            imag += rows[half][1]
                        rows[half] = [real, imag]
                start = i * channels + pair * 2 * GROUP
                for part in range(2):
                    joined = jnp.concatenate([rows[0][part], rows[1][part]], axis=0)
                    stack_ref[
                        slot, start : start + 2 * GROUP, pl.ds(part * bins + lanes, LANES)
                    ] = joined.astype(jnp.bfloat16)

    def lagged(chunk, slot):
        columns = pl.ds(pl.multiple_of(chunk * 2 * LANES, 2 * LANES), 2 * LANES)
        rows = jnp.dot(stack_ref[slot], table_ref[:, columns], preferred_element_type=jnp.float32)
        rows = (rows * scaling).astype(jnp.bfloat16)
        out_ref[:, 0, :, columns] = rows.reshape(GROUP, channels, 2 * LANES)

    def run(with_cross, with_lagged):
        def body(chunk, carry):
            if with_lagged:
                lagged(chunk, lax.rem(step + 1, 2))
            if with_cross:
                cross(chunk * 2, lax.rem(step, 2))
                cross(chunk * 2 + 1, lax.rem(step, 2))
            return carry

        lax.fori_loop(0, lane_groups // 2, body, 0)

    @pl.when(step == 0)
    def _():
        table_copy.start()
        run(True, False)
        table_copy.wait()

    @pl.when(jnp.logical_and(step > 0, step < last))
    def _():
        run(True, True)

    @pl.when(step == last)
    def _():
        run(False, True)


def correlate(win, a, b, table):
    _, lane_groups, windows, tiles = a.shape[:4]
    channels = b[0].shape[2] * GROUP
    bins = lane_groups * LANES
    lags = table.shape[1]
    scaling = 1.0 / math.sqrt(windows * bins)
    whole = lambda x: pl.BlockSpec(x.shape, lambda t: (0,) * len(x.shape))
    return pl.pallas_call(
        functools.partial(correlate_kernel, scaling),
        grid=(tiles + 1,),
        in_specs=[pl.BlockSpec(memory_space=pltpu.SMEM)]
        + [whole(x) for x in (a, *b)]
        + [pl.BlockSpec(memory_space=pltpu.HBM)],
        out_specs=pl.BlockSpec(
            (GROUP, 1, channels, lags), lambda t: (0, jnp.maximum(t - 1, 0), 0, 0)
        ),
        out_shape=jax.ShapeDtypeStruct((GROUP, tiles, channels, lags), jnp.bfloat16),
        scratch_shapes=[
            pltpu.VMEM((2, GROUP * channels, 2 * bins), jnp.bfloat16),
            pltpu.VMEM(table.shape, table.dtype),
            pltpu.SemaphoreType.DMA,
        ],
        compiler_params=pltpu.CompilerParams(vmem_limit_bytes=58 * 2**20),
        name="correlate",
    )(win, a, *b, table)


def lag_rows_table(bin_total):
    bin_index = jnp.arange(bin_total, dtype=jnp.int32) + F0
    lag_index = jnp.arange(LAGS, dtype=jnp.int32) - LAGS // 2
    wrapped = bin_index[:, None] * lag_index[None, :] % NS
    phases = wrapped.astype(jnp.float32) * (2.0 * math.pi / NS)
    return jnp.concatenate([jnp.cos(phases), -jnp.sin(phases)], axis=0).astype(jnp.bfloat16)


def local(spectra, send_blocks, tile_slots):
    windows, owners = lax.axis_size("win"), lax.axis_size("pair")
    blocks, _, parts, channels, bins = spectra.shape
    tiles = tile_slots.shape[0]
    groups = channels // GROUP
    exchange = lambda x: lax.all_to_all(x, "pair", split_axis=0, concat_axis=0, tiled=True)
    pieces = (parts, bins // LANES, groups, tiles, GROUP, LANES)

    win = lax.axis_index("win").astype(jnp.int32).reshape(1)
    outgoing = whiten_spread(win, spectra, send_blocks[0].T, tile_slots.T)
    spread = exchange(outgoing.reshape(owners, blocks + 1, GROUP, LANES))
    spread, table = lax.optimization_barrier((spread, lag_rows_table(bins)))
    second, index = pick_second(spread, tiles)
    first = pick_first(index, spread, tiles)
    turn = [
        (w * owners + j, (w + j) % windows * owners + j)
        for w in range(windows)
        for j in range(owners)
    ]
    first = lax.ppermute(first, ("win", "pair"), turn)
    second = exchange(second)
    second, first = lax.optimization_barrier((second, first))
    b = [second]
    for distance in range(1, windows):
        step = [(w, (w + distance) % windows) for w in range(windows)]
        b.append(lax.ppermute(second, "win", step))
    a = exchange(first).reshape(pieces)
    return correlate(win, a, [x.reshape(pieces) for x in b], table)


def solution(mesh):
    in_specs = (P("pair", "win", None, None, None), P("pair", None, None), P("pair", None))
    out_specs = P("win", "pair", None, None)
    return jax.shard_map(local, mesh=mesh, in_specs=in_specs, out_specs=out_specs, check_vma=False)
```

time: 134 us -> 128 us (0.955)
  blocking collectives: 23.3 us -> 0 us
  waiting for transfers between devices: 27.9 us -> 46.8 us
  local copies, waits for them, and re-layouts: 8.45 us -> 1.14 us
  Pallas kernels: 19 us -> 22.4 us
  starting transfers between devices: 34.6 us -> 36.8 us
    ppermute x6 -> x4, waiting for transfers between devices: 0.02 us -> 30.9 us  [the longest x3 22.6 us: local(): b.append(lax.ppermute(second, 'win', step))]
    all_to_all x1 -> x0, blocking collectives: 23.3 us -> none  [local(): lax.all_to_all(x, axis, split_axis=0, concat_axis=0, tiled=True)]
    all_to_all x4 -> x3, waiting for transfers between devices: 27.9 us -> 15.9 us  [local(): lax.all_to_all(x, 'pair', split_axis=0, concat_axis=0, tiled=True)]
    unnamed x10, local copies, waits for them, and re-layouts: 6.94 us -> 1.14 us
    pallas_call x4, Pallas kernels: 19 us -> 22.4 us  [the longest x1 15.1 us: correlate(): pl.pallas_call(functools.partial(correlate_kernel, scaling), grid=(tiles...]
    all_to_all x4 -> x3, starting transfers between devices: 27 us -> 28.9 us  [local(): lax.all_to_all(x, 'pair', split_axis=0, concat_axis=0, tiled=True)]
    slice x2 -> x0, local copies, waits for them, and re-layouts: 1.5 us -> none  [local(): first, second = (both[:, :count], both[:, count:])]
    ppermute x6 -> x4, starting transfers between devices: 7.6 us -> 7.94 us  [the longest x3 4.73 us: local(): b.append(lax.ppermute(second, 'win', step))]
  transfers between devices with their start and end apart: 10 -> 7, of which waited for: 4 -> 5; matrix products, arithmetic and copies ran while one was open for 16% -> 16% of each run, Pallas kernels for 5% -> 1%
where the time goes in v3:
time: 128 us; the launch traced here: 127 us
  waiting for transfers between devices  46.8 us (37%)
  starting transfers between devices  36.8 us (29%)
  Pallas kernels  22.4 us (18%)
  other arithmetic  19.8 us (15%)
    all_to_all x3, starting transfers between devices, local(): lax.all_to_all(x, 'pair', split_axis=0, concat_axis=0, tiled=True)  28.9 us
    ppermute x3, waiting for transfers between devices, local(): b.append(lax.ppermute(second, 'win', step))  22.6 us
    another operation x1, other arithmetic  17.4 us
    all_to_all x3, waiting for transfers between devices, local(): lax.all_to_all(x, 'pair', split_axis=0, concat_axis=0, tiled=True)  15.9 us
    pallas_call x1, Pallas kernels, correlate(): pl.pallas_call(functools.partial(correlate_kernel, scaling), grid=(tiles...  15.1 us
    ppermute x1, waiting for transfers between devices, local(): first = lax.ppermute(first, ('win', 'pair'), turn)  8.29 us
    ppermute x3, starting transfers between devices, local(): b.append(lax.ppermute(second, 'win', step))  4.73 us
    ppermute x1, starting transfers between devices, local(): first = lax.ppermute(first, ('win', 'pair'), turn)  3.21 us
  transfers between devices with their start and end apart: 7, of which 5 were waited for; matrix products, arithmetic and copies ran while one was open for 16% of the time, Pallas kernels for 1%

profile of v3, /device:TPU:1, one launch (start us, length us, event | category | flops | bytes accessed | tf_op | source)
XLA Modules:
  0.0 127.0 jit_solution(14410351182715994903)
XLA Ops:
  0.0 2.9 %whiten_spread.1 = bf16[2,8,4,9,8,128]{5,4,3,2,1,0:T(8,128)(2,1)} custom-call(s32[1]{0:T(128)} %bitcast.win_ref, bf16[8,1,2,32,1024]{4,3,2,1,0:T(8,128)(2,1)} %x_ref.1, s32[2,64]{1,0:T(2,128)} %bitcast.17, s32[2,4]{1,0:T(2,128)} %bitcast.18), custom_call_target="tpu_custom_call" | custom-call | tf_op jit(solution)/shard_map/whiten_spread/pallas_call | solution.py:58
  2.9 13.0 %all-to-all-start = ((bf16[64,9,8,128]{3,2,1,0:T(8,128)(2,1)}), bf16[64,9,8,128]{3,2,1,0:T(8,128)(2,1)S(1)}, u32[]{:S(2)}, u32[]{:S(2)}) async-start(bf16[64,9,8,128]{3,2,1,0:T(8,128)(2,1)} %bitcast.11), calls=%async_computation | async-start | bytes 2359296 | tf_op jit(solution)/shard_map/all_to_all | solution.py:270
  15.9 17.4 %cosine_convert_fusion = (bf16[1024,1024]{1,0:T(8,128)(2,1)S(1)}, bf16[1024,1024]{1,0:T(8,128)(2,1)S(1)}) fusion(s32[1024]{0:T(1024)S(1)} %get-tuple-element.19, s32[1024]{0:T(1024)S(1)} %get-tuple-element.20), kind=kLoop, calls=%fused_computation.10 | loop fusion | flops 17825792 | bytes 4202496 | tf_op jit(solution)/shard_map/convert
  33.3 2.4 %pad_maximum_fusion.refs_4_ = bf16[2048,1024]{1,0:T(8,128)(2,1)} fusion(bf16[1024,1024]{1,0:T(8,128)(2,1)S(1)} %get-tuple-element.18, bf16[1024,1024]{1,0:T(8,128)(2,1)S(1)} %get-tuple-element.17), kind=kLoop, calls=%fused_computation.8 | loop fusion | flops 8388608 | bytes 8388608 | tf_op jit(solution)/shard_map/concatenate | solution.py:262
  35.8 11.5 %all-to-all-done.x_ref = bf16[64,9,8,128]{3,2,1,0:T(8,128)(2,1)S(1)} async-done(((bf16[64,9,8,128]{3,2,1,0:T(8,128)(2,1)}), bf16[64,9,8,128]{3,2,1,0:T(8,128)(2,1)S(1)}, u32[]{:S(2)}, u32[]{:S(2)}) %all-to-all-start) | async-done | bytes 1179680 | tf_op jit(solution)/shard_map/all_to_all | solution.py:270
  47.3 3.0 %pick_second.1 = (bf16[64,4,8,128]{3,2,1,0:T(8,128)(2,1)}, s32[64,128]{1,0:T(8,128)S(1)}) custom-call(bf16[64,9,8,128]{3,2,1,0:T(8,128)(2,1)S(1)} %all-to-all-done.x_ref), custom_call_target="tpu_custom_call" | custom-call | tf_op jit(solution)/shard_map/pick_second/pallas_call | solution.py:111
  50.2 6.2 %all-to-all-start.1 = ((bf16[64,4,8,128]{3,2,1,0:T(8,128)(2,1)}), bf16[64,4,8,128]{3,2,1,0:T(8,128)(2,1)S(1)}, u32[]{:S(2)}, u32[]{:S(2)}) async-start(bf16[64,4,8,128]{3,2,1,0:T(8,128)(2,1)} %get-tuple-element.12), calls=%async_computation.1 | async-start | bytes 1048576 | tf_op jit(solution)/shard_map/all_to_all | solution.py:270
  56.4 1.4 %pick_first.1 = bf16[64,4,8,128]{3,2,1,0:T(8,128)(2,1)S(1)} custom-call(s32[64,128]{1,0:T(8,128)S(1)} %get-tuple-element.13.place_ref, bf16[64,9,8,128]{3,2,1,0:T(8,128)(2,1)S(1)} %all-to-all-done.x_ref), custom_call_target="tpu_custom_call" | custom-call | tf_op jit(solution)/shard_map/pick_first/pallas_call | solution.py:131
  57.9 3.2 %collective-permute-start = (bf16[64,4,8,128]{3,2,1,0:T(8,128)(2,1)S(1)}, bf16[64,4,8,128]{3,2,1,0:T(8,128)(2,1)}, u32[]{:S(2)}, u32[]{:S(2)}) collective-permute-start(bf16[64,4,8,128]{3,2,1,0:T(8,128)(2,1)S(1)} %pick_first.1), channel_id=1, source_target_pairs={{0,0},{1,65},{2,130},{3,195},{4,4},{5,69},{6,134},{7,199},{8,8},{9... | collective-permute-start | bytes 1572872 | tf_op jit(solution)/shard_map/ppermute | solution.py:284
  61.1 8.3 %collective-permute-done = bf16[64,4,8,128]{3,2,1,0:T(8,128)(2,1)} collective-permute-done((bf16[64,4,8,128]{3,2,1,0:T(8,128)(2,1)S(1)}, bf16[64,4,8,128]{3,2,1,0:T(8,128)(2,1)}, u32[]{:S(2)}, u32[]{:S(2)}) %collective-permute-start) | collective-permute-done | bytes 524320 | tf_op jit(solution)/shard_map/ppermute | solution.py:284
  69.4 4.4 %all-to-all-done.1 = bf16[64,4,8,128]{3,2,1,0:T(8,128)(2,1)S(1)} async-done(((bf16[64,4,8,128]{3,2,1,0:T(8,128)(2,1)}), bf16[64,4,8,128]{3,2,1,0:T(8,128)(2,1)S(1)}, u32[]{:S(2)}, u32[]{:S(2)}) %all-to-all-start.1) | async-done | bytes 524320 | tf_op jit(solution)/shard_map/all_to_all | solution.py:270
  73.8 0.0 copy-start
  73.8 9.7 %all-to-all-start.2 = ((bf16[64,4,8,128]{3,2,1,0:T(8,128)(2,1)}), bf16[64,4,8,128]{3,2,1,0:T(8,128)(2,1)S(1)}, u32[]{:S(2)}, u32[]{:S(2)}) async-start(bf16[64,4,8,128]{3,2,1,0:T(8,128)(2,1)} %collective-permute-done), calls=%async_computation.2 | async-start | bytes 1048576 | tf_op jit(solution)/shard_map/all_to_all | solution.py:270
  83.5 2.2 %collective-permute-start.1 = (bf16[64,4,8,128]{3,2,1,0:T(8,128)(2,1)S(1)}, bf16[64,4,8,128]{3,2,1,0:T(8,128)(2,1)S(1)}, u32[]{:S(2)}, u32[]{:S(2)}) collective-permute-start(bf16[64,4,8,128]{3,2,1,0:T(8,128)(2,1)S(1)} %all-to-all-done.1), channel_id=1, source_target_pairs={{0,64},{64,128},{128,192},{192,0},{1,65},{65,129},{129,193},{193,1... | collective-permute-start | bytes 1572872 | tf_op jit(solution)/shard_map/ppermute | solution.py:290
  85.7 2.2 %collective-permute-start.2 = (bf16[64,4,8,128]{3,2,1,0:T(8,128)(2,1)S(1)}, bf16[64,4,8,128]{3,2,1,0:T(8,128)(2,1)S(1)}, u32[]{:S(2)}, u32[]{:S(2)}) collective-permute-start(bf16[64,4,8,128]{3,2,1,0:T(8,128)(2,1)S(1)} %all-to-all-done.1), channel_id=1, source_target_pairs={{0,128},{64,192},{128,0},{192,64},{1,129},{65,193},{129,1},{193,65... | collective-permute-start | bytes 1572872 | tf_op jit(solution)/shard_map/ppermute | solution.py:290
  87.9 0.2 collective-permute-start.3
  88.2 10.5 %collective-permute-done.1 = bf16[64,4,8,128]{3,2,1,0:T(8,128)(2,1)S(1)} collective-permute-done((bf16[64,4,8,128]{3,2,1,0:T(8,128)(2,1)S(1)}, bf16[64,4,8,128]{3,2,1,0:T(8,128)(2,1)S(1)}, u32[]{:S(2)}, u32[]{:S(2)}) %collective-permute-start.1) | collective-permute-done | bytes 524320 | tf_op jit(solution)/shard_map/ppermute | solution.py:290
  98.7 0.0 copy-start.2
  98.7 12.1 %collective-permute-done.2 = bf16[64,4,8,128]{3,2,1,0:T(8,128)(2,1)S(1)} collective-permute-done((bf16[64,4,8,128]{3,2,1,0:T(8,128)(2,1)S(1)}, bf16[64,4,8,128]{3,2,1,0:T(8,128)(2,1)S(1)}, u32[]{:S(2)}, u32[]{:S(2)}) %collective-permute-start.2) | collective-permute-done | bytes 524320 | tf_op jit(solution)/shard_map/ppermute | solution.py:290
  110.8 0.0 copy-start.3
  110.8 0.0 collective-permute-done.3
  110.8 0.0 copy-start.4
  110.8 0.0 all-to-all-done.2
  110.8 0.0 copy-start.1
  110.8 0.0 copy-done
  110.8 0.0 copy-done.2
  110.8 0.8 copy-done.3
  111.6 0.2 copy-done.4
  111.8 0.2 copy-done.1
  111.9 15.1 %correlate.1 = bf16[8,4,32,1024]{3,2,1,0:T(8,128)(2,1)} custom-call(s32[1]{0:T(128)} %bitcast.win_ref, bf16[2,8,4,4,8,128]{5,4,3,2,1,0:T(8,128)(2,1)} %bitcast.13, bf16[2,8,4,4,8,128]{5,4,3,2,1,0:T(8,128)(2,1)} %bitcast.12, bf16[2,8,4,4,8,128]{5,4,3,2,1,0:T(8,128)(2,1)} %bitcast.14, bf16[2,8,4,4,8,128]{5,4,3,2,1,0:T(8,128)(2,1)} %bitcast.15, ...), custom_call_target="tpu_custom_call" | custom-call | tf_op jit(solution)/shard_map/correlate/pallas_call | solution.py:237
  (1 shorter events, 0.0 us)
Async XLA Ops:
  2.9 44.4 %all-to-all-start = ((bf16[64,9,8,128]{3,2,1,0:T(8,128)(2,1)}), bf16[64,9,8,128]{3,2,1,0:T(8,128)(2,1)S(1)}, u32[]{:S(2)}, u32[]{:S(2)}) async-start(bf16[64,9,8,128]{3,2,1,0:T(8,128)(2,1)} %bitcast.11), calls=%async_computation | async-start | bytes 2359296 | tf_op jit(solution)/shard_map/all_to_all | solution.py:270
  50.2 23.5 %all-to-all-start.1 = ((bf16[64,4,8,128]{3,2,1,0:T(8,128)(2,1)}), bf16[64,4,8,128]{3,2,1,0:T(8,128)(2,1)S(1)}, u32[]{:S(2)}, u32[]{:S(2)}) async-start(bf16[64,4,8,128]{3,2,1,0:T(8,128)(2,1)} %get-tuple-element.12), calls=%async_computation.1 | async-start | bytes 1048576 | tf_op jit(solution)/shard_map/all_to_all | solution.py:270
  57.9 11.5 %collective-permute-start = (bf16[64,4,8,128]{3,2,1,0:T(8,128)(2,1)S(1)}, bf16[64,4,8,128]{3,2,1,0:T(8,128)(2,1)}, u32[]{:S(2)}, u32[]{:S(2)}) collective-permute-start(bf16[64,4,8,128]{3,2,1,0:T(8,128)(2,1)S(1)} %pick_first.1), channel_id=1, source_target_pairs={{0,0},{1,65},{2,130},{3,195},{4,4},{5,69},{6,134},{7,199},{8,8},{9... | collective-permute-start | bytes 1572872 | tf_op jit(solution)/shard_map/ppermute | solution.py:284
  73.8 37.0 %copy-start = (bf16[64,4,8,128]{3,2,1,0:T(8,128)(2,1)}, bf16[64,4,8,128]{3,2,1,0:T(8,128)(2,1)S(1)}, u32[]{:S(2)}) copy-start(bf16[64,4,8,128]{3,2,1,0:T(8,128)(2,1)S(1)} %all-to-all-done.1) | copy-start | bytes 1572868
  73.8 37.0 %all-to-all-start.2 = ((bf16[64,4,8,128]{3,2,1,0:T(8,128)(2,1)}), bf16[64,4,8,128]{3,2,1,0:T(8,128)(2,1)S(1)}, u32[]{:S(2)}, u32[]{:S(2)}) async-start(bf16[64,4,8,128]{3,2,1,0:T(8,128)(2,1)} %collective-permute-done), calls=%async_computation.2 | async-start | bytes 1048576 | tf_op jit(solution)/shard_map/all_to_all | solution.py:270
  83.5 15.2 %collective-permute-start.1 = (bf16[64,4,8,128]{3,2,1,0:T(8,128)(2,1)S(1)}, bf16[64,4,8,128]{3,2,1,0:T(8,128)(2,1)S(1)}, u32[]{:S(2)}, u32[]{:S(2)}) collective-permute-start(bf16[64,4,8,128]{3,2,1,0:T(8,128)(2,1)S(1)} %all-to-all-done.1), channel_id=1, source_target_pairs={{0,64},{64,128},{128,192},{192,0},{1,65},{65,129},{129,193},{193,1... | collective-permute-start | bytes 1572872 | tf_op jit(solution)/shard_map/ppermute | solution.py:290
  85.7 25.1 %collective-permute-start.2 = (bf16[64,4,8,128]{3,2,1,0:T(8,128)(2,1)S(1)}, bf16[64,4,8,128]{3,2,1,0:T(8,128)(2,1)S(1)}, u32[]{:S(2)}, u32[]{:S(2)}) collective-permute-start(bf16[64,4,8,128]{3,2,1,0:T(8,128)(2,1)S(1)} %all-to-all-done.1), channel_id=1, source_target_pairs={{0,128},{64,192},{128,0},{192,64},{1,129},{65,193},{129,1},{193,65... | collective-permute-start | bytes 1572872 | tf_op jit(solution)/shard_map/ppermute | solution.py:290
  87.9 22.8 %collective-permute-start.3 = (bf16[64,4,8,128]{3,2,1,0:T(8,128)(2,1)S(1)}, bf16[64,4,8,128]{3,2,1,0:T(8,128)(2,1)S(1)}, u32[]{:S(2)}, u32[]{:S(2)}) collective-permute-start(bf16[64,4,8,128]{3,2,1,0:T(8,128)(2,1)S(1)} %all-to-all-done.1), channel_id=1, source_target_pairs={{0,192},{64,0},{128,64},{192,128},{1,193},{65,1},{129,65},{193,129... | collective-permute-start | bytes 1572872 | tf_op jit(solution)/shard_map/ppermute | solution.py:290
  98.7 12.1 %copy-start.2 = (bf16[64,4,8,128]{3,2,1,0:T(8,128)(2,1)}, bf16[64,4,8,128]{3,2,1,0:T(8,128)(2,1)S(1)}, u32[]{:S(2)}) copy-start(bf16[64,4,8,128]{3,2,1,0:T(8,128)(2,1)S(1)} %collective-permute-done.1) | copy-start | bytes 1572868
  110.8 0.8 copy-start.3
  110.8 1.0 copy-start.4
  110.8 1.2 copy-start.1

commit v4 on v3

--- a/solution.py
+++ b/solution.py
@@ -141,23 +141,23 @@
     )(index, spread)
 
 
-def correlate_kernel(scaling, win_ref, a_ref, *refs):
-    windows = a_ref.shape[2]
-    b_refs, table_hbm = refs[:windows], refs[windows]
-    out_ref, stack_ref, table_ref, sem = refs[windows + 1 :]
+def correlate_kernel(
+    scaling, win_ref, a_ref, b_ref, table_hbm, out_ref, stack_ref, table_ref, sem
+):
     step = pl.program_id(0)
     last = pl.num_programs(0) - 1
-    _, lane_groups, groups = b_refs[0].shape[:3]
+    windows, _, lane_groups, groups = b_ref.shape[:4]
     bins = lane_groups * LANES
     channels = groups * GROUP
+    sources = [lax.rem(win_ref[0] + windows - d, windows) for d in range(windows)]
     places = [
-        [lax.rem(group + distance + groups - win_ref[0], groups) for group in range(groups)]
-        for distance in range(windows)
+        [lax.rem(group + groups - source, groups) for group in range(groups)]
+        for source in sources
     ]
     table_copy = pltpu.make_async_copy(table_hbm, table_ref, sem)
 
     def cross(lane_group, slot):
-        lanes = pl.multiple_of(lane_group * LANES, LANES)
+        lanes = lane_group * LANES
         a = [
             [a_ref[part, lane_group, w, step].astype(jnp.float32) for part in range(2)]
             for w in range(windows)
@@ -166,9 +166,9 @@
             b = [
                 [
                     [
-                        b_refs[w][part, lane_group, places[w][pair * 2 + half], step].astype(
-                            jnp.float32
-                        )
+                        b_ref[
+                            sources[w], part, lane_group, places[w][pair * 2 + half], step
+                        ].astype(jnp.float32)
                         for part in range(2)
                     ]
                     for w in range(windows)
@@ -196,21 +196,18 @@
                     ] = joined.astype(jnp.bfloat16)
 
     def lagged(chunk, slot):
-        columns = pl.ds(pl.multiple_of(chunk * 2 * LANES, 2 * LANES), 2 * LANES)
+        columns = pl.ds(chunk * 2 * LANES, 2 * LANES)
         rows = jnp.dot(stack_ref[slot], table_ref[:, columns], preferred_element_type=jnp.float32)
         rows = (rows * scaling).astype(jnp.bfloat16)
         out_ref[:, 0, :, columns] = rows.reshape(GROUP, channels, 2 * LANES)
 
     def run(with_cross, with_lagged):
-        def body(chunk, carry):
+        for chunk in range(lane_groups // 2):
             if with_lagged:
                 lagged(chunk, lax.rem(step + 1, 2))
             if with_cross:
                 cross(chunk * 2, lax.rem(step, 2))
                 cross(chunk * 2 + 1, lax.rem(step, 2))
-            return carry
-
-        lax.fori_loop(0, lane_groups // 2, body, 0)
 
     @pl.when(step == 0)
     def _():
@@ -229,7 +226,7 @@
 
 def correlate(win, a, b, table):
     _, lane_groups, windows, tiles = a.shape[:4]
-    channels = b[0].shape[2] * GROUP
+    channels = b.shape[3] * GROUP
     bins = lane_groups * LANES
     lags = table.shape[1]
     scaling = 1.0 / math.sqrt(windows * bins)
@@ -238,7 +235,7 @@
         functools.partial(correlate_kernel, scaling),
         grid=(tiles + 1,),
         in_specs=[pl.BlockSpec(memory_space=pltpu.SMEM)]
-        + [whole(x) for x in (a, *b)]
+        + [whole(x) for x in (a, b)]
         + [pl.BlockSpec(memory_space=pltpu.HBM)],
         out_specs=pl.BlockSpec(
             (GROUP, 1, channels, lags), lambda t: (0, jnp.maximum(t - 1, 0), 0, 0)
@@ -249,9 +246,9 @@
             pltpu.VMEM(table.shape, table.dtype),
             pltpu.SemaphoreType.DMA,
         ],
-        compiler_params=pltpu.CompilerParams(vmem_limit_bytes=58 * 2**20),
+        compiler_params=pltpu.CompilerParams(vmem_limit_bytes=48 * 2**20),
         name="correlate",
-    )(win, a, *b, table)
+    )(win, a, b, table)
 
 
 def lag_rows_table(bin_total):
@@ -284,12 +281,9 @@
     first = lax.ppermute(first, ("win", "pair"), turn)
     second = exchange(second)
     second, first = lax.optimization_barrier((second, first))
-    b = [second]
-    for distance in range(1, windows):
-        step = [(w, (w + distance) % windows) for w in range(windows)]
-        b.append(lax.ppermute(second, "win", step))
+    b = lax.all_gather(second, "win", axis=0, tiled=False).reshape((windows,) + pieces)
     a = exchange(first).reshape(pieces)
-    return correlate(win, a, [x.reshape(pieces) for x in b], table)
+    return correlate(win, a, b, table)
 
 
 def solution(mesh):

time: 128 us -> 135 us (1.055)
  blocking collectives: 0 us -> 26.8 us
  waiting for transfers between devices: 46.8 us -> 31.7 us
  starting transfers between devices: 36.8 us -> 22.4 us
  between operations: 0.1 us -> 13.5 us
  Pallas kernels: 22.4 us -> 17.7 us
    all_to_all x0 -> x1, blocking collectives: none -> 26.8 us  [local(): lax.all_to_all(x, 'pair', split_axis=0, concat_axis=0, tiled=True)]
    ppermute x3 -> x0, waiting for transfers between devices: 22.6 us -> none  [local(): b.append(lax.ppermute(second, 'win', step))]
    all_to_all x3 -> x2, starting transfers between devices: 28.9 us -> 19.2 us  [local(): lax.all_to_all(x, 'pair', split_axis=0, concat_axis=0, tiled=True)]
    all_gather x0 -> x1, waiting for transfers between devices: none -> 7.51 us  [local(): lax.all_gather(second, 'win', axis=0, tiled=False)]
    ppermute x3 -> x0, starting transfers between devices: 4.73 us -> none  [local(): b.append(lax.ppermute(second, 'win', step))]
    pallas_call x1, Pallas kernels: 15.1 us -> 10.4 us  [correlate(): pl.pallas_call(functools.partial(correlate_kernel, scaling), grid=(tiles...]
    all_to_all x3 -> x2, waiting for transfers between devices: 15.9 us -> 15.9 us  [local(): lax.all_to_all(x, 'pair', split_axis=0, concat_axis=0, tiled=True)]
  transfers between devices with their start and end apart: 7 -> 4, of which waited for: 5 -> 4; matrix products, arithmetic and copies ran while one was open for 16% -> 15% of each run, Pallas kernels for 1% -> 1%
where the time goes in v4:
time: 135 us; the launch traced here: 134 us
  waiting for transfers between devices  31.7 us (23%)
  blocking collectives  26.8 us (20%)
  starting transfers between devices  22.4 us (17%)
  other arithmetic  19.8 us (15%)
  Pallas kernels  17.7 us (13%)
  between operations  13.5 us (10%)
  local copies, waits for them, and re-layouts  2.38 us (2%)
    all_to_all x1, blocking collectives, local(): lax.all_to_all(x, 'pair', split_axis=0, concat_axis=0, tiled=True)  26.8 us
    all_to_all x2, starting transfers between devices, local(): lax.all_to_all(x, 'pair', split_axis=0, concat_axis=0, tiled=True)  19.2 us
    another operation x1, other arithmetic  17.4 us
    all_to_all x2, waiting for transfers between devices, local(): lax.all_to_all(x, 'pair', split_axis=0, concat_axis=0, tiled=True)  15.9 us
    pallas_call x1, Pallas kernels, correlate(): pl.pallas_call(functools.partial(correlate_kernel, scaling), grid=(tiles...  10.4 us
    ppermute x1, waiting for transfers between devices, local(): first = lax.ppermute(first, ('win', 'pair'), turn)  8.29 us
    all_gather x1, waiting for transfers between devices, local(): lax.all_gather(second, 'win', axis=0, tiled=False)  7.51 us
    ppermute x1, starting transfers between devices, local(): first = lax.ppermute(first, ('win', 'pair'), turn)  3.21 us
  transfers between devices with their start and end apart: 4, of which 4 were waited for; matrix products, arithmetic and copies ran while one was open for 15% of the time, Pallas kernels for 1%

profile of v4, /device:TPU:1, one launch (start us, length us, event | category | flops | bytes accessed | tf_op | source)
XLA Modules:
  0.0 134.4 jit_solution(4598508900251504930)
XLA Ops:
  6.5 2.9 %whiten_spread.1 = bf16[2,8,4,9,8,128]{5,4,3,2,1,0:T(8,128)(2,1)} custom-call(s32[1]{0:T(128)} %bitcast.win_ref, bf16[8,1,2,32,1024]{4,3,2,1,0:T(8,128)(2,1)} %x_ref.1, s32[2,64]{1,0:T(2,128)} %bitcast.11, s32[2,4]{1,0:T(2,128)} %bitcast.12), custom_call_target="tpu_custom_call" | custom-call | tf_op jit(solution)/shard_map/whiten_spread/pallas_call | solution.py:58
  9.5 13.0 %all-to-all-start = ((bf16[64,9,8,128]{3,2,1,0:T(8,128)(2,1)}), bf16[64,9,8,128]{3,2,1,0:T(8,128)(2,1)S(1)}, u32[]{:S(2)}, u32[]{:S(2)}) async-start(bf16[64,9,8,128]{3,2,1,0:T(8,128)(2,1)} %bitcast.10), calls=%async_computation | async-start | bytes 2359296 | tf_op jit(solution)/shard_map/all_to_all | solution.py:267
  22.5 17.4 %cosine_convert_fusion = (bf16[1024,1024]{1,0:T(8,128)(2,1)S(1)}, bf16[1024,1024]{1,0:T(8,128)(2,1)S(1)}) fusion(s32[1024]{0:T(1024)S(1)} %get-tuple-element.19, s32[1024]{0:T(1024)S(1)} %get-tuple-element.20), kind=kLoop, calls=%fused_computation.10 | loop fusion | flops 17825792 | bytes 4202496 | tf_op jit(solution)/shard_map/convert
  39.9 2.4 %pad_maximum_fusion.table_hbm = bf16[2048,1024]{1,0:T(8,128)(2,1)} fusion(bf16[1024,1024]{1,0:T(8,128)(2,1)S(1)} %get-tuple-element.18, bf16[1024,1024]{1,0:T(8,128)(2,1)S(1)} %get-tuple-element.17), kind=kLoop, calls=%fused_computation.8 | loop fusion | flops 8388608 | bytes 8388608 | tf_op jit(solution)/shard_map/concatenate | solution.py:259
  42.3 11.5 %all-to-all-done.x_ref = bf16[64,9,8,128]{3,2,1,0:T(8,128)(2,1)S(1)} async-done(((bf16[64,9,8,128]{3,2,1,0:T(8,128)(2,1)}), bf16[64,9,8,128]{3,2,1,0:T(8,128)(2,1)S(1)}, u32[]{:S(2)}, u32[]{:S(2)}) %all-to-all-start) | async-done | bytes 1179680 | tf_op jit(solution)/shard_map/all_to_all | solution.py:267
  53.8 3.0 %pick_second.1 = (bf16[64,4,8,128]{3,2,1,0:T(8,128)(2,1)}, s32[64,128]{1,0:T(8,128)S(1)}) custom-call(bf16[64,9,8,128]{3,2,1,0:T(8,128)(2,1)S(1)} %all-to-all-done.x_ref), custom_call_target="tpu_custom_call" | custom-call | tf_op jit(solution)/shard_map/pick_second/pallas_call | solution.py:111
  56.8 6.2 %all-to-all-start.1 = ((bf16[64,4,8,128]{3,2,1,0:T(8,128)(2,1)}), bf16[64,4,8,128]{3,2,1,0:T(8,128)(2,1)S(1)}, u32[]{:S(2)}, u32[]{:S(2)}) async-start(bf16[64,4,8,128]{3,2,1,0:T(8,128)(2,1)} %get-tuple-element.12), calls=%async_computation.1 | async-start | bytes 1048576 | tf_op jit(solution)/shard_map/all_to_all | solution.py:267
  63.0 0.0 all-gather.3.cloned.1.call-start
  63.0 1.4 %pick_first.1 = bf16[64,4,8,128]{3,2,1,0:T(8,128)(2,1)S(1)} custom-call(s32[64,128]{1,0:T(8,128)S(1)} %get-tuple-element.13.place_ref, bf16[64,9,8,128]{3,2,1,0:T(8,128)(2,1)S(1)} %all-to-all-done.x_ref), custom_call_target="tpu_custom_call" | custom-call | tf_op jit(solution)/shard_map/pick_first/pallas_call | solution.py:131
  64.5 3.2 %collective-permute-start = (bf16[64,4,8,128]{3,2,1,0:T(8,128)(2,1)S(1)}, bf16[64,4,8,128]{3,2,1,0:T(8,128)(2,1)S(1)}, u32[]{:S(2)}, u32[]{:S(2)}) collective-permute-start(bf16[64,4,8,128]{3,2,1,0:T(8,128)(2,1)S(1)} %pick_first.1), channel_id=1, source_target_pairs={{0,0},{1,65},{2,130},{3,195},{4,4},{5,69},{6,134},{7,199},{8,8},{9... | collective-permute-start | bytes 1572872 | tf_op jit(solution)/shard_map/ppermute | solution.py:281
  67.7 8.3 %collective-permute-done = bf16[64,4,8,128]{3,2,1,0:T(8,128)(2,1)S(1)} collective-permute-done((bf16[64,4,8,128]{3,2,1,0:T(8,128)(2,1)S(1)}, bf16[64,4,8,128]{3,2,1,0:T(8,128)(2,1)S(1)}, u32[]{:S(2)}, u32[]{:S(2)}) %collective-permute-start) | collective-permute-done | bytes 524320 | tf_op jit(solution)/shard_map/ppermute | solution.py:281
  76.0 4.3 %all-to-all-done.1 = bf16[64,4,8,128]{3,2,1,0:T(8,128)(2,1)S(1)} async-done(((bf16[64,4,8,128]{3,2,1,0:T(8,128)(2,1)}), bf16[64,4,8,128]{3,2,1,0:T(8,128)(2,1)S(1)}, u32[]{:S(2)}, u32[]{:S(2)}) %all-to-all-start.1) | async-done | bytes 524320 | tf_op jit(solution)/shard_map/all_to_all | solution.py:267
  80.3 0.0 copy-start.1
  80.3 0.8 copy-done.1
  81.1 0.0 all-gather.3.cloned.1.call-update
  81.1 26.8 %all_to_all.15 = bf16[64,4,8,128]{3,2,1,0:T(8,128)(2,1)S(1)} all-to-all(bf16[64,4,8,128]{3,2,1,0:T(8,128)(2,1)S(1)} %collective-permute-done), channel_id=1, replica_groups=mesh['win'=4,'pair'=64] {'pair'}, dimensions={0} | all-to-all | bytes 1048576 | tf_op jit(solution)/shard_map/all_to_all | solution.py:267
  108.0 7.5 %all-gather.3.cloned.1.call-done = bf16[256,4,8,128]{3,2,1,0:T(8,128)(2,1)} async-done(((bf16[64,4,8,128]{3,2,1,0:T(8,128)(2,1)}), bf16[256,4,8,128]{3,2,1,0:T(8,128)(2,1)}) %all-gather.3.cloned.1.call-update) | async-done | bytes 2097168 | tf_op jit(solution)/shard_map/all_gather | solution.py:284
  115.5 0.0 copy-start
  115.5 1.6 %copy-done = bf16[256,4,8,128]{3,2,1,0:T(8,128)(2,1)S(1)} copy-done((bf16[256,4,8,128]{3,2,1,0:T(8,128)(2,1)S(1)}, bf16[256,4,8,128]{3,2,1,0:T(8,128)(2,1)}, u32[]{:S(2)}) %copy-start) | copy-done | bytes 2097176
  117.1 10.4 %correlate.1 = bf16[8,4,32,1024]{3,2,1,0:T(8,128)(2,1)} custom-call(s32[1]{0:T(128)} %bitcast.win_ref, bf16[2,8,4,4,8,128]{5,4,3,2,1,0:T(8,128)(2,1)S(1)} %bitcast.9, bf16[4,2,8,4,4,8,128]{6,5,4,3,2,1,0:T(8,128)(2,1)S(1)} %bitcast.8, bf16[2048,1024]{1,0:T(8,128)(2,1)} %pad_maximum_fusion.table_hbm), custom_call_target="tpu_custom_call" | custom-call | tf_op jit(solution)/shard_map/correlate/pallas_call | solution.py:234
  (1 shorter events, 0.0 us)
Async XLA Ops:
  9.5 44.4 %all-to-all-start = ((bf16[64,9,8,128]{3,2,1,0:T(8,128)(2,1)}), bf16[64,9,8,128]{3,2,1,0:T(8,128)(2,1)S(1)}, u32[]{:S(2)}, u32[]{:S(2)}) async-start(bf16[64,9,8,128]{3,2,1,0:T(8,128)(2,1)} %bitcast.10), calls=%async_computation | async-start | bytes 2359296 | tf_op jit(solution)/shard_map/all_to_all | solution.py:267
  56.8 23.5 %all-to-all-start.1 = ((bf16[64,4,8,128]{3,2,1,0:T(8,128)(2,1)}), bf16[64,4,8,128]{3,2,1,0:T(8,128)(2,1)S(1)}, u32[]{:S(2)}, u32[]{:S(2)}) async-start(bf16[64,4,8,128]{3,2,1,0:T(8,128)(2,1)} %get-tuple-element.12), calls=%async_computation.1 | async-start | bytes 1048576 | tf_op jit(solution)/shard_map/all_to_all | solution.py:267
  63.0 52.5 %all-gather.3.cloned.1.call-start = ((), (), s32[]{:S(2)}) async-start(), calls=%async_computation.3 | async-start | bytes 2621440 | tf_op jit(solution)/shard_map/all_gather | solution.py:284
  64.5 11.5 %collective-permute-start = (bf16[64,4,8,128]{3,2,1,0:T(8,128)(2,1)S(1)}, bf16[64,4,8,128]{3,2,1,0:T(8,128)(2,1)S(1)}, u32[]{:S(2)}, u32[]{:S(2)}) collective-permute-start(bf16[64,4,8,128]{3,2,1,0:T(8,128)(2,1)S(1)} %pick_first.1), channel_id=1, source_target_pairs={{0,0},{1,65},{2,130},{3,195},{4,4},{5,69},{6,134},{7,199},{8,8},{9... | collective-permute-start | bytes 1572872 | tf_op jit(solution)/shard_map/ppermute | solution.py:281
  80.3 0.8 copy-start.1
  115.5 1.6 %copy-start = (bf16[256,4,8,128]{3,2,1,0:T(8,128)(2,1)S(1)}, bf16[256,4,8,128]{3,2,1,0:T(8,128)(2,1)}, u32[]{:S(2)}) copy-start(bf16[256,4,8,128]{3,2,1,0:T(8,128)(2,1)} %all-gather.3.cloned.1.call-done) | copy-start | bytes 6291460
Sparse Core Ops, SparseCore 0:
  81.2 34.1 all-gather.2

commit v5 on v3

--- a/solution.py
+++ b/solution.py
@@ -15,6 +15,7 @@
 LANES = 128
 GROUP = 8
 HALF = 64
+SETTLE_FLOPS = 15 * 10**9
 
 
 def whiten_kernel(win_ref, x_ref, sent_ref, slots_ref, out_ref, table_ref):
@@ -157,7 +158,7 @@
     table_copy = pltpu.make_async_copy(table_hbm, table_ref, sem)
 
     def cross(lane_group, slot):
-        lanes = pl.multiple_of(lane_group * LANES, LANES)
+        lanes = lane_group * LANES
         a = [
             [a_ref[part, lane_group, w, step].astype(jnp.float32) for part in range(2)]
             for w in range(windows)
@@ -196,21 +197,18 @@
                     ] = joined.astype(jnp.bfloat16)
 
     def lagged(chunk, slot):
-        columns = pl.ds(pl.multiple_of(chunk * 2 * LANES, 2 * LANES), 2 * LANES)
+        columns = pl.ds(chunk * 2 * LANES, 2 * LANES)
         rows = jnp.dot(stack_ref[slot], table_ref[:, columns], preferred_element_type=jnp.float32)
         rows = (rows * scaling).astype(jnp.bfloat16)
         out_ref[:, 0, :, columns] = rows.reshape(GROUP, channels, 2 * LANES)
 
     def run(with_cross, with_lagged):
-        def body(chunk, carry):
+        for chunk in range(lane_groups // 2):
             if with_lagged:
                 lagged(chunk, lax.rem(step + 1, 2))
             if with_cross:
                 cross(chunk * 2, lax.rem(step, 2))
                 cross(chunk * 2 + 1, lax.rem(step, 2))
-            return carry
-
-        lax.fori_loop(0, lane_groups // 2, body, 0)
 
     @pl.when(step == 0)
     def _():
@@ -249,9 +247,26 @@
             pltpu.VMEM(table.shape, table.dtype),
             pltpu.SemaphoreType.DMA,
         ],
-        compiler_params=pltpu.CompilerParams(vmem_limit_bytes=58 * 2**20),
+        compiler_params=pltpu.CompilerParams(vmem_limit_bytes=48 * 2**20),
         name="correlate",
     )(win, a, *b, table)
+
+
+def settle_kernel(win_ref, *refs):
+    refs[-1][0] = win_ref[0]
+
+
+def settle(win, arrays):
+    return pl.pallas_call(
+        settle_kernel,
+        in_specs=[pl.BlockSpec(memory_space=pltpu.SMEM)]
+        + [pl.BlockSpec(memory_space=pl.ANY)] * len(arrays),
+        out_specs=pl.BlockSpec(memory_space=pltpu.SMEM),
+        out_shape=jax.ShapeDtypeStruct(win.shape, win.dtype),
+        compiler_params=pltpu.CompilerParams(vmem_limit_bytes=2**20),
+        cost_estimate=pl.CostEstimate(flops=SETTLE_FLOPS, bytes_accessed=0, transcendentals=0),
+        name="settle",
+    )(win, *arrays)
 
 
 def lag_rows_table(bin_total):
@@ -288,6 +303,7 @@
     for distance in range(1, windows):
         step = [(w, (w + distance) % windows) for w in range(windows)]
         b.append(lax.ppermute(second, "win", step))
+    win = settle(win, b[1:])
     a = exchange(first).reshape(pieces)
     return correlate(win, a, [x.reshape(pieces) for x in b], table)
 

time: 128 us -> 118 us (0.922)
  waiting for transfers between devices: 46.8 us -> 41 us
  Pallas kernels: 22.4 us -> 18.9 us
    ppermute x3, waiting for transfers between devices: 22.6 us -> 12.1 us  [local(): b.append(lax.ppermute(second, 'win', step))]
    all_to_all x3, waiting for transfers between devices: 15.9 us -> 20.6 us  [local(): lax.all_to_all(x, 'pair', split_axis=0, concat_axis=0, tiled=True)]
    pallas_call x1, Pallas kernels: 15.1 us -> 11.1 us  [correlate(): pl.pallas_call(functools.partial(correlate_kernel, scaling), grid=(tiles...]
  transfers between devices with their start and end apart: 7 -> 7, of which waited for: 5 -> 5; matrix products, arithmetic and copies ran while one was open for 16% -> 17% of each run, Pallas kernels for 1% -> 2%
where the time goes in v5:
time: 118 us; the launch traced here: 117 us
  waiting for transfers between devices  41 us (35%)
  starting transfers between devices  37.2 us (32%)
  other arithmetic  19.8 us (17%)
  Pallas kernels  18.9 us (16%)
    all_to_all x3, starting transfers between devices, local(): lax.all_to_all(x, 'pair', split_axis=0, concat_axis=0, tiled=True)  29 us
    all_to_all x3, waiting for transfers between devices, local(): lax.all_to_all(x, 'pair', split_axis=0, concat_axis=0, tiled=True)  20.6 us
    another operation x1, other arithmetic  17.4 us
    ppermute x3, waiting for transfers between devices, local(): b.append(lax.ppermute(second, 'win', step))  12.1 us
    pallas_call x1, Pallas kernels, correlate(): pl.pallas_call(functools.partial(correlate_kernel, scaling), grid=(tiles...  11.1 us
    ppermute x1, waiting for transfers between devices, local(): first = lax.ppermute(first, ('win', 'pair'), turn)  8.29 us
    ppermute x3, starting transfers between devices, local(): b.append(lax.ppermute(second, 'win', step))  4.99 us
    ppermute x1, starting transfers between devices, local(): first = lax.ppermute(first, ('win', 'pair'), turn)  3.21 us
  transfers between devices with their start and end apart: 7, of which 5 were waited for; matrix products, arithmetic and copies ran while one was open for 17% of the time, Pallas kernels for 2%

profile of v5, /device:TPU:1, one launch (start us, length us, event | category | flops | bytes accessed | tf_op | source)
XLA Modules:
  0.0 117.1 jit_solution(8213107623348892032)
XLA Ops:
  0.0 2.9 %whiten_spread.1 = bf16[2,8,4,9,8,128]{5,4,3,2,1,0:T(8,128)(2,1)} custom-call(s32[1]{0:T(128)} %bitcast.win_ref, bf16[8,1,2,32,1024]{4,3,2,1,0:T(8,128)(2,1)} %x_ref.1, s32[2,64]{1,0:T(2,128)} %bitcast.17, s32[2,4]{1,0:T(2,128)} %bitcast.18), custom_call_target="tpu_custom_call" | custom-call | tf_op jit(solution)/shard_map/whiten_spread/pallas_call | solution.py:59
  2.9 13.0 %all-to-all-start = ((bf16[64,9,8,128]{3,2,1,0:T(8,128)(2,1)}), bf16[64,9,8,128]{3,2,1,0:T(8,128)(2,1)S(1)}, u32[]{:S(2)}, u32[]{:S(2)}) async-start(bf16[64,9,8,128]{3,2,1,0:T(8,128)(2,1)} %bitcast.16), calls=%async_computation | async-start | bytes 2359296 | tf_op jit(solution)/shard_map/all_to_all | solution.py:285
  15.9 17.4 %cosine_convert_fusion = (bf16[1024,1024]{1,0:T(8,128)(2,1)S(1)}, bf16[1024,1024]{1,0:T(8,128)(2,1)S(1)}) fusion(s32[1024]{0:T(1024)S(1)} %get-tuple-element.19, s32[1024]{0:T(1024)S(1)} %get-tuple-element.20), kind=kLoop, calls=%fused_computation.10 | loop fusion | flops 17825792 | bytes 4202496 | tf_op jit(solution)/shard_map/convert
  33.4 2.4 %pad_maximum_fusion.refs_4_ = bf16[2048,1024]{1,0:T(8,128)(2,1)} fusion(bf16[1024,1024]{1,0:T(8,128)(2,1)S(1)} %get-tuple-element.18, bf16[1024,1024]{1,0:T(8,128)(2,1)S(1)} %get-tuple-element.17), kind=kLoop, calls=%fused_computation.8 | loop fusion | flops 8388608 | bytes 8388608 | tf_op jit(solution)/shard_map/concatenate | solution.py:277
  35.7 11.5 %all-to-all-done.x_ref = bf16[64,9,8,128]{3,2,1,0:T(8,128)(2,1)S(1)} async-done(((bf16[64,9,8,128]{3,2,1,0:T(8,128)(2,1)}), bf16[64,9,8,128]{3,2,1,0:T(8,128)(2,1)S(1)}, u32[]{:S(2)}, u32[]{:S(2)}) %all-to-all-start) | async-done | bytes 1179680 | tf_op jit(solution)/shard_map/all_to_all | solution.py:285
  47.3 3.0 %pick_second.1 = (bf16[64,4,8,128]{3,2,1,0:T(8,128)(2,1)}, s32[64,128]{1,0:T(8,128)S(1)}) custom-call(bf16[64,9,8,128]{3,2,1,0:T(8,128)(2,1)S(1)} %all-to-all-done.x_ref), custom_call_target="tpu_custom_call" | custom-call | tf_op jit(solution)/shard_map/pick_second/pallas_call | solution.py:112
  50.2 6.2 %all-to-all-start.1 = ((bf16[64,4,8,128]{3,2,1,0:T(8,128)(2,1)}), bf16[64,4,8,128]{3,2,1,0:T(8,128)(2,1)S(1)}, u32[]{:S(2)}, u32[]{:S(2)}) async-start(bf16[64,4,8,128]{3,2,1,0:T(8,128)(2,1)} %get-tuple-element.12), calls=%async_computation.1 | async-start | bytes 1048576 | tf_op jit(solution)/shard_map/all_to_all | solution.py:285
  56.4 1.4 %pick_first.1 = bf16[64,4,8,128]{3,2,1,0:T(8,128)(2,1)S(1)} custom-call(s32[64,128]{1,0:T(8,128)S(1)} %get-tuple-element.13.place_ref, bf16[64,9,8,128]{3,2,1,0:T(8,128)(2,1)S(1)} %all-to-all-done.x_ref), custom_call_target="tpu_custom_call" | custom-call | tf_op jit(solution)/shard_map/pick_first/pallas_call | solution.py:132
  57.9 3.2 %collective-permute-start = (bf16[64,4,8,128]{3,2,1,0:T(8,128)(2,1)S(1)}, bf16[64,4,8,128]{3,2,1,0:T(8,128)(2,1)}, u32[]{:S(2)}, u32[]{:S(2)}) collective-permute-start(bf16[64,4,8,128]{3,2,1,0:T(8,128)(2,1)S(1)} %pick_first.1), channel_id=1, source_target_pairs={{0,0},{1,65},{2,130},{3,195},{4,4},{5,69},{6,134},{7,199},{8,8},{9... | collective-permute-start | bytes 1572872 | tf_op jit(solution)/shard_map/ppermute | solution.py:299
  61.1 8.3 %collective-permute-done = bf16[64,4,8,128]{3,2,1,0:T(8,128)(2,1)} collective-permute-done((bf16[64,4,8,128]{3,2,1,0:T(8,128)(2,1)S(1)}, bf16[64,4,8,128]{3,2,1,0:T(8,128)(2,1)}, u32[]{:S(2)}, u32[]{:S(2)}) %collective-permute-start) | collective-permute-done | bytes 524320 | tf_op jit(solution)/shard_map/ppermute | solution.py:299
  69.4 4.4 %all-to-all-done.1 = bf16[64,4,8,128]{3,2,1,0:T(8,128)(2,1)S(1)} async-done(((bf16[64,4,8,128]{3,2,1,0:T(8,128)(2,1)}), bf16[64,4,8,128]{3,2,1,0:T(8,128)(2,1)S(1)}, u32[]{:S(2)}, u32[]{:S(2)}) %all-to-all-start.1) | async-done | bytes 524320 | tf_op jit(solution)/shard_map/all_to_all | solution.py:285
  73.8 1.3 %collective-permute-start.1 = (bf16[64,4,8,128]{3,2,1,0:T(8,128)(2,1)S(1)}, bf16[64,4,8,128]{3,2,1,0:T(8,128)(2,1)S(1)}, u32[]{:S(2)}, u32[]{:S(2)}) collective-permute-start(bf16[64,4,8,128]{3,2,1,0:T(8,128)(2,1)S(1)} %all-to-all-done.1), channel_id=1, source_target_pairs={{0,64},{64,128},{128,192},{192,0},{1,65},{65,129},{129,193},{193,1... | collective-permute-start | bytes 1572872 | tf_op jit(solution)/shard_map/ppermute | solution.py:305
  75.1 2.6 %collective-permute-start.2 = (bf16[64,4,8,128]{3,2,1,0:T(8,128)(2,1)S(1)}, bf16[64,4,8,128]{3,2,1,0:T(8,128)(2,1)S(1)}, u32[]{:S(2)}, u32[]{:S(2)}) collective-permute-start(bf16[64,4,8,128]{3,2,1,0:T(8,128)(2,1)S(1)} %all-to-all-done.1), channel_id=1, source_target_pairs={{0,128},{64,192},{128,0},{192,64},{1,129},{65,193},{129,1},{193,65... | collective-permute-start | bytes 1572872 | tf_op jit(solution)/shard_map/ppermute | solution.py:305
  77.7 1.1 collective-permute-start.3
  78.8 9.8 %all-to-all-start.2 = ((bf16[64,4,8,128]{3,2,1,0:T(8,128)(2,1)}), bf16[64,4,8,128]{3,2,1,0:T(8,128)(2,1)S(1)}, u32[]{:S(2)}, u32[]{:S(2)}) async-start(bf16[64,4,8,128]{3,2,1,0:T(8,128)(2,1)} %collective-permute-done), calls=%async_computation.2 | async-start | bytes 1048576 | tf_op jit(solution)/shard_map/all_to_all | solution.py:285
  88.6 0.0 collective-permute-done.1.refs_0_
  88.6 12.1 %collective-permute-done.2.refs_1_ = bf16[64,4,8,128]{3,2,1,0:T(8,128)(2,1)S(1)} collective-permute-done((bf16[64,4,8,128]{3,2,1,0:T(8,128)(2,1)S(1)}, bf16[64,4,8,128]{3,2,1,0:T(8,128)(2,1)S(1)}, u32[]{:S(2)}, u32[]{:S(2)}) %collective-permute-start.2) | collective-permute-done | bytes 524320 | tf_op jit(solution)/shard_map/ppermute | solution.py:305
  100.7 0.0 collective-permute-done.3.refs_2_
  100.7 0.5 settle.1.win_ref
  101.2 4.7 %all-to-all-done.2 = bf16[64,4,8,128]{3,2,1,0:T(8,128)(2,1)S(1)} async-done(((bf16[64,4,8,128]{3,2,1,0:T(8,128)(2,1)}), bf16[64,4,8,128]{3,2,1,0:T(8,128)(2,1)S(1)}, u32[]{:S(2)}, u32[]{:S(2)}) %all-to-all-start.2) | async-done | bytes 524320 | tf_op jit(solution)/shard_map/all_to_all | solution.py:285
  105.9 11.1 %correlate.1 = bf16[8,4,32,1024]{3,2,1,0:T(8,128)(2,1)} custom-call(s32[1]{0:T(128)} %settle.1.win_ref, bf16[2,8,4,4,8,128]{5,4,3,2,1,0:T(8,128)(2,1)S(1)} %bitcast.12, bf16[2,8,4,4,8,128]{5,4,3,2,1,0:T(8,128)(2,1)S(1)} %bitcast.11, bf16[2,8,4,4,8,128]{5,4,3,2,1,0:T(8,128)(2,1)S(1)} %bitcast.13, bf16[2,8,4,4,8,128]{5,4,3,2,1,0:T(8,128)(2,1)S(1)} %bitcast.14, ...), custom_call_target="tpu_custom_call" | custom-call | tf_op jit(solution)/shard_map/correlate/pallas_call | solution.py:235
  (1 shorter events, 0.0 us)
Async XLA Ops:
  2.9 44.4 %all-to-all-start = ((bf16[64,9,8,128]{3,2,1,0:T(8,128)(2,1)}), bf16[64,9,8,128]{3,2,1,0:T(8,128)(2,1)S(1)}, u32[]{:S(2)}, u32[]{:S(2)}) async-start(bf16[64,9,8,128]{3,2,1,0:T(8,128)(2,1)} %bitcast.16), calls=%async_computation | async-start | bytes 2359296 | tf_op jit(solution)/shard_map/all_to_all | solution.py:285
  50.2 23.5 %all-to-all-start.1 = ((bf16[64,4,8,128]{3,2,1,0:T(8,128)(2,1)}), bf16[64,4,8,128]{3,2,1,0:T(8,128)(2,1)S(1)}, u32[]{:S(2)}, u32[]{:S(2)}) async-start(bf16[64,4,8,128]{3,2,1,0:T(8,128)(2,1)} %get-tuple-element.12), calls=%async_computation.1 | async-start | bytes 1048576 | tf_op jit(solution)/shard_map/all_to_all | solution.py:285
  57.9 11.5 %collective-permute-start = (bf16[64,4,8,128]{3,2,1,0:T(8,128)(2,1)S(1)}, bf16[64,4,8,128]{3,2,1,0:T(8,128)(2,1)}, u32[]{:S(2)}, u32[]{:S(2)}) collective-permute-start(bf16[64,4,8,128]{3,2,1,0:T(8,128)(2,1)S(1)} %pick_first.1), channel_id=1, source_target_pairs={{0,0},{1,65},{2,130},{3,195},{4,4},{5,69},{6,134},{7,199},{8,8},{9... | collective-permute-start | bytes 1572872 | tf_op jit(solution)/shard_map/ppermute | solution.py:299
  73.8 14.8 %collective-permute-start.1 = (bf16[64,4,8,128]{3,2,1,0:T(8,128)(2,1)S(1)}, bf16[64,4,8,128]{3,2,1,0:T(8,128)(2,1)S(1)}, u32[]{:S(2)}, u32[]{:S(2)}) collective-permute-start(bf16[64,4,8,128]{3,2,1,0:T(8,128)(2,1)S(1)} %all-to-all-done.1), channel_id=1, source_target_pairs={{0,64},{64,128},{128,192},{192,0},{1,65},{65,129},{129,193},{193,1... | collective-permute-start | bytes 1572872 | tf_op jit(solution)/shard_map/ppermute | solution.py:305
  75.1 25.6 %collective-permute-start.2 = (bf16[64,4,8,128]{3,2,1,0:T(8,128)(2,1)S(1)}, bf16[64,4,8,128]{3,2,1,0:T(8,128)(2,1)S(1)}, u32[]{:S(2)}, u32[]{:S(2)}) collective-permute-start(bf16[64,4,8,128]{3,2,1,0:T(8,128)(2,1)S(1)} %all-to-all-done.1), channel_id=1, source_target_pairs={{0,128},{64,192},{128,0},{192,64},{1,129},{65,193},{129,1},{193,65... | collective-permute-start | bytes 1572872 | tf_op jit(solution)/shard_map/ppermute | solution.py:305
  77.7 23.0 %collective-permute-start.3 = (bf16[64,4,8,128]{3,2,1,0:T(8,128)(2,1)S(1)}, bf16[64,4,8,128]{3,2,1,0:T(8,128)(2,1)S(1)}, u32[]{:S(2)}, u32[]{:S(2)}) collective-permute-start(bf16[64,4,8,128]{3,2,1,0:T(8,128)(2,1)S(1)} %all-to-all-done.1), channel_id=1, source_target_pairs={{0,192},{64,0},{128,64},{192,128},{1,193},{65,1},{129,65},{193,129... | collective-permute-start | bytes 1572872 | tf_op jit(solution)/shard_map/ppermute | solution.py:305
  78.8 27.1 %all-to-all-start.2 = ((bf16[64,4,8,128]{3,2,1,0:T(8,128)(2,1)}), bf16[64,4,8,128]{3,2,1,0:T(8,128)(2,1)S(1)}, u32[]{:S(2)}, u32[]{:S(2)}) async-start(bf16[64,4,8,128]{3,2,1,0:T(8,128)(2,1)} %collective-permute-done), calls=%async_computation.2 | async-start | bytes 1048576 | tf_op jit(solution)/shard_map/all_to_all | solution.py:285

commit v6 on v5

--- a/solution.py
+++ b/solution.py
@@ -15,7 +15,7 @@
 LANES = 128
 GROUP = 8
 HALF = 64
-SETTLE_FLOPS = 15 * 10**9
+SETTLE_FLOPS = 8 * 10**9
 
 
 def whiten_kernel(win_ref, x_ref, sent_ref, slots_ref, out_ref, table_ref):
@@ -303,7 +303,7 @@
     for distance in range(1, windows):
         step = [(w, (w + distance) % windows) for w in range(windows)]
         b.append(lax.ppermute(second, "win", step))
-    win = settle(win, b[1:])
+    win = settle(win, b[windows // 2 : windows // 2 + 1])
     a = exchange(first).reshape(pieces)
     return correlate(win, a, [x.reshape(pieces) for x in b], table)
 

time: 118 us -> 114 us (0.966)
  waiting for transfers between devices: 41 us -> 36.7 us
    all_to_all x3, waiting for transfers between devices: 20.6 us -> 17.3 us  [local(): lax.all_to_all(x, 'pair', split_axis=0, concat_axis=0, tiled=True)]
    ppermute x3, starting transfers between devices: 4.99 us -> 7.26 us  [local(): b.append(lax.ppermute(second, 'win', step))]
    all_to_all x3, starting transfers between devices: 29 us -> 26.8 us  [local(): lax.all_to_all(x, 'pair', split_axis=0, concat_axis=0, tiled=True)]
  transfers between devices with their start and end apart: 7 -> 7, of which waited for: 5 -> 5; matrix products, arithmetic and copies ran while one was open for 17% -> 18% of each run, Pallas kernels for 2% -> 2%
where the time goes in v6:
time: 114 us; the launch traced here: 113 us
  starting transfers between devices  37.2 us (33%)
  waiting for transfers between devices  36.7 us (32%)
  other arithmetic  19.8 us (17%)
  Pallas kernels  18.9 us (17%)
    all_to_all x3, starting transfers between devices, local(): lax.all_to_all(x, 'pair', split_axis=0, concat_axis=0, tiled=True)  26.8 us
    another operation x1, other arithmetic  17.4 us
    all_to_all x3, waiting for transfers between devices, local(): lax.all_to_all(x, 'pair', split_axis=0, concat_axis=0, tiled=True)  17.3 us
    ppermute x3, waiting for transfers between devices, local(): b.append(lax.ppermute(second, 'win', step))  11.1 us
    pallas_call x1, Pallas kernels, correlate(): pl.pallas_call(functools.partial(correlate_kernel, scaling), grid=(tiles...  11 us
    ppermute x1, waiting for transfers between devices, local(): first = lax.ppermute(first, ('win', 'pair'), turn)  8.29 us
    ppermute x3, starting transfers between devices, local(): b.append(lax.ppermute(second, 'win', step))  7.26 us
    ppermute x1, starting transfers between devices, local(): first = lax.ppermute(first, ('win', 'pair'), turn)  3.21 us
  transfers between devices with their start and end apart: 7, of which 5 were waited for; matrix products, arithmetic and copies ran while one was open for 18% of the time, Pallas kernels for 2%

profile of v6, /device:TPU:1, one launch (start us, length us, event | category | flops | bytes accessed | tf_op | source)
XLA Modules:
  0.0 112.8 jit_solution(8281487078248034084)
XLA Ops:
  0.0 2.9 %whiten_spread.1 = bf16[2,8,4,9,8,128]{5,4,3,2,1,0:T(8,128)(2,1)} custom-call(s32[1]{0:T(128)} %bitcast.win_ref, bf16[8,1,2,32,1024]{4,3,2,1,0:T(8,128)(2,1)} %x_ref.1, s32[2,64]{1,0:T(2,128)} %bitcast.17, s32[2,4]{1,0:T(2,128)} %bitcast.18), custom_call_target="tpu_custom_call" | custom-call | tf_op jit(solution)/shard_map/whiten_spread/pallas_call | solution.py:59
  2.9 13.0 %all-to-all-start = ((bf16[64,9,8,128]{3,2,1,0:T(8,128)(2,1)}), bf16[64,9,8,128]{3,2,1,0:T(8,128)(2,1)S(1)}, u32[]{:S(2)}, u32[]{:S(2)}) async-start(bf16[64,9,8,128]{3,2,1,0:T(8,128)(2,1)} %bitcast.16), calls=%async_computation | async-start | bytes 2359296 | tf_op jit(solution)/shard_map/all_to_all | solution.py:285
  15.9 17.4 %cosine_convert_fusion = (bf16[1024,1024]{1,0:T(8,128)(2,1)S(1)}, bf16[1024,1024]{1,0:T(8,128)(2,1)S(1)}) fusion(s32[1024]{0:T(1024)S(1)} %get-tuple-element.19, s32[1024]{0:T(1024)S(1)} %get-tuple-element.20), kind=kLoop, calls=%fused_computation.10 | loop fusion | flops 17825792 | bytes 4202496 | tf_op jit(solution)/shard_map/convert
  33.4 2.4 %pad_maximum_fusion.refs_4_ = bf16[2048,1024]{1,0:T(8,128)(2,1)} fusion(bf16[1024,1024]{1,0:T(8,128)(2,1)S(1)} %get-tuple-element.18, bf16[1024,1024]{1,0:T(8,128)(2,1)S(1)} %get-tuple-element.17), kind=kLoop, calls=%fused_computation.8 | loop fusion | flops 8388608 | bytes 8388608 | tf_op jit(solution)/shard_map/concatenate | solution.py:277
  35.7 11.5 %all-to-all-done.x_ref = bf16[64,9,8,128]{3,2,1,0:T(8,128)(2,1)S(1)} async-done(((bf16[64,9,8,128]{3,2,1,0:T(8,128)(2,1)}), bf16[64,9,8,128]{3,2,1,0:T(8,128)(2,1)S(1)}, u32[]{:S(2)}, u32[]{:S(2)}) %all-to-all-start) | async-done | bytes 1179680 | tf_op jit(solution)/shard_map/all_to_all | solution.py:285
  47.3 3.0 %pick_second.1 = (bf16[64,4,8,128]{3,2,1,0:T(8,128)(2,1)}, s32[64,128]{1,0:T(8,128)S(1)}) custom-call(bf16[64,9,8,128]{3,2,1,0:T(8,128)(2,1)S(1)} %all-to-all-done.x_ref), custom_call_target="tpu_custom_call" | custom-call | tf_op jit(solution)/shard_map/pick_second/pallas_call | solution.py:112
  50.2 6.2 %all-to-all-start.1 = ((bf16[64,4,8,128]{3,2,1,0:T(8,128)(2,1)}), bf16[64,4,8,128]{3,2,1,0:T(8,128)(2,1)S(1)}, u32[]{:S(2)}, u32[]{:S(2)}) async-start(bf16[64,4,8,128]{3,2,1,0:T(8,128)(2,1)} %get-tuple-element.12), calls=%async_computation.1 | async-start | bytes 1048576 | tf_op jit(solution)/shard_map/all_to_all | solution.py:285
  56.4 1.4 %pick_first.1 = bf16[64,4,8,128]{3,2,1,0:T(8,128)(2,1)S(1)} custom-call(s32[64,128]{1,0:T(8,128)S(1)} %get-tuple-element.13.place_ref, bf16[64,9,8,128]{3,2,1,0:T(8,128)(2,1)S(1)} %all-to-all-done.x_ref), custom_call_target="tpu_custom_call" | custom-call | tf_op jit(solution)/shard_map/pick_first/pallas_call | solution.py:132
  57.9 3.2 %collective-permute-start = (bf16[64,4,8,128]{3,2,1,0:T(8,128)(2,1)S(1)}, bf16[64,4,8,128]{3,2,1,0:T(8,128)(2,1)}, u32[]{:S(2)}, u32[]{:S(2)}) collective-permute-start(bf16[64,4,8,128]{3,2,1,0:T(8,128)(2,1)S(1)} %pick_first.1), channel_id=1, source_target_pairs={{0,0},{1,65},{2,130},{3,195},{4,4},{5,69},{6,134},{7,199},{8,8},{9... | collective-permute-start | bytes 1572872 | tf_op jit(solution)/shard_map/ppermute | solution.py:299
  61.1 8.3 %collective-permute-done = bf16[64,4,8,128]{3,2,1,0:T(8,128)(2,1)} collective-permute-done((bf16[64,4,8,128]{3,2,1,0:T(8,128)(2,1)S(1)}, bf16[64,4,8,128]{3,2,1,0:T(8,128)(2,1)}, u32[]{:S(2)}, u32[]{:S(2)}) %collective-permute-start) | collective-permute-done | bytes 524320 | tf_op jit(solution)/shard_map/ppermute | solution.py:299
  69.4 4.4 %all-to-all-done.1 = bf16[64,4,8,128]{3,2,1,0:T(8,128)(2,1)S(1)} async-done(((bf16[64,4,8,128]{3,2,1,0:T(8,128)(2,1)}), bf16[64,4,8,128]{3,2,1,0:T(8,128)(2,1)S(1)}, u32[]{:S(2)}, u32[]{:S(2)}) %all-to-all-start.1) | async-done | bytes 524320 | tf_op jit(solution)/shard_map/all_to_all | solution.py:285
  73.8 2.9 %collective-permute-start.1 = (bf16[64,4,8,128]{3,2,1,0:T(8,128)(2,1)S(1)}, bf16[64,4,8,128]{3,2,1,0:T(8,128)(2,1)S(1)}, u32[]{:S(2)}, u32[]{:S(2)}) collective-permute-start(bf16[64,4,8,128]{3,2,1,0:T(8,128)(2,1)S(1)} %all-to-all-done.1), channel_id=1, source_target_pairs={{0,128},{64,192},{128,0},{192,64},{1,129},{65,193},{129,1},{193,65... | collective-permute-start | bytes 1572872 | tf_op jit(solution)/shard_map/ppermute | solution.py:305
  76.7 7.6 %all-to-all-start.2 = ((bf16[64,4,8,128]{3,2,1,0:T(8,128)(2,1)}), bf16[64,4,8,128]{3,2,1,0:T(8,128)(2,1)S(1)}, u32[]{:S(2)}, u32[]{:S(2)}) async-start(bf16[64,4,8,128]{3,2,1,0:T(8,128)(2,1)} %collective-permute-done), calls=%async_computation.2 | async-start | bytes 1048576 | tf_op jit(solution)/shard_map/all_to_all | solution.py:285
  84.3 3.0 %collective-permute-start.2 = (bf16[64,4,8,128]{3,2,1,0:T(8,128)(2,1)S(1)}, bf16[64,4,8,128]{3,2,1,0:T(8,128)(2,1)S(1)}, u32[]{:S(2)}, u32[]{:S(2)}) collective-permute-start(bf16[64,4,8,128]{3,2,1,0:T(8,128)(2,1)S(1)} %all-to-all-done.1), channel_id=1, source_target_pairs={{0,64},{64,128},{128,192},{192,0},{1,65},{65,129},{129,193},{193,1... | collective-permute-start | bytes 1572872 | tf_op jit(solution)/shard_map/ppermute | solution.py:305
  87.3 1.3 %collective-permute-start.3 = (bf16[64,4,8,128]{3,2,1,0:T(8,128)(2,1)S(1)}, bf16[64,4,8,128]{3,2,1,0:T(8,128)(2,1)S(1)}, u32[]{:S(2)}, u32[]{:S(2)}) collective-permute-start(bf16[64,4,8,128]{3,2,1,0:T(8,128)(2,1)S(1)} %all-to-all-done.1), channel_id=1, source_target_pairs={{0,192},{64,0},{128,64},{192,128},{1,193},{65,1},{129,65},{193,129... | collective-permute-start | bytes 1572872 | tf_op jit(solution)/shard_map/ppermute | solution.py:305
  88.6 0.0 collective-permute-done.1.refs_0_
  88.6 0.5 settle.1.win_ref
  89.2 11.1 %collective-permute-done.2 = bf16[64,4,8,128]{3,2,1,0:T(8,128)(2,1)S(1)} collective-permute-done((bf16[64,4,8,128]{3,2,1,0:T(8,128)(2,1)S(1)}, bf16[64,4,8,128]{3,2,1,0:T(8,128)(2,1)S(1)}, u32[]{:S(2)}, u32[]{:S(2)}) %collective-permute-start.2) | collective-permute-done | bytes 524320 | tf_op jit(solution)/shard_map/ppermute | solution.py:305
  100.3 0.0 collective-permute-done.3
  100.3 1.3 %all-to-all-done.2 = bf16[64,4,8,128]{3,2,1,0:T(8,128)(2,1)S(1)} async-done(((bf16[64,4,8,128]{3,2,1,0:T(8,128)(2,1)}), bf16[64,4,8,128]{3,2,1,0:T(8,128)(2,1)S(1)}, u32[]{:S(2)}, u32[]{:S(2)}) %all-to-all-start.2) | async-done | bytes 524320 | tf_op jit(solution)/shard_map/all_to_all | solution.py:285
  101.6 11.0 %correlate.1 = bf16[8,4,32,1024]{3,2,1,0:T(8,128)(2,1)} custom-call(s32[1]{0:T(128)} %settle.1.win_ref, bf16[2,8,4,4,8,128]{5,4,3,2,1,0:T(8,128)(2,1)S(1)} %bitcast.12, bf16[2,8,4,4,8,128]{5,4,3,2,1,0:T(8,128)(2,1)S(1)} %bitcast.11, bf16[2,8,4,4,8,128]{5,4,3,2,1,0:T(8,128)(2,1)S(1)} %bitcast.14, bf16[2,8,4,4,8,128]{5,4,3,2,1,0:T(8,128)(2,1)S(1)} %bitcast.13, ...), custom_call_target="tpu_custom_call" | custom-call | tf_op jit(solution)/shard_map/correlate/pallas_call | solution.py:235
  (1 shorter events, 0.0 us)
Async XLA Ops:
  2.9 44.4 %all-to-all-start = ((bf16[64,9,8,128]{3,2,1,0:T(8,128)(2,1)}), bf16[64,9,8,128]{3,2,1,0:T(8,128)(2,1)S(1)}, u32[]{:S(2)}, u32[]{:S(2)}) async-start(bf16[64,9,8,128]{3,2,1,0:T(8,128)(2,1)} %bitcast.16), calls=%async_computation | async-start | bytes 2359296 | tf_op jit(solution)/shard_map/all_to_all | solution.py:285
  50.2 23.5 %all-to-all-start.1 = ((bf16[64,4,8,128]{3,2,1,0:T(8,128)(2,1)}), bf16[64,4,8,128]{3,2,1,0:T(8,128)(2,1)S(1)}, u32[]{:S(2)}, u32[]{:S(2)}) async-start(bf16[64,4,8,128]{3,2,1,0:T(8,128)(2,1)} %get-tuple-element.12), calls=%async_computation.1 | async-start | bytes 1048576 | tf_op jit(solution)/shard_map/all_to_all | solution.py:285
  57.9 11.5 %collective-permute-start = (bf16[64,4,8,128]{3,2,1,0:T(8,128)(2,1)S(1)}, bf16[64,4,8,128]{3,2,1,0:T(8,128)(2,1)}, u32[]{:S(2)}, u32[]{:S(2)}) collective-permute-start(bf16[64,4,8,128]{3,2,1,0:T(8,128)(2,1)S(1)} %pick_first.1), channel_id=1, source_target_pairs={{0,0},{1,65},{2,130},{3,195},{4,4},{5,69},{6,134},{7,199},{8,8},{9... | collective-permute-start | bytes 1572872 | tf_op jit(solution)/shard_map/ppermute | solution.py:299
  73.8 14.9 %collective-permute-start.1 = (bf16[64,4,8,128]{3,2,1,0:T(8,128)(2,1)S(1)}, bf16[64,4,8,128]{3,2,1,0:T(8,128)(2,1)S(1)}, u32[]{:S(2)}, u32[]{:S(2)}) collective-permute-start(bf16[64,4,8,128]{3,2,1,0:T(8,128)(2,1)S(1)} %all-to-all-done.1), channel_id=1, source_target_pairs={{0,128},{64,192},{128,0},{192,64},{1,129},{65,193},{129,1},{193,65... | collective-permute-start | bytes 1572872 | tf_op jit(solution)/shard_map/ppermute | solution.py:305
  76.7 24.9 %all-to-all-start.2 = ((bf16[64,4,8,128]{3,2,1,0:T(8,128)(2,1)}), bf16[64,4,8,128]{3,2,1,0:T(8,128)(2,1)S(1)}, u32[]{:S(2)}, u32[]{:S(2)}) async-start(bf16[64,4,8,128]{3,2,1,0:T(8,128)(2,1)} %collective-permute-done), calls=%async_computation.2 | async-start | bytes 1048576 | tf_op jit(solution)/shard_map/all_to_all | solution.py:285
  84.3 16.0 %collective-permute-start.2 = (bf16[64,4,8,128]{3,2,1,0:T(8,128)(2,1)S(1)}, bf16[64,4,8,128]{3,2,1,0:T(8,128)(2,1)S(1)}, u32[]{:S(2)}, u32[]{:S(2)}) collective-permute-start(bf16[64,4,8,128]{3,2,1,0:T(8,128)(2,1)S(1)} %all-to-all-done.1), channel_id=1, source_target_pairs={{0,64},{64,128},{128,192},{192,0},{1,65},{65,129},{129,193},{193,1... | collective-permute-start | bytes 1572872 | tf_op jit(solution)/shard_map/ppermute | solution.py:305
  87.3 12.9 %collective-permute-start.3 = (bf16[64,4,8,128]{3,2,1,0:T(8,128)(2,1)S(1)}, bf16[64,4,8,128]{3,2,1,0:T(8,128)(2,1)S(1)}, u32[]{:S(2)}, u32[]{:S(2)}) collective-permute-start(bf16[64,4,8,128]{3,2,1,0:T(8,128)(2,1)S(1)} %all-to-all-done.1), channel_id=1, source_target_pairs={{0,192},{64,0},{128,64},{192,128},{1,193},{65,1},{129,65},{193,129... | collective-permute-start | bytes 1572872 | tf_op jit(solution)/shard_map/ppermute | solution.py:305

commit v7 on v6

--- a/solution.py
+++ b/solution.py
@@ -299,11 +299,14 @@
     first = lax.ppermute(first, ("win", "pair"), turn)
     second = exchange(second)
     second, first = lax.optimization_barrier((second, first))
-    b = [second]
-    for distance in range(1, windows):
-        step = [(w, (w + distance) % windows) for w in range(windows)]
-        b.append(lax.ppermute(second, "win", step))
-    win = settle(win, b[windows // 2 : windows // 2 + 1])
+    b = [second] * windows
+    ahead = [(w, (w + 1) % windows) for w in range(windows)]
+    behind = [(w, (w - 1) % windows) for w in range(windows)]
+    for distance in range(1, windows // 2 + 1):
+        b[distance] = lax.ppermute(b[distance - 1], "win", ahead)
+    for distance in range(windows - 1, windows // 2, -1):
+        b[distance] = lax.ppermute(b[(distance + 1) % windows], "win", behind)
+    win = settle(win, b[1:2])
     a = exchange(first).reshape(pieces)
     return correlate(win, a, [x.reshape(pieces) for x in b], table)
 

time: 114 us -> 115 us (level)
  waiting for transfers between devices: 36.7 us -> 40.1 us
  starting transfers between devices: 37.2 us -> 35.4 us
    ppermute x3, starting transfers between devices: 7.26 us -> 2.16 us  [the longest x2 1.3 us: local(): b[distance] = lax.ppermute(b[distance - 1], 'win', ahead)]
    all_to_all x3, starting transfers between devices: 26.8 us -> 30 us  [local(): lax.all_to_all(x, 'pair', split_axis=0, concat_axis=0, tiled=True)]
    all_to_all x3, waiting for transfers between devices: 17.3 us -> 20.1 us  [local(): lax.all_to_all(x, 'pair', split_axis=0, concat_axis=0, tiled=True)]
  transfers between devices with their start and end apart: 7 -> 7, of which waited for: 5 -> 6; matrix products, arithmetic and copies ran while one was open for 18% -> 17% of each run, Pallas kernels for 2% -> 2%
where the time goes in v7:
time: 115 us; the launch traced here: 114 us
  waiting for transfers between devices  40.1 us (35%)
  starting transfers between devices  35.4 us (31%)
  other arithmetic  19.8 us (17%)
  Pallas kernels  18.9 us (16%)
    all_to_all x3, starting transfers between devices, local(): lax.all_to_all(x, 'pair', split_axis=0, concat_axis=0, tiled=True)  30 us
    all_to_all x3, waiting for transfers between devices, local(): lax.all_to_all(x, 'pair', split_axis=0, concat_axis=0, tiled=True)  20.1 us
    another operation x1, other arithmetic  17.4 us
    pallas_call x1, Pallas kernels, correlate(): pl.pallas_call(functools.partial(correlate_kernel, scaling), grid=(tiles...  11.1 us
    ppermute x1, waiting for transfers between devices, local(): b[distance] = lax.ppermute(b[(distance + 1) % windows], 'win', behind)  10.2 us
    ppermute x1, waiting for transfers between devices, local(): first = lax.ppermute(first, ('win', 'pair'), turn)  8.29 us
    ppermute x1, starting transfers between devices, local(): first = lax.ppermute(first, ('win', 'pair'), turn)  3.21 us
    pallas_call x1, Pallas kernels, pick_second(): pl.pallas_call(pick_second_kernel, in_specs=[pl.BlockSpec(memory_space=pl...  2.96 us
  transfers between devices with their start and end apart: 7, of which 6 were waited for; matrix products, arithmetic and copies ran while one was open for 17% of the time, Pallas kernels for 2%

profile of v7, /device:TPU:1, one launch (start us, length us, event | category | flops | bytes accessed | tf_op | source)
XLA Modules:
  0.0 114.5 jit_solution(11861686088878061124)
XLA Ops:
  0.0 2.9 %whiten_spread.1 = bf16[2,8,4,9,8,128]{5,4,3,2,1,0:T(8,128)(2,1)} custom-call(s32[1]{0:T(128)} %bitcast.win_ref, bf16[8,1,2,32,1024]{4,3,2,1,0:T(8,128)(2,1)} %x_ref.1, s32[2,64]{1,0:T(2,128)} %bitcast.17, s32[2,4]{1,0:T(2,128)} %bitcast.18), custom_call_target="tpu_custom_call" | custom-call | tf_op jit(solution)/shard_map/whiten_spread/pallas_call | solution.py:59
  2.9 13.0 %all-to-all-start = ((bf16[64,9,8,128]{3,2,1,0:T(8,128)(2,1)}), bf16[64,9,8,128]{3,2,1,0:T(8,128)(2,1)S(1)}, u32[]{:S(2)}, u32[]{:S(2)}) async-start(bf16[64,9,8,128]{3,2,1,0:T(8,128)(2,1)} %bitcast.16), calls=%async_computation | async-start | bytes 2359296 | tf_op jit(solution)/shard_map/all_to_all | solution.py:285
  15.9 17.4 %cosine_convert_fusion = (bf16[1024,1024]{1,0:T(8,128)(2,1)S(1)}, bf16[1024,1024]{1,0:T(8,128)(2,1)S(1)}) fusion(s32[1024]{0:T(1024)S(1)} %get-tuple-element.19, s32[1024]{0:T(1024)S(1)} %get-tuple-element.20), kind=kLoop, calls=%fused_computation.10 | loop fusion | flops 17825792 | bytes 4202496 | tf_op jit(solution)/shard_map/convert
  33.4 2.4 %pad_maximum_fusion.refs_4_ = bf16[2048,1024]{1,0:T(8,128)(2,1)} fusion(bf16[1024,1024]{1,0:T(8,128)(2,1)S(1)} %get-tuple-element.18, bf16[1024,1024]{1,0:T(8,128)(2,1)S(1)} %get-tuple-element.17), kind=kLoop, calls=%fused_computation.8 | loop fusion | flops 8388608 | bytes 8388608 | tf_op jit(solution)/shard_map/concatenate | solution.py:277
  35.7 11.5 %all-to-all-done.x_ref = bf16[64,9,8,128]{3,2,1,0:T(8,128)(2,1)S(1)} async-done(((bf16[64,9,8,128]{3,2,1,0:T(8,128)(2,1)}), bf16[64,9,8,128]{3,2,1,0:T(8,128)(2,1)S(1)}, u32[]{:S(2)}, u32[]{:S(2)}) %all-to-all-start) | async-done | bytes 1179680 | tf_op jit(solution)/shard_map/all_to_all | solution.py:285
  47.3 3.0 %pick_second.1 = (bf16[64,4,8,128]{3,2,1,0:T(8,128)(2,1)}, s32[64,128]{1,0:T(8,128)S(1)}) custom-call(bf16[64,9,8,128]{3,2,1,0:T(8,128)(2,1)S(1)} %all-to-all-done.x_ref), custom_call_target="tpu_custom_call" | custom-call | tf_op jit(solution)/shard_map/pick_second/pallas_call | solution.py:112
  50.2 6.2 %all-to-all-start.1 = ((bf16[64,4,8,128]{3,2,1,0:T(8,128)(2,1)}), bf16[64,4,8,128]{3,2,1,0:T(8,128)(2,1)S(1)}, u32[]{:S(2)}, u32[]{:S(2)}) async-start(bf16[64,4,8,128]{3,2,1,0:T(8,128)(2,1)} %get-tuple-element.12), calls=%async_computation.1 | async-start | bytes 1048576 | tf_op jit(solution)/shard_map/all_to_all | solution.py:285
  56.4 1.4 %pick_first.1 = bf16[64,4,8,128]{3,2,1,0:T(8,128)(2,1)S(1)} custom-call(s32[64,128]{1,0:T(8,128)S(1)} %get-tuple-element.13.place_ref, bf16[64,9,8,128]{3,2,1,0:T(8,128)(2,1)S(1)} %all-to-all-done.x_ref), custom_call_target="tpu_custom_call" | custom-call | tf_op jit(solution)/shard_map/pick_first/pallas_call | solution.py:132
  57.9 3.2 %collective-permute-start = (bf16[64,4,8,128]{3,2,1,0:T(8,128)(2,1)S(1)}, bf16[64,4,8,128]{3,2,1,0:T(8,128)(2,1)}, u32[]{:S(2)}, u32[]{:S(2)}) collective-permute-start(bf16[64,4,8,128]{3,2,1,0:T(8,128)(2,1)S(1)} %pick_first.1), channel_id=1, source_target_pairs={{0,0},{1,65},{2,130},{3,195},{4,4},{5,69},{6,134},{7,199},{8,8},{9... | collective-permute-start | bytes 1572872 | tf_op jit(solution)/shard_map/ppermute | solution.py:299
  61.1 8.3 %collective-permute-done = bf16[64,4,8,128]{3,2,1,0:T(8,128)(2,1)} collective-permute-done((bf16[64,4,8,128]{3,2,1,0:T(8,128)(2,1)S(1)}, bf16[64,4,8,128]{3,2,1,0:T(8,128)(2,1)}, u32[]{:S(2)}, u32[]{:S(2)}) %collective-permute-start) | collective-permute-done | bytes 524320 | tf_op jit(solution)/shard_map/ppermute | solution.py:299
  69.4 4.4 %all-to-all-done.1 = bf16[64,4,8,128]{3,2,1,0:T(8,128)(2,1)S(1)} async-done(((bf16[64,4,8,128]{3,2,1,0:T(8,128)(2,1)}), bf16[64,4,8,128]{3,2,1,0:T(8,128)(2,1)S(1)}, u32[]{:S(2)}, u32[]{:S(2)}) %all-to-all-start.1) | async-done | bytes 524320 | tf_op jit(solution)/shard_map/all_to_all | solution.py:285
  73.8 1.3 %collective-permute-start.1 = (bf16[64,4,8,128]{3,2,1,0:T(8,128)(2,1)S(1)}, bf16[64,4,8,128]{3,2,1,0:T(8,128)(2,1)S(1)}, u32[]{:S(2)}, u32[]{:S(2)}) collective-permute-start(bf16[64,4,8,128]{3,2,1,0:T(8,128)(2,1)S(1)} %all-to-all-done.1), channel_id=1, source_target_pairs={{0,64},{64,128},{128,192},{192,0},{1,65},{65,129},{129,193},{193,1... | collective-permute-start | bytes 1572872 | tf_op jit(solution)/shard_map/ppermute | solution.py:306
  75.1 10.8 %all-to-all-start.2 = ((bf16[64,4,8,128]{3,2,1,0:T(8,128)(2,1)}), bf16[64,4,8,128]{3,2,1,0:T(8,128)(2,1)S(1)}, u32[]{:S(2)}, u32[]{:S(2)}) async-start(bf16[64,4,8,128]{3,2,1,0:T(8,128)(2,1)} %collective-permute-done), calls=%async_computation.2 | async-start | bytes 1048576 | tf_op jit(solution)/shard_map/all_to_all | solution.py:285
  85.9 0.9 collective-permute-start.3
  86.8 1.6 %collective-permute-done.1.refs_0_ = bf16[64,4,8,128]{3,2,1,0:T(8,128)(2,1)S(1)} collective-permute-done((bf16[64,4,8,128]{3,2,1,0:T(8,128)(2,1)S(1)}, bf16[64,4,8,128]{3,2,1,0:T(8,128)(2,1)S(1)}, u32[]{:S(2)}, u32[]{:S(2)}) %collective-permute-start.1) | collective-permute-done | bytes 524320 | tf_op jit(solution)/shard_map/ppermute | solution.py:306
  88.3 0.0 collective-permute-start.2
  88.3 0.5 settle.1.win_ref
  88.8 10.2 %collective-permute-done.3 = bf16[64,4,8,128]{3,2,1,0:T(8,128)(2,1)S(1)} collective-permute-done((bf16[64,4,8,128]{3,2,1,0:T(8,128)(2,1)S(1)}, bf16[64,4,8,128]{3,2,1,0:T(8,128)(2,1)S(1)}, u32[]{:S(2)}, u32[]{:S(2)}) %collective-permute-start.3) | collective-permute-done | bytes 524320 | tf_op jit(solution)/shard_map/ppermute | solution.py:308
  99.0 4.2 %all-to-all-done.2 = bf16[64,4,8,128]{3,2,1,0:T(8,128)(2,1)S(1)} async-done(((bf16[64,4,8,128]{3,2,1,0:T(8,128)(2,1)}), bf16[64,4,8,128]{3,2,1,0:T(8,128)(2,1)S(1)}, u32[]{:S(2)}, u32[]{:S(2)}) %all-to-all-start.2) | async-done | bytes 524320 | tf_op jit(solution)/shard_map/all_to_all | solution.py:285
  103.2 0.0 collective-permute-done.2
  103.2 11.1 %correlate.1 = bf16[8,4,32,1024]{3,2,1,0:T(8,128)(2,1)} custom-call(s32[1]{0:T(128)} %settle.1.win_ref, bf16[2,8,4,4,8,128]{5,4,3,2,1,0:T(8,128)(2,1)S(1)} %bitcast.12, bf16[2,8,4,4,8,128]{5,4,3,2,1,0:T(8,128)(2,1)S(1)} %bitcast.11, bf16[2,8,4,4,8,128]{5,4,3,2,1,0:T(8,128)(2,1)S(1)} %bitcast.13, bf16[2,8,4,4,8,128]{5,4,3,2,1,0:T(8,128)(2,1)S(1)} %bitcast.15, ...), custom_call_target="tpu_custom_call" | custom-call | tf_op jit(solution)/shard_map/correlate/pallas_call | solution.py:235
  (1 shorter events, 0.0 us)
Async XLA Ops:
  2.9 44.4 %all-to-all-start = ((bf16[64,9,8,128]{3,2,1,0:T(8,128)(2,1)}), bf16[64,9,8,128]{3,2,1,0:T(8,128)(2,1)S(1)}, u32[]{:S(2)}, u32[]{:S(2)}) async-start(bf16[64,9,8,128]{3,2,1,0:T(8,128)(2,1)} %bitcast.16), calls=%async_computation | async-start | bytes 2359296 | tf_op jit(solution)/shard_map/all_to_all | solution.py:285
  50.2 23.5 %all-to-all-start.1 = ((bf16[64,4,8,128]{3,2,1,0:T(8,128)(2,1)}), bf16[64,4,8,128]{3,2,1,0:T(8,128)(2,1)S(1)}, u32[]{:S(2)}, u32[]{:S(2)}) async-start(bf16[64,4,8,128]{3,2,1,0:T(8,128)(2,1)} %get-tuple-element.12), calls=%async_computation.1 | async-start | bytes 1048576 | tf_op jit(solution)/shard_map/all_to_all | solution.py:285
  57.9 11.5 %collective-permute-start = (bf16[64,4,8,128]{3,2,1,0:T(8,128)(2,1)S(1)}, bf16[64,4,8,128]{3,2,1,0:T(8,128)(2,1)}, u32[]{:S(2)}, u32[]{:S(2)}) collective-permute-start(bf16[64,4,8,128]{3,2,1,0:T(8,128)(2,1)S(1)} %pick_first.1), channel_id=1, source_target_pairs={{0,0},{1,65},{2,130},{3,195},{4,4},{5,69},{6,134},{7,199},{8,8},{9... | collective-permute-start | bytes 1572872 | tf_op jit(solution)/shard_map/ppermute | solution.py:299
  73.8 14.5 %collective-permute-start.1 = (bf16[64,4,8,128]{3,2,1,0:T(8,128)(2,1)S(1)}, bf16[64,4,8,128]{3,2,1,0:T(8,128)(2,1)S(1)}, u32[]{:S(2)}, u32[]{:S(2)}) collective-permute-start(bf16[64,4,8,128]{3,2,1,0:T(8,128)(2,1)S(1)} %all-to-all-done.1), channel_id=1, source_target_pairs={{0,64},{64,128},{128,192},{192,0},{1,65},{65,129},{129,193},{193,1... | collective-permute-start | bytes 1572872 | tf_op jit(solution)/shard_map/ppermute | solution.py:306
  75.1 28.1 %all-to-all-start.2 = ((bf16[64,4,8,128]{3,2,1,0:T(8,128)(2,1)}), bf16[64,4,8,128]{3,2,1,0:T(8,128)(2,1)S(1)}, u32[]{:S(2)}, u32[]{:S(2)}) async-start(bf16[64,4,8,128]{3,2,1,0:T(8,128)(2,1)} %collective-permute-done), calls=%async_computation.2 | async-start | bytes 1048576 | tf_op jit(solution)/shard_map/all_to_all | solution.py:285
  85.9 13.1 %collective-permute-start.3 = (bf16[64,4,8,128]{3,2,1,0:T(8,128)(2,1)S(1)}, bf16[64,4,8,128]{3,2,1,0:T(8,128)(2,1)S(1)}, u32[]{:S(2)}, u32[]{:S(2)}) collective-permute-start(bf16[64,4,8,128]{3,2,1,0:T(8,128)(2,1)S(1)} %all-to-all-done.1), channel_id=1, source_target_pairs={{0,192},{64,0},{128,64},{192,128},{1,193},{65,1},{129,65},{193,129... | collective-permute-start | bytes 1572872 | tf_op jit(solution)/shard_map/ppermute | solution.py:308
  88.3 14.9 %collective-permute-start.2 = (bf16[64,4,8,128]{3,2,1,0:T(8,128)(2,1)S(1)}, bf16[64,4,8,128]{3,2,1,0:T(8,128)(2,1)S(1)}, u32[]{:S(2)}, u32[]{:S(2)}) collective-permute-start(bf16[64,4,8,128]{3,2,1,0:T(8,128)(2,1)S(1)} %collective-permute-done.1.refs_0_), channel_id=1, source_target_pairs={{0,64},{64,128},{128,192},{192,0},{1,65},{65,129},{129,193},{193,1... | collective-permute-start | bytes 1572872 | tf_op jit(solution)/shard_map/ppermute | solution.py:306

commit v8 on v6

--- a/solution.py
+++ b/solution.py
@@ -18,7 +18,7 @@
 SETTLE_FLOPS = 8 * 10**9
 
 
-def whiten_kernel(win_ref, x_ref, sent_ref, slots_ref, out_ref, table_ref):
+def whiten_kernel(win_ref, x_ref, out_ref):
     blocks = x_ref.shape[0]
     _, lane_groups, groups = out_ref.shape[:3]
     step = pl.program_id(0)
@@ -41,36 +41,24 @@
             rows = rows.reshape(blocks, 2, GROUP, LANES)
             for half in range(2):
                 place = lax.rem(2 * step + half + groups - win_ref[0], groups)
-                out_ref[part, lane_group, place, :blocks] = rows[:, half].astype(jnp.bfloat16)
-
-    @pl.when(step == 0)
-    def _():
-        table_ref[...] = jnp.zeros_like(table_ref)
-        table_ref[0:2, : sent_ref.shape[1]] = sent_ref[...].astype(jnp.float32)
-        table_ref[2:4, : slots_ref.shape[1]] = slots_ref[...].astype(jnp.float32)
-        piece = table_ref[...].astype(jnp.bfloat16)
-        shape = out_ref.shape
-        out_ref[:, :, :, blocks] = jnp.broadcast_to(piece, shape[:3] + shape[4:])
-
-
-def whiten_spread(win, spectra, sent, slots):
+                out_ref[part, lane_group, place] = rows[:, half].astype(jnp.bfloat16)
+
+
+def whiten_spread(win, spectra):
     blocks, _, parts, channels, bins = spectra.shape
-    shape = (parts, bins // LANES, channels // GROUP, blocks + 1, GROUP, LANES)
+    shape = (parts, bins // LANES, channels // GROUP, blocks, GROUP, LANES)
     return pl.pallas_call(
         whiten_kernel,
         grid=(channels // 16,),
         in_specs=[
             pl.BlockSpec(memory_space=pltpu.SMEM),
             pl.BlockSpec((blocks, 1, parts, 16, bins), lambda g: (0, 0, 0, g, 0)),
-            pl.BlockSpec(sent.shape, lambda g: (0, 0)),
-            pl.BlockSpec(slots.shape, lambda g: (0, 0)),
         ],
         out_specs=pl.BlockSpec(shape, lambda g: (0,) * len(shape)),
         out_shape=jax.ShapeDtypeStruct(shape, jnp.bfloat16),
-        scratch_shapes=[pltpu.VMEM((GROUP, LANES), jnp.float32)],
         compiler_params=pltpu.CompilerParams(vmem_limit_bytes=60 * 2**20),
         name="whiten_spread",
-    )(win, spectra, sent, slots)
+    )(win, spectra)
 
 
 def copy_pieces(place_ref, x_ref, out_ref, start):
@@ -84,53 +72,46 @@
     lax.fori_loop(0, out_ref.shape[0], one_owner, 0, unroll=4)
 
 
-def pick_second_kernel(x_ref, out_ref, index_ref, table_ref, place_ref, sem):
-    owners, stride = x_ref.shape[:2]
-    tiles = out_ref.shape[1]
-    table_ref[...] = x_ref[:, stride - 1].astype(jnp.float32).reshape(table_ref.shape)
-    sent = [table_ref[pl.ds(k, owners, stride=GROUP), :] for k in range(2)]
+def places_kernel(tiles, stride, me_ref, near_ref, places_ref, table_ref):
+    owners = near_ref.shape[0]
+    for owner in range(owners):
+        table_ref[4 * owner : 4 * owner + 4, :] = near_ref[me_ref[0] ^ owner]
+    sent = [table_ref[pl.ds(k, owners, stride=4), :] for k in range(2)]
     lane = lax.broadcasted_iota(jnp.int32, (owners, LANES), 1)
     by_owner = jnp.concatenate(sent, axis=0).T[:owners].astype(jnp.int32)
     by_owner = by_owner + stride * (lane % HALF)
     places = jnp.zeros((owners, LANES), jnp.int32)
     for part in range(2):
-        slots = table_ref[pl.ds(2 + part, owners, stride=GROUP), :].astype(jnp.int32)
+        slots = table_ref[pl.ds(2 + part, owners, stride=4), :].astype(jnp.int32)
         for tile in range(tiles):
             slot = slots[:, tile : tile + 1]
             hit = lane == (slot % 2) * HALF + slot // 2
             place = jnp.sum(jnp.where(hit, by_owner, 0), axis=1, keepdims=True)
             places = jnp.where(lane == part * tiles + tile, place, places)
-    index_ref[...] = places
-    copy = pltpu.make_async_copy(index_ref, place_ref, sem)
-    copy.start()
-    copy.wait()
-    copy_pieces(place_ref, x_ref, out_ref, tiles)
-
-
-def pick_second(spread, tiles):
+    places_ref[...] = places
+
+
+def find_places(near, tiles, stride):
+    owners = near.shape[0]
+    me = lax.axis_index("pair").astype(jnp.int32).reshape(1)
+    return pl.pallas_call(
+        functools.partial(places_kernel, tiles, stride),
+        in_specs=[
+            pl.BlockSpec(memory_space=pltpu.SMEM),
+            pl.BlockSpec(memory_space=pltpu.VMEM),
+        ],
+        out_specs=pl.BlockSpec(memory_space=pltpu.VMEM),
+        out_shape=jax.ShapeDtypeStruct((owners, LANES), jnp.int32),
+        scratch_shapes=[pltpu.VMEM((owners * 4, LANES), jnp.float32)],
+        compiler_params=pltpu.CompilerParams(vmem_limit_bytes=8 * 2**20),
+        name="find_places",
+    )(me, near)
+
+
+def pick(index, spread, tiles, start):
     owners = spread.shape[0]
     return pl.pallas_call(
-        pick_second_kernel,
-        in_specs=[pl.BlockSpec(memory_space=pltpu.VMEM)],
-        out_specs=[pl.BlockSpec(memory_space=pltpu.VMEM)] * 2,
-        out_shape=[
-            jax.ShapeDtypeStruct((owners, tiles, GROUP, LANES), jnp.bfloat16),
-            jax.ShapeDtypeStruct((owners, LANES), jnp.int32),
-        ],
-        scratch_shapes=[
-            pltpu.VMEM((owners * GROUP, LANES), jnp.float32),
-            pltpu.SMEM((owners, LANES), jnp.int32),
-            pltpu.SemaphoreType.DMA,
-        ],
-        compiler_params=pltpu.CompilerParams(vmem_limit_bytes=24 * 2**20),
-        name="pick_second",
-    )(spread)
-
-
-def pick_first(index, spread, tiles):
-    owners = spread.shape[0]
-    return pl.pallas_call(
-        lambda place_ref, x_ref, out_ref: copy_pieces(place_ref, x_ref, out_ref, 0),
+        lambda place_ref, x_ref, out_ref: copy_pieces(place_ref, x_ref, out_ref, start),
         in_specs=[
             pl.BlockSpec(memory_space=pltpu.SMEM),
             pl.BlockSpec(memory_space=pltpu.VMEM),
@@ -138,8 +119,24 @@
         out_specs=pl.BlockSpec(memory_space=pltpu.VMEM),
         out_shape=jax.ShapeDtypeStruct((owners, tiles, GROUP, LANES), jnp.bfloat16),
         compiler_params=pltpu.CompilerParams(vmem_limit_bytes=24 * 2**20),
-        name="pick_first",
+        name="pick_second" if start else "pick_first",
     )(index, spread)
+
+
+def share_tables(send_blocks, tile_slots, strides):
+    owners = lax.axis_size("pair")
+    rows = [send_blocks[0].T, tile_slots.T]
+    rows = [jnp.pad(x.astype(jnp.float32), ((0, 0), (0, LANES - x.shape[1]))) for x in rows]
+    near = jnp.concatenate(rows, axis=0)[None]
+    step = 1
+    for size in strides:
+        parts = [near]
+        for k in range(1, size):
+            turn = [(j, j ^ (k * step)) for j in range(owners)]
+            parts.append(lax.ppermute(near, "pair", turn))
+        near = jnp.concatenate(parts, axis=0)
+        step *= size
+    return near
 
 
 def correlate_kernel(scaling, win_ref, a_ref, *refs):
@@ -270,11 +267,23 @@
 
 
 def lag_rows_table(bin_total):
-    bin_index = jnp.arange(bin_total, dtype=jnp.int32) + F0
+    fine = 16
     lag_index = jnp.arange(LAGS, dtype=jnp.int32) - LAGS // 2
-    wrapped = bin_index[:, None] * lag_index[None, :] % NS
-    phases = wrapped.astype(jnp.float32) * (2.0 * math.pi / NS)
-    return jnp.concatenate([jnp.cos(phases), -jnp.sin(phases)], axis=0).astype(jnp.bfloat16)
+
+    def turns(bins):
+        wrapped = bins[:, None] * lag_index[None, :] % NS
+        phases = wrapped.astype(jnp.float32) * (2.0 * math.pi / NS)
+        return jnp.cos(phases), jnp.sin(phases)
+
+    coarse_bins = jnp.arange(bin_total // fine, dtype=jnp.int32) * fine + F0
+    pairs = turns(jnp.concatenate([coarse_bins, jnp.arange(fine, dtype=jnp.int32)]))
+    cosine, sine = lax.optimization_barrier(pairs)
+    coarse = [x[:-fine, None, :] for x in (cosine, sine)]
+    small = [x[None, -fine:, :] for x in (cosine, sine)]
+    real = coarse[0] * small[0] - coarse[1] * small[1]
+    imag = coarse[1] * small[0] + coarse[0] * small[1]
+    table = jnp.stack([real, -imag]).astype(jnp.bfloat16)
+    return table.reshape(2 * bin_total, LAGS)
 
 
 def local(spectra, send_blocks, tile_slots):
@@ -286,11 +295,14 @@
     pieces = (parts, bins // LANES, groups, tiles, GROUP, LANES)
 
     win = lax.axis_index("win").astype(jnp.int32).reshape(1)
-    outgoing = whiten_spread(win, spectra, send_blocks[0].T, tile_slots.T)
-    spread = exchange(outgoing.reshape(owners, blocks + 1, GROUP, LANES))
-    spread, table = lax.optimization_barrier((spread, lag_rows_table(bins)))
-    second, index = pick_second(spread, tiles)
-    first = pick_first(index, spread, tiles)
+    outgoing = whiten_spread(win, spectra)
+    outgoing, *tables = lax.optimization_barrier((outgoing, send_blocks, tile_slots))
+    spread = exchange(outgoing.reshape(owners, blocks, GROUP, LANES))
+    near = share_tables(*tables, (2, 8, owners // 16))
+    index = find_places(near, tiles, blocks)
+    spread, index, table = lax.optimization_barrier((spread, index, lag_rows_table(bins)))
+    second = pick(index, spread, tiles, tiles)
+    first = pick(index, spread, tiles, 0)
     turn = [
         (w * owners + j, (w + j) % windows * owners + j)
         for w in range(windows)

time: 114 us -> 131 us (1.15)
  starting transfers between devices: 37.2 us -> 60.2 us
  other arithmetic: 19.8 us -> 5.66 us
  waiting for transfers between devices: 36.7 us -> 45.1 us
    ppermute x0 -> x11, waiting for transfers between devices: none -> 19 us  [share_tables(): parts.append(lax.ppermute(near, 'pair', turn))]
    ppermute x0 -> x11, starting transfers between devices: none -> 17.6 us  [share_tables(): parts.append(lax.ppermute(near, 'pair', turn))]
    another operation x1 -> x2, other arithmetic: 17.4 us -> 4.19 us  [the longest x1 2.32 us: lag_rows_table(): table = jnp.stack([real, -imag]).astype(jnp.bfloat16)]
    all_to_all x3, waiting for transfers between devices: 17.3 us -> 4.4 us  [local(): lax.all_to_all(x, 'pair', split_axis=0, concat_axis=0, tiled=True)]
    all_to_all x3, starting transfers between devices: 26.8 us -> 32.4 us  [local(): lax.all_to_all(x, 'pair', split_axis=0, concat_axis=0, tiled=True)]
    concatenate x1 -> x2, other arithmetic: 2.39 us -> 0.08 us  [the longest x1 0.08 us: lag_rows_table(): jnp.concatenate([coarse_bins, jnp.arange(fine, dtype=jnp.int32)])]
    ppermute x3, waiting for transfers between devices: 11.1 us -> 13.4 us  [local(): b.append(lax.ppermute(second, 'win', step))]
    sin x0 -> x1, other arithmetic: none -> 1.35 us  [turns(): return (jnp.cos(phases), jnp.sin(phases))]
  transfers between devices with their start and end apart: 7 -> 18, of which waited for: 5 -> 9; matrix products, arithmetic and copies ran while one was open for 18% -> 4% of each run, Pallas kernels for 2% -> 2%
where the time goes in v8:
time: 131 us; the launch traced here: 130 us
  starting transfers between devices  60.2 us (46%)
  waiting for transfers between devices  45.1 us (34%)
  Pallas kernels  18.8 us (14%)
  other arithmetic  5.66 us (4%)
    all_to_all x3, starting transfers between devices, local(): lax.all_to_all(x, 'pair', split_axis=0, concat_axis=0, tiled=True)  32.4 us
    ppermute x11, waiting for transfers between devices, share_tables(): parts.append(lax.ppermute(near, 'pair', turn))  19 us
    ppermute x11, starting transfers between devices, share_tables(): parts.append(lax.ppermute(near, 'pair', turn))  17.6 us
    ppermute x3, waiting for transfers between devices, local(): b.append(lax.ppermute(second, 'win', step))  13.4 us
    pallas_call x1, Pallas kernels, correlate(): pl.pallas_call(functools.partial(correlate_kernel, scaling), grid=(tiles...  11 us
    ppermute x1, waiting for transfers between devices, local(): first = lax.ppermute(first, ('win', 'pair'), turn)  8.29 us
    ppermute x3, starting transfers between devices, local(): b.append(lax.ppermute(second, 'win', step))  7 us
    all_to_all x3, waiting for transfers between devices, local(): lax.all_to_all(x, 'pair', split_axis=0, concat_axis=0, tiled=True)  4.4 us
  transfers between devices with their start and end apart: 18, of which 9 were waited for; matrix products, arithmetic and copies ran while one was open for 4% of the time, Pallas kernels for 2%

profile of v8, /device:TPU:1, one launch (start us, length us, event | category | flops | bytes accessed | tf_op | source)
XLA Modules:
  0.0 130.3 jit_solution(2353765311950690756)
XLA Ops:
  0.0 0.0 copy-start.1
  0.0 0.0 copy-start
  0.0 2.9 %whiten_spread.1 = bf16[2,8,4,8,8,128]{5,4,3,2,1,0:T(8,128)(2,1)} custom-call(s32[1]{0:T(128)} %bitcast.win_ref, bf16[8,1,2,32,1024]{4,3,2,1,0:T(8,128)(2,1)} %x_ref.1), custom_call_target="tpu_custom_call" | custom-call | tf_op jit(solution)/shard_map/whiten_spread/pallas_call | solution.py:50
  2.9 13.0 %all-to-all-start = ((bf16[64,8,8,128]{3,2,1,0:T(8,128)(2,1)}), bf16[64,8,8,128]{3,2,1,0:T(8,128)(2,1)S(1)}, u32[]{:S(2)}, u32[]{:S(2)}) async-start(bf16[64,8,8,128]{3,2,1,0:T(8,128)(2,1)} %bitcast.27), calls=%async_computation | async-start | bytes 2097152 | tf_op jit(solution)/shard_map/all_to_all | solution.py:294
  15.9 0.0 copy-done
  15.9 0.0 copy-done.1
  15.9 0.5 collective-permute-start
  16.5 0.1 pad_add_fusion
  16.6 1.4 %fusion.3 = (f32[80,1024]{1,0:T(8,128)S(1)}, f32[80,1024]{1,0:T(8,128)S(1)}) fusion(s32[1024]{0:T(1024)S(1)} %iota_add_fusion, s32[80]{0:T(128)S(1)} %pad_add_fusion), kind=kLoop, calls=%fused_computation.11 | loop fusion | flops 1146880 | bytes 659776 | tf_op jit(solution)/shard_map/sin | solution.py:276
  18.0 1.9 %subtract_convert_fusion = (bf16[1,64,16,1024]{3,2,1,0:T(8,128)(2,1)S(1)}, bf16[1,64,16,1024]{3,2,1,0:T(8,128)(2,1)S(1)}) fusion(f32[16,1024]{1,0:T(8,128)S(1)} %slice.15, f32[64,1024]{1,0:T(8,128)S(1)} %slice.14, f32[16,1024]{1,0:T(8,128)S(1)} %slice.13, f32[64,1024]{1,0:T(8,128)S(1)} %slice.12), kind=kLoop, calls=%fused_computation.2 | loop fusion | flops 9437184 | bytes 4849664 | tf_op jit(solution)/shard_map/convert
  19.9 0.0 collective-permute-done
  19.9 2.6 %collective-permute-start.7 = (f32[2,4,128]{2,1,0:T(4,128)S(1)}, f32[2,4,128]{2,1,0:T(4,128)S(1)}, u32[]{:S(2)}, u32[]{:S(2)}) collective-permute-start(f32[2,4,128]{2,1,0:T(4,128)S(1)} %pad_maximum_fusion.1), channel_id=1, source_target_pairs={{0,14},{1,15},{2,12},{3,13},{4,10},{5,11},{6,8},{7,9},{8,6},{9,7},... | collective-permute-start | bytes 12296 | tf_op jit(solution)/shard_map/ppermute | solution.py:136
  22.5 2.1 %collective-permute-start.6 = (f32[2,4,128]{2,1,0:T(4,128)S(1)}, f32[2,4,128]{2,1,0:T(4,128)S(1)}, u32[]{:S(2)}, u32[]{:S(2)}) collective-permute-start(f32[2,4,128]{2,1,0:T(4,128)S(1)} %pad_maximum_fusion.1), channel_id=1, source_target_pairs={{0,12},{1,13},{2,14},{3,15},{4,8},{5,9},{6,10},{7,11},{8,4},{9,5},... | collective-permute-start | bytes 12296 | tf_op jit(solution)/shard_map/ppermute | solution.py:136
  24.6 3.3 %collective-permute-start.5 = (f32[2,4,128]{2,1,0:T(4,128)S(1)}, f32[2,4,128]{2,1,0:T(4,128)S(1)}, u32[]{:S(2)}, u32[]{:S(2)}) collective-permute-start(f32[2,4,128]{2,1,0:T(4,128)S(1)} %pad_maximum_fusion.1), channel_id=1, source_target_pairs={{0,10},{1,11},{2,8},{3,9},{4,14},{5,15},{6,12},{7,13},{8,2},{9,3},... | collective-permute-start | bytes 12296 | tf_op jit(solution)/shard_map/ppermute | solution.py:136
  27.9 0.9 collective-permute-start.4
  28.8 1.5 %collective-permute-start.1 = (f32[2,4,128]{2,1,0:T(4,128)S(1)}, f32[2,4,128]{2,1,0:T(4,128)S(1)}, u32[]{:S(2)}, u32[]{:S(2)}) collective-permute-start(f32[2,4,128]{2,1,0:T(4,128)S(1)} %pad_maximum_fusion.1), channel_id=1, source_target_pairs={{0,2},{1,3},{2,0},{3,1},{4,6},{5,7},{6,4},{7,5},{8,10},{9,11},{10,... | collective-permute-start | bytes 12296 | tf_op jit(solution)/shard_map/ppermute | solution.py:136
  30.3 10.3 %collective-permute-done.1 = f32[2,4,128]{2,1,0:T(4,128)S(1)} collective-permute-done((f32[2,4,128]{2,1,0:T(4,128)S(1)}, f32[2,4,128]{2,1,0:T(4,128)S(1)}, u32[]{:S(2)}, u32[]{:S(2)}) %collective-permute-start.1) | collective-permute-done | bytes 4128 | tf_op jit(solution)/shard_map/ppermute | solution.py:136
  40.5 0.5 collective-permute-start.2
  41.1 3.1 %collective-permute-done.2 = f32[2,4,128]{2,1,0:T(4,128)S(1)} collective-permute-done((f32[2,4,128]{2,1,0:T(4,128)S(1)}, f32[2,4,128]{2,1,0:T(4,128)S(1)}, u32[]{:S(2)}, u32[]{:S(2)}) %collective-permute-start.2) | collective-permute-done | bytes 4128 | tf_op jit(solution)/shard_map/ppermute | solution.py:136
  44.2 2.2 %collective-permute-start.3 = (f32[2,4,128]{2,1,0:T(4,128)S(1)}, f32[2,4,128]{2,1,0:T(4,128)S(1)}, u32[]{:S(2)}, u32[]{:S(2)}) collective-permute-start(f32[2,4,128]{2,1,0:T(4,128)S(1)} %pad_maximum_fusion.1), channel_id=1, source_target_pairs={{0,6},{1,7},{2,4},{3,5},{4,2},{5,3},{6,0},{7,1},{8,14},{9,15},{10,... | collective-permute-start | bytes 12296 | tf_op jit(solution)/shard_map/ppermute | solution.py:136
  46.4 2.1 %collective-permute-done.3 = f32[2,4,128]{2,1,0:T(4,128)S(1)} collective-permute-done((f32[2,4,128]{2,1,0:T(4,128)S(1)}, f32[2,4,128]{2,1,0:T(4,128)S(1)}, u32[]{:S(2)}, u32[]{:S(2)}) %collective-permute-start.3) | collective-permute-done | bytes 4128 | tf_op jit(solution)/shard_map/ppermute | solution.py:136
  48.5 0.0 collective-permute-done.4
  48.5 0.0 collective-permute-done.5
  48.5 0.0 collective-permute-done.6
  48.5 0.0 collective-permute-done.7
  48.5 1.5 %collective-permute-start.8 = (f32[16,4,128]{2,1,0:T(4,128)S(1)}, f32[16,4,128]{2,1,0:T(4,128)S(1)}, u32[]{:S(2)}, u32[]{:S(2)}) collective-permute-start(f32[16,4,128]{2,1,0:T(4,128)S(1)} %get-tuple-element.29), channel_id=1, source_target_pairs={{0,16},{1,17},{2,18},{3,19},{4,20},{5,21},{6,22},{7,23},{8,24},{9,... | collective-permute-start | bytes 98312 | tf_op jit(solution)/shard_map/ppermute | solution.py:136
  50.0 2.3 %pad_maximum_fusion = bf16[2,64,16,1024]{3,2,1,0:T(8,128)(2,1)} fusion(bf16[1,64,16,1024]{3,2,1,0:T(8,128)(2,1)S(1)} %get-tuple-element.26, bf16[1,64,16,1024]{3,2,1,0:T(8,128)(2,1)S(1)} %get-tuple-element.25), kind=kLoop, calls=%fused_computation | loop fusion | flops 2097152 | bytes 8388608 | tf_op jit(solution)/shard_map/stack | solution.py:285
  52.3 1.9 %collective-permute-start.10 = (f32[16,4,128]{2,1,0:T(4,128)S(1)}, f32[16,4,128]{2,1,0:T(4,128)S(1)}, u32[]{:S(2)}, u32[]{:S(2)}) collective-permute-start(f32[16,4,128]{2,1,0:T(4,128)S(1)} %get-tuple-element.29), channel_id=1, source_target_pairs={{0,48},{1,49},{2,50},{3,51},{4,52},{5,53},{6,54},{7,55},{8,56},{9,... | collective-permute-start | bytes 98312 | tf_op jit(solution)/shard_map/ppermute | solution.py:136
  54.2 0.7 collective-permute-start.9
  54.9 0.0 collective-permute-done.8
  54.9 3.5 %collective-permute-done.9 = f32[16,4,128]{2,1,0:T(4,128)S(1)} collective-permute-done((f32[16,4,128]{2,1,0:T(4,128)S(1)}, f32[16,4,128]{2,1,0:T(4,128)S(1)}, u32[]{:S(2)}, u32[]{:S(2)}) %collective-permute-start.9) | collective-permute-done | bytes 32800 | tf_op jit(solution)/shard_map/ppermute | solution.py:136
  58.5 0.0 collective-permute-done.10
  58.5 0.8 find_places.1.place_ref
  59.3 0.0 all-to-all-done.x_ref
  59.3 2.2 %pick_second.1 = bf16[64,4,8,128]{3,2,1,0:T(8,128)(2,1)} custom-call(s32[64,128]{1,0:T(8,128)S(1)} %find_places.1.place_ref, bf16[64,8,8,128]{3,2,1,0:T(8,128)(2,1)S(1)} %all-to-all-done.x_ref), custom_call_target="tpu_custom_call" | custom-call | tf_op jit(solution)/shard_map/pick_second/pallas_call | solution.py:113
  61.5 11.8 %all-to-all-start.1 = ((bf16[64,4,8,128]{3,2,1,0:T(8,128)(2,1)}), bf16[64,4,8,128]{3,2,1,0:T(8,128)(2,1)S(1)}, u32[]{:S(2)}, u32[]{:S(2)}) async-start(bf16[64,4,8,128]{3,2,1,0:T(8,128)(2,1)} %pick_second.1), calls=%async_computation.1 | async-start | bytes 1048576 | tf_op jit(solution)/shard_map/all_to_all | solution.py:294
  73.3 1.4 %pick_first.1 = bf16[64,4,8,128]{3,2,1,0:T(8,128)(2,1)S(1)} custom-call(s32[64,128]{1,0:T(8,128)S(1)} %find_places.1.place_ref, bf16[64,8,8,128]{3,2,1,0:T(8,128)(2,1)S(1)} %all-to-all-done.x_ref), custom_call_target="tpu_custom_call" | custom-call | tf_op jit(solution)/shard_map/pick_first/pallas_call | solution.py:113
  74.7 3.2 %collective-permute-start.11 = (bf16[64,4,8,128]{3,2,1,0:T(8,128)(2,1)S(1)}, bf16[64,4,8,128]{3,2,1,0:T(8,128)(2,1)}, u32[]{:S(2)}, u32[]{:S(2)}) collective-permute-start(bf16[64,4,8,128]{3,2,1,0:T(8,128)(2,1)S(1)} %pick_first.1), channel_id=1, source_target_pairs={{0,0},{1,65},{2,130},{3,195},{4,4},{5,69},{6,134},{7,199},{8,8},{9... | collective-permute-start | bytes 1572872 | tf_op jit(solution)/shard_map/ppermute | solution.py:311
  77.9 8.3 %collective-permute-done.11 = bf16[64,4,8,128]{3,2,1,0:T(8,128)(2,1)} collective-permute-done((bf16[64,4,8,128]{3,2,1,0:T(8,128)(2,1)S(1)}, bf16[64,4,8,128]{3,2,1,0:T(8,128)(2,1)}, u32[]{:S(2)}, u32[]{:S(2)}) %collective-permute-start.11) | collective-permute-done | bytes 524320 | tf_op jit(solution)/shard_map/ppermute | solution.py:311
  86.2 4.4 %all-to-all-done.1 = bf16[64,4,8,128]{3,2,1,0:T(8,128)(2,1)S(1)} async-done(((bf16[64,4,8,128]{3,2,1,0:T(8,128)(2,1)}), bf16[64,4,8,128]{3,2,1,0:T(8,128)(2,1)S(1)}, u32[]{:S(2)}, u32[]{:S(2)}) %all-to-all-start.1) | async-done | bytes 524320 | tf_op jit(solution)/shard_map/all_to_all | solution.py:294
  90.6 2.9 %collective-permute-start.12 = (bf16[64,4,8,128]{3,2,1,0:T(8,128)(2,1)S(1)}, bf16[64,4,8,128]{3,2,1,0:T(8,128)(2,1)S(1)}, u32[]{:S(2)}, u32[]{:S(2)}) collective-permute-start(bf16[64,4,8,128]{3,2,1,0:T(8,128)(2,1)S(1)} %all-to-all-done.1), channel_id=1, source_target_pairs={{0,128},{64,192},{128,0},{192,64},{1,129},{65,193},{129,1},{193,65... | collective-permute-start | bytes 1572872 | tf_op jit(solution)/shard_map/ppermute | solution.py:317
  93.5 7.6 %all-to-all-start.2 = ((bf16[64,4,8,128]{3,2,1,0:T(8,128)(2,1)}), bf16[64,4,8,128]{3,2,1,0:T(8,128)(2,1)S(1)}, u32[]{:S(2)}, u32[]{:S(2)}) async-start(bf16[64,4,8,128]{3,2,1,0:T(8,128)(2,1)} %collective-permute-done.11), calls=%async_computation.2 | async-start | bytes 1048576 | tf_op jit(solution)/shard_map/all_to_all | solution.py:294
  101.1 4.1 %collective-permute-start.14 = (bf16[64,4,8,128]{3,2,1,0:T(8,128)(2,1)S(1)}, bf16[64,4,8,128]{3,2,1,0:T(8,128)(2,1)S(1)}, u32[]{:S(2)}, u32[]{:S(2)}) collective-permute-start(bf16[64,4,8,128]{3,2,1,0:T(8,128)(2,1)S(1)} %all-to-all-done.1), channel_id=1, source_target_pairs={{0,192},{64,0},{128,64},{192,128},{1,193},{65,1},{129,65},{193,129... | collective-permute-start | bytes 1572872 | tf_op jit(solution)/shard_map/ppermute | solution.py:317
  105.2 0.0 collective-permute-start.13
  105.2 0.1 collective-permute-done.12.refs_0_
  105.3 0.5 settle.1.win_ref
  105.8 11.1 %collective-permute-done.14 = bf16[64,4,8,128]{3,2,1,0:T(8,128)(2,1)S(1)} collective-permute-done((bf16[64,4,8,128]{3,2,1,0:T(8,128)(2,1)S(1)}, bf16[64,4,8,128]{3,2,1,0:T(8,128)(2,1)S(1)}, u32[]{:S(2)}, u32[]{:S(2)}) %collective-permute-start.14) | collective-permute-done | bytes 524320 | tf_op jit(solution)/shard_map/ppermute | solution.py:317
  116.9 2.2 %collective-permute-done.13 = bf16[64,4,8,128]{3,2,1,0:T(8,128)(2,1)S(1)} collective-permute-done((bf16[64,4,8,128]{3,2,1,0:T(8,128)(2,1)S(1)}, bf16[64,4,8,128]{3,2,1,0:T(8,128)(2,1)S(1)}, u32[]{:S(2)}, u32[]{:S(2)}) %collective-permute-start.13) | collective-permute-done | bytes 524320 | tf_op jit(solution)/shard_map/ppermute | solution.py:317
  119.1 0.0 all-to-all-done.2
  119.1 11.0 %correlate.1 = bf16[8,4,32,1024]{3,2,1,0:T(8,128)(2,1)} custom-call(s32[1]{0:T(128)} %settle.1.win_ref, bf16[2,8,4,4,8,128]{5,4,3,2,1,0:T(8,128)(2,1)S(1)} %bitcast.22, bf16[2,8,4,4,8,128]{5,4,3,2,1,0:T(8,128)(2,1)S(1)} %bitcast.21, bf16[2,8,4,4,8,128]{5,4,3,2,1,0:T(8,128)(2,1)S(1)} %bitcast.25, bf16[2,8,4,4,8,128]{5,4,3,2,1,0:T(8,128)(2,1)S(1)} %bitcast.23, ...), custom_call_target="tpu_custom_call" | custom-call | tf_op jit(solution)/shard_map/correlate/pallas_call | solution.py:232
  (23 shorter events, 0.2 us)
Async XLA Ops:
  0.0 15.9 %copy-start.1 = (s32[4,2]{0,1:T(2,128)S(1)}, s32[4,2]{0,1:T(2,128)}, u32[]{:S(2)}) copy-start(s32[4,2]{0,1:T(2,128)} %param.5) | copy-start | bytes 100
  0.0 15.9 %copy-start = (s32[1,64,2]{1,2,0:T(2,128)S(1)}, s32[1,64,2]{1,2,0:T(2,128)}, u32[]{:S(2)}) copy-start(s32[1,64,2]{1,2,0:T(2,128)} %param.4) | copy-start | bytes 1540
  2.9 56.4 %all-to-all-start = ((bf16[64,8,8,128]{3,2,1,0:T(8,128)(2,1)}), bf16[64,8,8,128]{3,2,1,0:T(8,128)(2,1)S(1)}, u32[]{:S(2)}, u32[]{:S(2)}) async-start(bf16[64,8,8,128]{3,2,1,0:T(8,128)(2,1)} %bitcast.27), calls=%async_computation | async-start | bytes 2097152 | tf_op jit(solution)/shard_map/all_to_all | solution.py:294
  15.9 4.0 %collective-permute-start = (f32[1,4,128]{2,1,0:T(4,128)S(1)}, f32[1,4,128]{2,1,0:T(4,128)S(1)}, u32[]{:S(2)}, u32[]{:S(2)}) collective-permute-start(f32[1,4,128]{2,1,0:T(4,128)S(1)} %fusion.5), channel_id=1, source_target_pairs={{0,1},{1,0},{2,3},{3,2},{4,5},{5,4},{6,7},{7,6},{8,9},{9,8},{10,11... | collective-permute-start | bytes 6152 | tf_op jit(solution)/shard_map/ppermute | solution.py:136
  19.9 28.6 %collective-permute-start.7 = (f32[2,4,128]{2,1,0:T(4,128)S(1)}, f32[2,4,128]{2,1,0:T(4,128)S(1)}, u32[]{:S(2)}, u32[]{:S(2)}) collective-permute-start(f32[2,4,128]{2,1,0:T(4,128)S(1)} %pad_maximum_fusion.1), channel_id=1, source_target_pairs={{0,14},{1,15},{2,12},{3,13},{4,10},{5,11},{6,8},{7,9},{8,6},{9,7},... | collective-permute-start | bytes 12296 | tf_op jit(solution)/shard_map/ppermute | solution.py:136
  22.5 26.0 %collective-permute-start.6 = (f32[2,4,128]{2,1,0:T(4,128)S(1)}, f32[2,4,128]{2,1,0:T(4,128)S(1)}, u32[]{:S(2)}, u32[]{:S(2)}) collective-permute-start(f32[2,4,128]{2,1,0:T(4,128)S(1)} %pad_maximum_fusion.1), channel_id=1, source_target_pairs={{0,12},{1,13},{2,14},{3,15},{4,8},{5,9},{6,10},{7,11},{8,4},{9,5},... | collective-permute-start | bytes 12296 | tf_op jit(solution)/shard_map/ppermute | solution.py:136
  24.6 23.9 %collective-permute-start.5 = (f32[2,4,128]{2,1,0:T(4,128)S(1)}, f32[2,4,128]{2,1,0:T(4,128)S(1)}, u32[]{:S(2)}, u32[]{:S(2)}) collective-permute-start(f32[2,4,128]{2,1,0:T(4,128)S(1)} %pad_maximum_fusion.1), channel_id=1, source_target_pairs={{0,10},{1,11},{2,8},{3,9},{4,14},{5,15},{6,12},{7,13},{8,2},{9,3},... | collective-permute-start | bytes 12296 | tf_op jit(solution)/shard_map/ppermute | solution.py:136
  27.9 20.6 %collective-permute-start.4 = (f32[2,4,128]{2,1,0:T(4,128)S(1)}, f32[2,4,128]{2,1,0:T(4,128)S(1)}, u32[]{:S(2)}, u32[]{:S(2)}) collective-permute-start(f32[2,4,128]{2,1,0:T(4,128)S(1)} %pad_maximum_fusion.1), channel_id=1, source_target_pairs={{0,8},{1,9},{2,10},{3,11},{4,12},{5,13},{6,14},{7,15},{8,0},{9,1},... | collective-permute-start | bytes 12296 | tf_op jit(solution)/shard_map/ppermute | solution.py:136
  28.8 11.7 %collective-permute-start.1 = (f32[2,4,128]{2,1,0:T(4,128)S(1)}, f32[2,4,128]{2,1,0:T(4,128)S(1)}, u32[]{:S(2)}, u32[]{:S(2)}) collective-permute-start(f32[2,4,128]{2,1,0:T(4,128)S(1)} %pad_maximum_fusion.1), channel_id=1, source_target_pairs={{0,2},{1,3},{2,0},{3,1},{4,6},{5,7},{6,4},{7,5},{8,10},{9,11},{10,... | collective-permute-start | bytes 12296 | tf_op jit(solution)/shard_map/ppermute | solution.py:136
  40.5 3.7 %collective-permute-start.2 = (f32[2,4,128]{2,1,0:T(4,128)S(1)}, f32[2,4,128]{2,1,0:T(4,128)S(1)}, u32[]{:S(2)}, u32[]{:S(2)}) collective-permute-start(f32[2,4,128]{2,1,0:T(4,128)S(1)} %pad_maximum_fusion.1), channel_id=1, source_target_pairs={{0,4},{1,5},{2,6},{3,7},{4,0},{5,1},{6,2},{7,3},{8,12},{9,13},{10,... | collective-permute-start | bytes 12296 | tf_op jit(solution)/shard_map/ppermute | solution.py:136
  44.2 4.3 %collective-permute-start.3 = (f32[2,4,128]{2,1,0:T(4,128)S(1)}, f32[2,4,128]{2,1,0:T(4,128)S(1)}, u32[]{:S(2)}, u32[]{:S(2)}) collective-permute-start(f32[2,4,128]{2,1,0:T(4,128)S(1)} %pad_maximum_fusion.1), channel_id=1, source_target_pairs={{0,6},{1,7},{2,4},{3,5},{4,2},{5,3},{6,0},{7,1},{8,14},{9,15},{10,... | collective-permute-start | bytes 12296 | tf_op jit(solution)/shard_map/ppermute | solution.py:136
  48.5 6.4 %collective-permute-start.8 = (f32[16,4,128]{2,1,0:T(4,128)S(1)}, f32[16,4,128]{2,1,0:T(4,128)S(1)}, u32[]{:S(2)}, u32[]{:S(2)}) collective-permute-start(f32[16,4,128]{2,1,0:T(4,128)S(1)} %get-tuple-element.29), channel_id=1, source_target_pairs={{0,16},{1,17},{2,18},{3,19},{4,20},{5,21},{6,22},{7,23},{8,24},{9,... | collective-permute-start | bytes 98312 | tf_op jit(solution)/shard_map/ppermute | solution.py:136
  52.3 6.1 %collective-permute-start.10 = (f32[16,4,128]{2,1,0:T(4,128)S(1)}, f32[16,4,128]{2,1,0:T(4,128)S(1)}, u32[]{:S(2)}, u32[]{:S(2)}) collective-permute-start(f32[16,4,128]{2,1,0:T(4,128)S(1)} %get-tuple-element.29), channel_id=1, source_target_pairs={{0,48},{1,49},{2,50},{3,51},{4,52},{5,53},{6,54},{7,55},{8,56},{9,... | collective-permute-start | bytes 98312 | tf_op jit(solution)/shard_map/ppermute | solution.py:136
  54.2 4.3 %collective-permute-start.9 = (f32[16,4,128]{2,1,0:T(4,128)S(1)}, f32[16,4,128]{2,1,0:T(4,128)S(1)}, u32[]{:S(2)}, u32[]{:S(2)}) collective-permute-start(f32[16,4,128]{2,1,0:T(4,128)S(1)} %get-tuple-element.29), channel_id=1, source_target_pairs={{0,32},{1,33},{2,34},{3,35},{4,36},{5,37},{6,38},{7,39},{8,40},{9,... | collective-permute-start | bytes 98312 | tf_op jit(solution)/shard_map/ppermute | solution.py:136
  61.5 29.1 %all-to-all-start.1 = ((bf16[64,4,8,128]{3,2,1,0:T(8,128)(2,1)}), bf16[64,4,8,128]{3,2,1,0:T(8,128)(2,1)S(1)}, u32[]{:S(2)}, u32[]{:S(2)}) async-start(bf16[64,4,8,128]{3,2,1,0:T(8,128)(2,1)} %pick_second.1), calls=%async_computation.1 | async-start | bytes 1048576 | tf_op jit(solution)/shard_map/all_to_all | solution.py:294
  74.7 11.5 %collective-permute-start.11 = (bf16[64,4,8,128]{3,2,1,0:T(8,128)(2,1)S(1)}, bf16[64,4,8,128]{3,2,1,0:T(8,128)(2,1)}, u32[]{:S(2)}, u32[]{:S(2)}) collective-permute-start(bf16[64,4,8,128]{3,2,1,0:T(8,128)(2,1)S(1)} %pick_first.1), channel_id=1, source_target_pairs={{0,0},{1,65},{2,130},{3,195},{4,4},{5,69},{6,134},{7,199},{8,8},{9... | collective-permute-start | bytes 1572872 | tf_op jit(solution)/shard_map/ppermute | solution.py:311
  90.6 14.7 %collective-permute-start.12 = (bf16[64,4,8,128]{3,2,1,0:T(8,128)(2,1)S(1)}, bf16[64,4,8,128]{3,2,1,0:T(8,128)(2,1)S(1)}, u32[]{:S(2)}, u32[]{:S(2)}) collective-permute-start(bf16[64,4,8,128]{3,2,1,0:T(8,128)(2,1)S(1)} %all-to-all-done.1), channel_id=1, source_target_pairs={{0,128},{64,192},{128,0},{192,64},{1,129},{65,193},{129,1},{193,65... | collective-permute-start | bytes 1572872 | tf_op jit(solution)/shard_map/ppermute | solution.py:317
  93.5 25.6 %all-to-all-start.2 = ((bf16[64,4,8,128]{3,2,1,0:T(8,128)(2,1)}), bf16[64,4,8,128]{3,2,1,0:T(8,128)(2,1)S(1)}, u32[]{:S(2)}, u32[]{:S(2)}) async-start(bf16[64,4,8,128]{3,2,1,0:T(8,128)(2,1)} %collective-permute-done.11), calls=%async_computation.2 | async-start | bytes 1048576 | tf_op jit(solution)/shard_map/all_to_all | solution.py:294
  101.1 15.8 %collective-permute-start.14 = (bf16[64,4,8,128]{3,2,1,0:T(8,128)(2,1)S(1)}, bf16[64,4,8,128]{3,2,1,0:T(8,128)(2,1)S(1)}, u32[]{:S(2)}, u32[]{:S(2)}) collective-permute-start(bf16[64,4,8,128]{3,2,1,0:T(8,128)(2,1)S(1)} %all-to-all-done.1), channel_id=1, source_target_pairs={{0,192},{64,0},{128,64},{192,128},{1,193},{65,1},{129,65},{193,129... | collective-permute-start | bytes 1572872 | tf_op jit(solution)/shard_map/ppermute | solution.py:317
  105.2 13.9 %collective-permute-start.13 = (bf16[64,4,8,128]{3,2,1,0:T(8,128)(2,1)S(1)}, bf16[64,4,8,128]{3,2,1,0:T(8,128)(2,1)S(1)}, u32[]{:S(2)}, u32[]{:S(2)}) collective-permute-start(bf16[64,4,8,128]{3,2,1,0:T(8,128)(2,1)S(1)} %all-to-all-done.1), channel_id=1, source_target_pairs={{0,64},{64,128},{128,192},{192,0},{1,65},{65,129},{129,193},{193,1... | collective-permute-start | bytes 1572872 | tf_op jit(solution)/shard_map/ppermute | solution.py:317

commit v9 on v6

--- a/solution.py
+++ b/solution.py
@@ -19,17 +19,19 @@
 
 
 def whiten_kernel(win_ref, x_ref, sent_ref, slots_ref, out_ref, table_ref):
-    blocks = x_ref.shape[0]
+    blocks, _, _, channels, _ = x_ref.shape
     _, lane_groups, groups = out_ref.shape[:3]
-    step = pl.program_id(0)
     row_band = lax.broadcasted_iota(jnp.int32, (LANES, LANES), 0) // BAND
     column_band = lax.broadcasted_iota(jnp.int32, (LANES, LANES), 1) // BAND
     ones = jnp.where(row_band == column_band, 1.0, 0.0).astype(jnp.bfloat16)
     ones = jnp.concatenate([ones, ones, ones], axis=0)
+    places = [lax.rem(group + groups - win_ref[0], groups) for group in range(groups)]
     for lane_group in range(lane_groups):
         lanes = slice(lane_group * LANES, (lane_group + 1) * LANES)
-        real = x_ref[:, 0, 0, :, lanes].astype(jnp.float32).reshape(blocks * 16, LANES)
-        imag = x_ref[:, 0, 1, :, lanes].astype(jnp.float32).reshape(blocks * 16, LANES)
+        real, imag = [
+            x_ref[:, 0, part, :, lanes].astype(jnp.float32).reshape(blocks * channels, LANES)
+            for part in range(2)
+        ]
         rest = real * real + imag * imag
         terms = []
         for _ in range(3):
@@ -38,34 +40,40 @@
         power = jnp.dot(jnp.concatenate(terms, axis=1), ones, preferred_element_type=jnp.float32)
         scale = lax.rsqrt(power * (1.0 / (2 * BAND)) + 1e-06)
         for part, rows in enumerate((real * scale, imag * scale)):
-            rows = rows.reshape(blocks, 2, GROUP, LANES)
-            for half in range(2):
-                place = lax.rem(2 * step + half + groups - win_ref[0], groups)
-                out_ref[part, lane_group, place, :blocks] = rows[:, half].astype(jnp.bfloat16)
-
-    @pl.when(step == 0)
+            rows = rows.reshape(blocks, groups, GROUP, LANES)
+            for group in range(groups):
+                out_ref[part, lane_group, places[group], :blocks] = rows[:, group].astype(
+                    jnp.bfloat16
+                )
+
+    @pl.when(pl.program_id(0) == 0)
     def _():
         table_ref[...] = jnp.zeros_like(table_ref)
         table_ref[0:2, : sent_ref.shape[1]] = sent_ref[...].astype(jnp.float32)
         table_ref[2:4, : slots_ref.shape[1]] = slots_ref[...].astype(jnp.float32)
-        piece = table_ref[...].astype(jnp.bfloat16)
-        shape = out_ref.shape
-        out_ref[:, :, :, blocks] = jnp.broadcast_to(piece, shape[:3] + shape[4:])
+
+    piece = table_ref[...].astype(jnp.bfloat16)
+    shape = out_ref.shape
+    out_ref[:, :, :, blocks] = jnp.broadcast_to(piece, shape[:3] + shape[4:])
 
 
 def whiten_spread(win, spectra, sent, slots):
     blocks, _, parts, channels, bins = spectra.shape
     shape = (parts, bins // LANES, channels // GROUP, blocks + 1, GROUP, LANES)
+    steps = 2
+    width = bins // steps
     return pl.pallas_call(
         whiten_kernel,
-        grid=(channels // 16,),
+        grid=(steps,),
         in_specs=[
             pl.BlockSpec(memory_space=pltpu.SMEM),
-            pl.BlockSpec((blocks, 1, parts, 16, bins), lambda g: (0, 0, 0, g, 0)),
+            pl.BlockSpec((blocks, 1, parts, channels, width), lambda g: (0, 0, 0, 0, g)),
             pl.BlockSpec(sent.shape, lambda g: (0, 0)),
             pl.BlockSpec(slots.shape, lambda g: (0, 0)),
         ],
-        out_specs=pl.BlockSpec(shape, lambda g: (0,) * len(shape)),
+        out_specs=pl.BlockSpec(
+            (parts, width // LANES) + shape[2:], lambda g: (0, g, 0, 0, 0, 0)
+        ),
         out_shape=jax.ShapeDtypeStruct(shape, jnp.bfloat16),
         scratch_shapes=[pltpu.VMEM((GROUP, LANES), jnp.float32)],
         compiler_params=pltpu.CompilerParams(vmem_limit_bytes=60 * 2**20),
@@ -78,7 +86,7 @@
 
     def one_owner(owner, carry):
         for tile in range(out_ref.shape[1]):
-            out_ref[owner, tile] = flat[place_ref[owner, start + tile]]
+            out_ref[owner, tile] = flat[place_ref[start + tile, owner]]
         return carry
 
     lax.fori_loop(0, out_ref.shape[0], one_owner, 0, unroll=4)
@@ -100,7 +108,8 @@
             hit = lane == (slot % 2) * HALF + slot // 2
             place = jnp.sum(jnp.where(hit, by_owner, 0), axis=1, keepdims=True)
             places = jnp.where(lane == part * tiles + tile, place, places)
-    index_ref[...] = places
+    wide = jnp.concatenate([places, places], axis=0).astype(jnp.float32).T
+    index_ref[...] = wide[: 2 * tiles].astype(jnp.int32)
     copy = pltpu.make_async_copy(index_ref, place_ref, sem)
     copy.start()
     copy.wait()
@@ -115,11 +124,11 @@
         out_specs=[pl.BlockSpec(memory_space=pltpu.VMEM)] * 2,
         out_shape=[
             jax.ShapeDtypeStruct((owners, tiles, GROUP, LANES), jnp.bfloat16),
-            jax.ShapeDtypeStruct((owners, LANES), jnp.int32),
+            jax.ShapeDtypeStruct((2 * tiles, LANES), jnp.int32),
         ],
         scratch_shapes=[
             pltpu.VMEM((owners * GROUP, LANES), jnp.float32),
-            pltpu.SMEM((owners, LANES), jnp.int32),
+            pltpu.SMEM((2 * tiles, LANES), jnp.int32),
             pltpu.SemaphoreType.DMA,
         ],
         compiler_params=pltpu.CompilerParams(vmem_limit_bytes=24 * 2**20),

time: 114 us -> 113 us (level)
  transfers between devices with their start and end apart: 7 -> 7, of which waited for: 5 -> 6; matrix products, arithmetic and copies ran while one was open for 18% -> 18% of each run, Pallas kernels for 2% -> 1%
where the time goes in v9:
time: 113 us; the launch traced here: 112 us
  waiting for transfers between devices  37 us (33%)
  starting transfers between devices  36.9 us (33%)
  other arithmetic  19.8 us (18%)
  Pallas kernels  18 us (16%)
    all_to_all x3, starting transfers between devices, local(): lax.all_to_all(x, 'pair', split_axis=0, concat_axis=0, tiled=True)  26.4 us
    all_to_all x3, waiting for transfers between devices, local(): lax.all_to_all(x, 'pair', split_axis=0, concat_axis=0, tiled=True)  17.6 us
    another operation x1, other arithmetic  17.4 us
    ppermute x3, waiting for transfers between devices, local(): b.append(lax.ppermute(second, 'win', step))  11.1 us
    pallas_call x1, Pallas kernels, correlate(): pl.pallas_call(functools.partial(correlate_kernel, scaling), grid=(tiles...  11.1 us
    ppermute x1, waiting for transfers between devices, local(): first = lax.ppermute(first, ('win', 'pair'), turn)  8.29 us
    ppermute x3, starting transfers between devices, local(): b.append(lax.ppermute(second, 'win', step))  7.27 us
    ppermute x1, starting transfers between devices, local(): first = lax.ppermute(first, ('win', 'pair'), turn)  3.21 us
  transfers between devices with their start and end apart: 7, of which 6 were waited for; matrix products, arithmetic and copies ran while one was open for 18% of the time, Pallas kernels for 1%

profile of v9, /device:TPU:1, one launch (start us, length us, event | category | flops | bytes accessed | tf_op | source)
XLA Modules:
  0.0 112.0 jit_solution(16915248487386524583)
XLA Ops:
  0.0 2.7 %whiten_spread.1 = bf16[2,8,4,9,8,128]{5,4,3,2,1,0:T(8,128)(2,1)} custom-call(s32[1]{0:T(128)} %bitcast.win_ref, bf16[8,1,2,32,1024]{4,3,2,1,0:T(8,128)(2,1)} %x_ref.1, s32[2,64]{1,0:T(2,128)} %bitcast.17, s32[2,4]{1,0:T(2,128)} %bitcast.18), custom_call_target="tpu_custom_call" | custom-call | tf_op jit(solution)/shard_map/whiten_spread/pallas_call | solution.py:65
  2.7 13.0 %all-to-all-start = ((bf16[64,9,8,128]{3,2,1,0:T(8,128)(2,1)}), bf16[64,9,8,128]{3,2,1,0:T(8,128)(2,1)S(1)}, u32[]{:S(2)}, u32[]{:S(2)}) async-start(bf16[64,9,8,128]{3,2,1,0:T(8,128)(2,1)} %bitcast.16), calls=%async_computation | async-start | bytes 2359296 | tf_op jit(solution)/shard_map/all_to_all | solution.py:294
  15.7 17.4 %cosine_convert_fusion = (bf16[1024,1024]{1,0:T(8,128)(2,1)S(1)}, bf16[1024,1024]{1,0:T(8,128)(2,1)S(1)}) fusion(s32[1024]{0:T(1024)S(1)} %get-tuple-element.19, s32[1024]{0:T(1024)S(1)} %get-tuple-element.20), kind=kLoop, calls=%fused_computation.10 | loop fusion | flops 17825792 | bytes 4202496 | tf_op jit(solution)/shard_map/convert
  33.2 2.4 %pad_maximum_fusion.refs_4_ = bf16[2048,1024]{1,0:T(8,128)(2,1)} fusion(bf16[1024,1024]{1,0:T(8,128)(2,1)S(1)} %get-tuple-element.18, bf16[1024,1024]{1,0:T(8,128)(2,1)S(1)} %get-tuple-element.17), kind=kLoop, calls=%fused_computation.8 | loop fusion | flops 8388608 | bytes 8388608 | tf_op jit(solution)/shard_map/concatenate | solution.py:286
  35.6 11.5 %all-to-all-done.x_ref = bf16[64,9,8,128]{3,2,1,0:T(8,128)(2,1)S(1)} async-done(((bf16[64,9,8,128]{3,2,1,0:T(8,128)(2,1)}), bf16[64,9,8,128]{3,2,1,0:T(8,128)(2,1)S(1)}, u32[]{:S(2)}, u32[]{:S(2)}) %all-to-all-start) | async-done | bytes 1179680 | tf_op jit(solution)/shard_map/all_to_all | solution.py:294
  47.1 2.6 %pick_second.1 = (bf16[64,4,8,128]{3,2,1,0:T(8,128)(2,1)}, s32[8,128]{1,0:T(8,128)S(1)}) custom-call(bf16[64,9,8,128]{3,2,1,0:T(8,128)(2,1)S(1)} %all-to-all-done.x_ref), custom_call_target="tpu_custom_call" | custom-call | tf_op jit(solution)/shard_map/pick_second/pallas_call | solution.py:121
  49.8 6.2 %all-to-all-start.1 = ((bf16[64,4,8,128]{3,2,1,0:T(8,128)(2,1)}), bf16[64,4,8,128]{3,2,1,0:T(8,128)(2,1)S(1)}, u32[]{:S(2)}, u32[]{:S(2)}) async-start(bf16[64,4,8,128]{3,2,1,0:T(8,128)(2,1)} %get-tuple-element.12), calls=%async_computation.1 | async-start | bytes 1048576 | tf_op jit(solution)/shard_map/all_to_all | solution.py:294
  56.0 1.0 pick_first.1
  57.0 3.2 %collective-permute-start = (bf16[64,4,8,128]{3,2,1,0:T(8,128)(2,1)S(1)}, bf16[64,4,8,128]{3,2,1,0:T(8,128)(2,1)}, u32[]{:S(2)}, u32[]{:S(2)}) collective-permute-start(bf16[64,4,8,128]{3,2,1,0:T(8,128)(2,1)S(1)} %pick_first.1), channel_id=1, source_target_pairs={{0,0},{1,65},{2,130},{3,195},{4,4},{5,69},{6,134},{7,199},{8,8},{9... | collective-permute-start | bytes 1572872 | tf_op jit(solution)/shard_map/ppermute | solution.py:308
  60.2 8.3 %collective-permute-done = bf16[64,4,8,128]{3,2,1,0:T(8,128)(2,1)} collective-permute-done((bf16[64,4,8,128]{3,2,1,0:T(8,128)(2,1)S(1)}, bf16[64,4,8,128]{3,2,1,0:T(8,128)(2,1)}, u32[]{:S(2)}, u32[]{:S(2)}) %collective-permute-start) | collective-permute-done | bytes 524320 | tf_op jit(solution)/shard_map/ppermute | solution.py:308
  68.5 4.8 %all-to-all-done.1 = bf16[64,4,8,128]{3,2,1,0:T(8,128)(2,1)S(1)} async-done(((bf16[64,4,8,128]{3,2,1,0:T(8,128)(2,1)}), bf16[64,4,8,128]{3,2,1,0:T(8,128)(2,1)S(1)}, u32[]{:S(2)}, u32[]{:S(2)}) %all-to-all-start.1) | async-done | bytes 524320 | tf_op jit(solution)/shard_map/all_to_all | solution.py:294
  73.3 2.9 %collective-permute-start.1 = (bf16[64,4,8,128]{3,2,1,0:T(8,128)(2,1)S(1)}, bf16[64,4,8,128]{3,2,1,0:T(8,128)(2,1)S(1)}, u32[]{:S(2)}, u32[]{:S(2)}) collective-permute-start(bf16[64,4,8,128]{3,2,1,0:T(8,128)(2,1)S(1)} %all-to-all-done.1), channel_id=1, source_target_pairs={{0,128},{64,192},{128,0},{192,64},{1,129},{65,193},{129,1},{193,65... | collective-permute-start | bytes 1572872 | tf_op jit(solution)/shard_map/ppermute | solution.py:314
  76.2 7.2 %all-to-all-start.2 = ((bf16[64,4,8,128]{3,2,1,0:T(8,128)(2,1)}), bf16[64,4,8,128]{3,2,1,0:T(8,128)(2,1)S(1)}, u32[]{:S(2)}, u32[]{:S(2)}) async-start(bf16[64,4,8,128]{3,2,1,0:T(8,128)(2,1)} %collective-permute-done), calls=%async_computation.2 | async-start | bytes 1048576 | tf_op jit(solution)/shard_map/all_to_all | solution.py:294
  83.4 3.0 %collective-permute-start.2 = (bf16[64,4,8,128]{3,2,1,0:T(8,128)(2,1)S(1)}, bf16[64,4,8,128]{3,2,1,0:T(8,128)(2,1)S(1)}, u32[]{:S(2)}, u32[]{:S(2)}) collective-permute-start(bf16[64,4,8,128]{3,2,1,0:T(8,128)(2,1)S(1)} %all-to-all-done.1), channel_id=1, source_target_pairs={{0,64},{64,128},{128,192},{192,0},{1,65},{65,129},{129,193},{193,1... | collective-permute-start | bytes 1572872 | tf_op jit(solution)/shard_map/ppermute | solution.py:314
  86.5 1.3 %collective-permute-start.3 = (bf16[64,4,8,128]{3,2,1,0:T(8,128)(2,1)S(1)}, bf16[64,4,8,128]{3,2,1,0:T(8,128)(2,1)S(1)}, u32[]{:S(2)}, u32[]{:S(2)}) collective-permute-start(bf16[64,4,8,128]{3,2,1,0:T(8,128)(2,1)S(1)} %all-to-all-done.1), channel_id=1, source_target_pairs={{0,192},{64,0},{128,64},{192,128},{1,193},{65,1},{129,65},{193,129... | collective-permute-start | bytes 1572872 | tf_op jit(solution)/shard_map/ppermute | solution.py:314
  87.8 0.2 collective-permute-done.1.refs_0_
  88.0 0.5 settle.1.win_ref
  88.5 10.9 %collective-permute-done.2 = bf16[64,4,8,128]{3,2,1,0:T(8,128)(2,1)S(1)} collective-permute-done((bf16[64,4,8,128]{3,2,1,0:T(8,128)(2,1)S(1)}, bf16[64,4,8,128]{3,2,1,0:T(8,128)(2,1)S(1)}, u32[]{:S(2)}, u32[]{:S(2)}) %collective-permute-start.2) | collective-permute-done | bytes 524320 | tf_op jit(solution)/shard_map/ppermute | solution.py:314
  99.4 0.0 collective-permute-done.3
  99.4 1.3 %all-to-all-done.2 = bf16[64,4,8,128]{3,2,1,0:T(8,128)(2,1)S(1)} async-done(((bf16[64,4,8,128]{3,2,1,0:T(8,128)(2,1)}), bf16[64,4,8,128]{3,2,1,0:T(8,128)(2,1)S(1)}, u32[]{:S(2)}, u32[]{:S(2)}) %all-to-all-start.2) | async-done | bytes 524320 | tf_op jit(solution)/shard_map/all_to_all | solution.py:294
  100.7 11.1 %correlate.1 = bf16[8,4,32,1024]{3,2,1,0:T(8,128)(2,1)} custom-call(s32[1]{0:T(128)} %settle.1.win_ref, bf16[2,8,4,4,8,128]{5,4,3,2,1,0:T(8,128)(2,1)S(1)} %bitcast.12, bf16[2,8,4,4,8,128]{5,4,3,2,1,0:T(8,128)(2,1)S(1)} %bitcast.11, bf16[2,8,4,4,8,128]{5,4,3,2,1,0:T(8,128)(2,1)S(1)} %bitcast.14, bf16[2,8,4,4,8,128]{5,4,3,2,1,0:T(8,128)(2,1)S(1)} %bitcast.13, ...), custom_call_target="tpu_custom_call" | custom-call | tf_op jit(solution)/shard_map/correlate/pallas_call | solution.py:244
  (1 shorter events, 0.0 us)
Async XLA Ops:
  2.7 44.4 %all-to-all-start = ((bf16[64,9,8,128]{3,2,1,0:T(8,128)(2,1)}), bf16[64,9,8,128]{3,2,1,0:T(8,128)(2,1)S(1)}, u32[]{:S(2)}, u32[]{:S(2)}) async-start(bf16[64,9,8,128]{3,2,1,0:T(8,128)(2,1)} %bitcast.16), calls=%async_computation | async-start | bytes 2359296 | tf_op jit(solution)/shard_map/all_to_all | solution.py:294
  49.8 23.5 %all-to-all-start.1 = ((bf16[64,4,8,128]{3,2,1,0:T(8,128)(2,1)}), bf16[64,4,8,128]{3,2,1,0:T(8,128)(2,1)S(1)}, u32[]{:S(2)}, u32[]{:S(2)}) async-start(bf16[64,4,8,128]{3,2,1,0:T(8,128)(2,1)} %get-tuple-element.12), calls=%async_computation.1 | async-start | bytes 1048576 | tf_op jit(solution)/shard_map/all_to_all | solution.py:294
  57.0 11.5 %collective-permute-start = (bf16[64,4,8,128]{3,2,1,0:T(8,128)(2,1)S(1)}, bf16[64,4,8,128]{3,2,1,0:T(8,128)(2,1)}, u32[]{:S(2)}, u32[]{:S(2)}) collective-permute-start(bf16[64,4,8,128]{3,2,1,0:T(8,128)(2,1)S(1)} %pick_first.1), channel_id=1, source_target_pairs={{0,0},{1,65},{2,130},{3,195},{4,4},{5,69},{6,134},{7,199},{8,8},{9... | collective-permute-start | bytes 1572872 | tf_op jit(solution)/shard_map/ppermute | solution.py:308
  73.3 14.7 %collective-permute-start.1 = (bf16[64,4,8,128]{3,2,1,0:T(8,128)(2,1)S(1)}, bf16[64,4,8,128]{3,2,1,0:T(8,128)(2,1)S(1)}, u32[]{:S(2)}, u32[]{:S(2)}) collective-permute-start(bf16[64,4,8,128]{3,2,1,0:T(8,128)(2,1)S(1)} %all-to-all-done.1), channel_id=1, source_target_pairs={{0,128},{64,192},{128,0},{192,64},{1,129},{65,193},{129,1},{193,65... | collective-permute-start | bytes 1572872 | tf_op jit(solution)/shard_map/ppermute | solution.py:314
  76.2 24.5 %all-to-all-start.2 = ((bf16[64,4,8,128]{3,2,1,0:T(8,128)(2,1)}), bf16[64,4,8,128]{3,2,1,0:T(8,128)(2,1)S(1)}, u32[]{:S(2)}, u32[]{:S(2)}) async-start(bf16[64,4,8,128]{3,2,1,0:T(8,128)(2,1)} %collective-permute-done), calls=%async_computation.2 | async-start | bytes 1048576 | tf_op jit(solution)/shard_map/all_to_all | solution.py:294
  83.4 16.0 %collective-permute-start.2 = (bf16[64,4,8,128]{3,2,1,0:T(8,128)(2,1)S(1)}, bf16[64,4,8,128]{3,2,1,0:T(8,128)(2,1)S(1)}, u32[]{:S(2)}, u32[]{:S(2)}) collective-permute-start(bf16[64,4,8,128]{3,2,1,0:T(8,128)(2,1)S(1)} %all-to-all-done.1), channel_id=1, source_target_pairs={{0,64},{64,128},{128,192},{192,0},{1,65},{65,129},{129,193},{193,1... | collective-permute-start | bytes 1572872 | tf_op jit(solution)/shard_map/ppermute | solution.py:314
  86.5 12.9 %collective-permute-start.3 = (bf16[64,4,8,128]{3,2,1,0:T(8,128)(2,1)S(1)}, bf16[64,4,8,128]{3,2,1,0:T(8,128)(2,1)S(1)}, u32[]{:S(2)}, u32[]{:S(2)}) collective-permute-start(bf16[64,4,8,128]{3,2,1,0:T(8,128)(2,1)S(1)} %all-to-all-done.1), channel_id=1, source_target_pairs={{0,192},{64,0},{128,64},{192,128},{1,193},{65,1},{129,65},{193,129... | collective-permute-start | bytes 1572872 | tf_op jit(solution)/shard_map/ppermute | solution.py:314

commit v10 on v9

--- a/solution.py
+++ b/solution.py
@@ -312,7 +312,7 @@
     for distance in range(1, windows):
         step = [(w, (w + distance) % windows) for w in range(windows)]
         b.append(lax.ppermute(second, "win", step))
-    win = settle(win, b[windows // 2 : windows // 2 + 1])
+    win = settle(win, b[1:2] + b[-1:])
     a = exchange(first).reshape(pieces)
     return correlate(win, a, [x.reshape(pieces) for x in b], table)
 

time: 113 us -> 115 us (1.018)
  waiting for transfers between devices: 37 us -> 39.9 us
    ppermute x3, starting transfers between devices: 7.27 us -> 4.19 us  [local(): b.append(lax.ppermute(second, 'win', step))]
    all_to_all x3, starting transfers between devices: 26.4 us -> 29 us  [local(): lax.all_to_all(x, 'pair', split_axis=0, concat_axis=0, tiled=True)]
    ppermute x3, waiting for transfers between devices: 11.1 us -> 12.8 us  [local(): b.append(lax.ppermute(second, 'win', step))]
    all_to_all x3, waiting for transfers between devices: 17.6 us -> 18.8 us  [local(): lax.all_to_all(x, 'pair', split_axis=0, concat_axis=0, tiled=True)]
  transfers between devices with their start and end apart: 7 -> 7, of which waited for: 6 -> 6; matrix products, arithmetic and copies ran while one was open for 18% -> 17% of each run, Pallas kernels for 1% -> 1%
where the time goes in v10:
time: 115 us; the launch traced here: 114 us
  waiting for transfers between devices  39.9 us (35%)
  starting transfers between devices  36.4 us (32%)
  other arithmetic  19.8 us (17%)
  Pallas kernels  18 us (16%)
    all_to_all x3, starting transfers between devices, local(): lax.all_to_all(x, 'pair', split_axis=0, concat_axis=0, tiled=True)  29 us
    all_to_all x3, waiting for transfers between devices, local(): lax.all_to_all(x, 'pair', split_axis=0, concat_axis=0, tiled=True)  18.8 us
    another operation x1, other arithmetic  17.4 us
    ppermute x3, waiting for transfers between devices, local(): b.append(lax.ppermute(second, 'win', step))  12.8 us
    pallas_call x1, Pallas kernels, correlate(): pl.pallas_call(functools.partial(correlate_kernel, scaling), grid=(tiles...  11.1 us
    ppermute x1, waiting for transfers between devices, local(): first = lax.ppermute(first, ('win', 'pair'), turn)  8.29 us
    ppermute x3, starting transfers between devices, local(): b.append(lax.ppermute(second, 'win', step))  4.19 us
    ppermute x1, starting transfers between devices, local(): first = lax.ppermute(first, ('win', 'pair'), turn)  3.21 us
  transfers between devices with their start and end apart: 7, of which 6 were waited for; matrix products, arithmetic and copies ran while one was open for 17% of the time, Pallas kernels for 1%

profile of v10, /device:TPU:1, one launch (start us, length us, event | category | flops | bytes accessed | tf_op | source)
XLA Modules:
  0.0 114.4 jit_solution(3729712223993361113)
XLA Ops:
  0.0 2.7 %whiten_spread.1 = bf16[2,8,4,9,8,128]{5,4,3,2,1,0:T(8,128)(2,1)} custom-call(s32[1]{0:T(128)} %bitcast.win_ref, bf16[8,1,2,32,1024]{4,3,2,1,0:T(8,128)(2,1)} %x_ref.1, s32[2,64]{1,0:T(2,128)} %bitcast.17, s32[2,4]{1,0:T(2,128)} %bitcast.18), custom_call_target="tpu_custom_call" | custom-call | tf_op jit(solution)/shard_map/whiten_spread/pallas_call | solution.py:65
  2.7 13.0 %all-to-all-start = ((bf16[64,9,8,128]{3,2,1,0:T(8,128)(2,1)}), bf16[64,9,8,128]{3,2,1,0:T(8,128)(2,1)S(1)}, u32[]{:S(2)}, u32[]{:S(2)}) async-start(bf16[64,9,8,128]{3,2,1,0:T(8,128)(2,1)} %bitcast.16), calls=%async_computation | async-start | bytes 2359296 | tf_op jit(solution)/shard_map/all_to_all | solution.py:294
  15.7 17.4 %cosine_convert_fusion = (bf16[1024,1024]{1,0:T(8,128)(2,1)S(1)}, bf16[1024,1024]{1,0:T(8,128)(2,1)S(1)}) fusion(s32[1024]{0:T(1024)S(1)} %get-tuple-element.19, s32[1024]{0:T(1024)S(1)} %get-tuple-element.20), kind=kLoop, calls=%fused_computation.10 | loop fusion | flops 17825792 | bytes 4202496 | tf_op jit(solution)/shard_map/convert
  33.2 2.4 %pad_maximum_fusion.refs_4_ = bf16[2048,1024]{1,0:T(8,128)(2,1)} fusion(bf16[1024,1024]{1,0:T(8,128)(2,1)S(1)} %get-tuple-element.18, bf16[1024,1024]{1,0:T(8,128)(2,1)S(1)} %get-tuple-element.17), kind=kLoop, calls=%fused_computation.8 | loop fusion | flops 8388608 | bytes 8388608 | tf_op jit(solution)/shard_map/concatenate | solution.py:286
  35.6 11.5 %all-to-all-done.x_ref = bf16[64,9,8,128]{3,2,1,0:T(8,128)(2,1)S(1)} async-done(((bf16[64,9,8,128]{3,2,1,0:T(8,128)(2,1)}), bf16[64,9,8,128]{3,2,1,0:T(8,128)(2,1)S(1)}, u32[]{:S(2)}, u32[]{:S(2)}) %all-to-all-start) | async-done | bytes 1179680 | tf_op jit(solution)/shard_map/all_to_all | solution.py:294
  47.1 2.6 %pick_second.1 = (bf16[64,4,8,128]{3,2,1,0:T(8,128)(2,1)}, s32[8,128]{1,0:T(8,128)S(1)}) custom-call(bf16[64,9,8,128]{3,2,1,0:T(8,128)(2,1)S(1)} %all-to-all-done.x_ref), custom_call_target="tpu_custom_call" | custom-call | tf_op jit(solution)/shard_map/pick_second/pallas_call | solution.py:121
  49.8 6.2 %all-to-all-start.1 = ((bf16[64,4,8,128]{3,2,1,0:T(8,128)(2,1)}), bf16[64,4,8,128]{3,2,1,0:T(8,128)(2,1)S(1)}, u32[]{:S(2)}, u32[]{:S(2)}) async-start(bf16[64,4,8,128]{3,2,1,0:T(8,128)(2,1)} %get-tuple-element.12), calls=%async_computation.1 | async-start | bytes 1048576 | tf_op jit(solution)/shard_map/all_to_all | solution.py:294
  56.0 1.0 pick_first.1
  57.0 3.2 %collective-permute-start = (bf16[64,4,8,128]{3,2,1,0:T(8,128)(2,1)S(1)}, bf16[64,4,8,128]{3,2,1,0:T(8,128)(2,1)}, u32[]{:S(2)}, u32[]{:S(2)}) collective-permute-start(bf16[64,4,8,128]{3,2,1,0:T(8,128)(2,1)S(1)} %pick_first.1), channel_id=1, source_target_pairs={{0,0},{1,65},{2,130},{3,195},{4,4},{5,69},{6,134},{7,199},{8,8},{9... | collective-permute-start | bytes 1572872 | tf_op jit(solution)/shard_map/ppermute | solution.py:308
  60.2 8.3 %collective-permute-done = bf16[64,4,8,128]{3,2,1,0:T(8,128)(2,1)} collective-permute-done((bf16[64,4,8,128]{3,2,1,0:T(8,128)(2,1)S(1)}, bf16[64,4,8,128]{3,2,1,0:T(8,128)(2,1)}, u32[]{:S(2)}, u32[]{:S(2)}) %collective-permute-start) | collective-permute-done | bytes 524320 | tf_op jit(solution)/shard_map/ppermute | solution.py:308
  68.5 4.8 %all-to-all-done.1 = bf16[64,4,8,128]{3,2,1,0:T(8,128)(2,1)S(1)} async-done(((bf16[64,4,8,128]{3,2,1,0:T(8,128)(2,1)}), bf16[64,4,8,128]{3,2,1,0:T(8,128)(2,1)S(1)}, u32[]{:S(2)}, u32[]{:S(2)}) %all-to-all-start.1) | async-done | bytes 524320 | tf_op jit(solution)/shard_map/all_to_all | solution.py:294
  73.3 1.3 %collective-permute-start.1 = (bf16[64,4,8,128]{3,2,1,0:T(8,128)(2,1)S(1)}, bf16[64,4,8,128]{3,2,1,0:T(8,128)(2,1)S(1)}, u32[]{:S(2)}, u32[]{:S(2)}) collective-permute-start(bf16[64,4,8,128]{3,2,1,0:T(8,128)(2,1)S(1)} %all-to-all-done.1), channel_id=1, source_target_pairs={{0,64},{64,128},{128,192},{192,0},{1,65},{65,129},{129,193},{193,1... | collective-permute-start | bytes 1572872 | tf_op jit(solution)/shard_map/ppermute | solution.py:314
  74.6 1.4 %collective-permute-start.2 = (bf16[64,4,8,128]{3,2,1,0:T(8,128)(2,1)S(1)}, bf16[64,4,8,128]{3,2,1,0:T(8,128)(2,1)S(1)}, u32[]{:S(2)}, u32[]{:S(2)}) collective-permute-start(bf16[64,4,8,128]{3,2,1,0:T(8,128)(2,1)S(1)} %all-to-all-done.1), channel_id=1, source_target_pairs={{0,192},{64,0},{128,64},{192,128},{1,193},{65,1},{129,65},{193,129... | collective-permute-start | bytes 1572872 | tf_op jit(solution)/shard_map/ppermute | solution.py:314
  76.0 9.8 %all-to-all-start.2 = ((bf16[64,4,8,128]{3,2,1,0:T(8,128)(2,1)}), bf16[64,4,8,128]{3,2,1,0:T(8,128)(2,1)S(1)}, u32[]{:S(2)}, u32[]{:S(2)}) async-start(bf16[64,4,8,128]{3,2,1,0:T(8,128)(2,1)} %collective-permute-done), calls=%async_computation.2 | async-start | bytes 1048576 | tf_op jit(solution)/shard_map/all_to_all | solution.py:294
  85.8 1.4 %collective-permute-start.3 = (bf16[64,4,8,128]{3,2,1,0:T(8,128)(2,1)S(1)}, bf16[64,4,8,128]{3,2,1,0:T(8,128)(2,1)S(1)}, u32[]{:S(2)}, u32[]{:S(2)}) collective-permute-start(bf16[64,4,8,128]{3,2,1,0:T(8,128)(2,1)S(1)} %all-to-all-done.1), channel_id=1, source_target_pairs={{0,128},{64,192},{128,0},{192,64},{1,129},{65,193},{129,1},{193,65... | collective-permute-start | bytes 1572872 | tf_op jit(solution)/shard_map/ppermute | solution.py:314
  87.3 0.6 collective-permute-done.1.refs_0_
  87.8 0.0 collective-permute-done.2.refs_1_
  87.8 0.5 settle.1.win_ref
  88.4 12.3 %collective-permute-done.3 = bf16[64,4,8,128]{3,2,1,0:T(8,128)(2,1)S(1)} collective-permute-done((bf16[64,4,8,128]{3,2,1,0:T(8,128)(2,1)S(1)}, bf16[64,4,8,128]{3,2,1,0:T(8,128)(2,1)S(1)}, u32[]{:S(2)}, u32[]{:S(2)}) %collective-permute-start.3) | collective-permute-done | bytes 524320 | tf_op jit(solution)/shard_map/ppermute | solution.py:314
  100.6 2.5 %all-to-all-done.2 = bf16[64,4,8,128]{3,2,1,0:T(8,128)(2,1)S(1)} async-done(((bf16[64,4,8,128]{3,2,1,0:T(8,128)(2,1)}), bf16[64,4,8,128]{3,2,1,0:T(8,128)(2,1)S(1)}, u32[]{:S(2)}, u32[]{:S(2)}) %all-to-all-start.2) | async-done | bytes 524320 | tf_op jit(solution)/shard_map/all_to_all | solution.py:294
  103.1 11.1 %correlate.1 = bf16[8,4,32,1024]{3,2,1,0:T(8,128)(2,1)} custom-call(s32[1]{0:T(128)} %settle.1.win_ref, bf16[2,8,4,4,8,128]{5,4,3,2,1,0:T(8,128)(2,1)S(1)} %bitcast.12, bf16[2,8,4,4,8,128]{5,4,3,2,1,0:T(8,128)(2,1)S(1)} %bitcast.11, bf16[2,8,4,4,8,128]{5,4,3,2,1,0:T(8,128)(2,1)S(1)} %bitcast.13, bf16[2,8,4,4,8,128]{5,4,3,2,1,0:T(8,128)(2,1)S(1)} %bitcast.15, ...), custom_call_target="tpu_custom_call" | custom-call | tf_op jit(solution)/shard_map/correlate/pallas_call | solution.py:244
  (1 shorter events, 0.0 us)
Async XLA Ops:
  2.7 44.4 %all-to-all-start = ((bf16[64,9,8,128]{3,2,1,0:T(8,128)(2,1)}), bf16[64,9,8,128]{3,2,1,0:T(8,128)(2,1)S(1)}, u32[]{:S(2)}, u32[]{:S(2)}) async-start(bf16[64,9,8,128]{3,2,1,0:T(8,128)(2,1)} %bitcast.16), calls=%async_computation | async-start | bytes 2359296 | tf_op jit(solution)/shard_map/all_to_all | solution.py:294
  49.8 23.5 %all-to-all-start.1 = ((bf16[64,4,8,128]{3,2,1,0:T(8,128)(2,1)}), bf16[64,4,8,128]{3,2,1,0:T(8,128)(2,1)S(1)}, u32[]{:S(2)}, u32[]{:S(2)}) async-start(bf16[64,4,8,128]{3,2,1,0:T(8,128)(2,1)} %get-tuple-element.12), calls=%async_computation.1 | async-start | bytes 1048576 | tf_op jit(solution)/shard_map/all_to_all | solution.py:294
  57.0 11.5 %collective-permute-start = (bf16[64,4,8,128]{3,2,1,0:T(8,128)(2,1)S(1)}, bf16[64,4,8,128]{3,2,1,0:T(8,128)(2,1)}, u32[]{:S(2)}, u32[]{:S(2)}) collective-permute-start(bf16[64,4,8,128]{3,2,1,0:T(8,128)(2,1)S(1)} %pick_first.1), channel_id=1, source_target_pairs={{0,0},{1,65},{2,130},{3,195},{4,4},{5,69},{6,134},{7,199},{8,8},{9... | collective-permute-start | bytes 1572872 | tf_op jit(solution)/shard_map/ppermute | solution.py:308
  73.3 14.5 %collective-permute-start.1 = (bf16[64,4,8,128]{3,2,1,0:T(8,128)(2,1)S(1)}, bf16[64,4,8,128]{3,2,1,0:T(8,128)(2,1)S(1)}, u32[]{:S(2)}, u32[]{:S(2)}) collective-permute-start(bf16[64,4,8,128]{3,2,1,0:T(8,128)(2,1)S(1)} %all-to-all-done.1), channel_id=1, source_target_pairs={{0,64},{64,128},{128,192},{192,0},{1,65},{65,129},{129,193},{193,1... | collective-permute-start | bytes 1572872 | tf_op jit(solution)/shard_map/ppermute | solution.py:314
  74.6 13.2 %collective-permute-start.2 = (bf16[64,4,8,128]{3,2,1,0:T(8,128)(2,1)S(1)}, bf16[64,4,8,128]{3,2,1,0:T(8,128)(2,1)S(1)}, u32[]{:S(2)}, u32[]{:S(2)}) collective-permute-start(bf16[64,4,8,128]{3,2,1,0:T(8,128)(2,1)S(1)} %all-to-all-done.1), channel_id=1, source_target_pairs={{0,192},{64,0},{128,64},{192,128},{1,193},{65,1},{129,65},{193,129... | collective-permute-start | bytes 1572872 | tf_op jit(solution)/shard_map/ppermute | solution.py:314
  76.0 27.1 %all-to-all-start.2 = ((bf16[64,4,8,128]{3,2,1,0:T(8,128)(2,1)}), bf16[64,4,8,128]{3,2,1,0:T(8,128)(2,1)S(1)}, u32[]{:S(2)}, u32[]{:S(2)}) async-start(bf16[64,4,8,128]{3,2,1,0:T(8,128)(2,1)} %collective-permute-done), calls=%async_computation.2 | async-start | bytes 1048576 | tf_op jit(solution)/shard_map/all_to_all | solution.py:294
  85.8 14.8 %collective-permute-start.3 = (bf16[64,4,8,128]{3,2,1,0:T(8,128)(2,1)S(1)}, bf16[64,4,8,128]{3,2,1,0:T(8,128)(2,1)S(1)}, u32[]{:S(2)}, u32[]{:S(2)}) collective-permute-start(bf16[64,4,8,128]{3,2,1,0:T(8,128)(2,1)S(1)} %all-to-all-done.1), channel_id=1, source_target_pairs={{0,128},{64,192},{128,0},{192,64},{1,129},{65,193},{129,1},{193,65... | collective-permute-start | bytes 1572872 | tf_op jit(solution)/shard_map/ppermute | solution.py:314

commit v11 on v9

--- a/solution.py
+++ b/solution.py
@@ -154,9 +154,8 @@
 def correlate_kernel(scaling, win_ref, a_ref, *refs):
     windows = a_ref.shape[2]
     b_refs, table_hbm = refs[:windows], refs[windows]
-    out_ref, stack_ref, table_ref, sem = refs[windows + 1 :]
-    step = pl.program_id(0)
-    last = pl.num_programs(0) - 1
+    out_hbm, stack_ref, table_ref, panel_ref, sem, out_sems = refs[windows + 1 :]
+    tiles = last = a_ref.shape[3]
     _, lane_groups, groups = b_refs[0].shape[:3]
     bins = lane_groups * LANES
     channels = groups * GROUP
@@ -166,7 +165,11 @@
     ]
     table_copy = pltpu.make_async_copy(table_hbm, table_ref, sem)
 
-    def cross(lane_group, slot):
+    def out_copy(tile):
+        slot = lax.rem(tile, 2)
+        return pltpu.make_async_copy(panel_ref.at[slot], out_hbm.at[:, tile], out_sems.at[slot])
+
+    def cross(step, lane_group, slot):
         lanes = lane_group * LANES
         a = [
             [a_ref[part, lane_group, w, step].astype(jnp.float32) for part in range(2)]
@@ -209,29 +212,44 @@
         columns = pl.ds(chunk * 2 * LANES, 2 * LANES)
         rows = jnp.dot(stack_ref[slot], table_ref[:, columns], preferred_element_type=jnp.float32)
         rows = (rows * scaling).astype(jnp.bfloat16)
-        out_ref[:, 0, :, columns] = rows.reshape(GROUP, channels, 2 * LANES)
-
-    def run(with_cross, with_lagged):
+        panel_ref[slot, :, :, columns] = rows.reshape(GROUP, channels, 2 * LANES)
+
+    def run(step, with_cross, with_lagged):
         for chunk in range(lane_groups // 2):
             if with_lagged:
                 lagged(chunk, lax.rem(step + 1, 2))
             if with_cross:
-                cross(chunk * 2, lax.rem(step, 2))
-                cross(chunk * 2 + 1, lax.rem(step, 2))
-
-    @pl.when(step == 0)
-    def _():
-        table_copy.start()
-        run(True, False)
-        table_copy.wait()
-
-    @pl.when(jnp.logical_and(step > 0, step < last))
-    def _():
-        run(True, True)
-
-    @pl.when(step == last)
-    def _():
-        run(False, True)
+                cross(step, chunk * 2, lax.rem(step, 2))
+                cross(step, chunk * 2 + 1, lax.rem(step, 2))
+
+    def one_step(step, carry):
+        @pl.when(step > 2)
+        def _():
+            out_copy(step - 3).wait()
+
+        @pl.when(step == 0)
+        def _():
+            table_copy.start()
+            run(step, True, False)
+            table_copy.wait()
+
+        @pl.when(jnp.logical_and(step > 0, step < last))
+        def _():
+            run(step, True, True)
+
+        @pl.when(step == last)
+        def _():
+            run(step, False, True)
+
+        @pl.when(step > 0)
+        def _():
+            out_copy(step - 1).start()
+
+        return carry
+
+    lax.fori_loop(0, tiles + 1, one_step, 0)
+    for tile in range(max(tiles - 2, 0), tiles):
+        out_copy(tile).wait()
 
 
 def correlate(win, a, b, table):
@@ -240,21 +258,19 @@
     bins = lane_groups * LANES
     lags = table.shape[1]
     scaling = 1.0 / math.sqrt(windows * bins)
-    whole = lambda x: pl.BlockSpec(x.shape, lambda t: (0,) * len(x.shape))
     return pl.pallas_call(
         functools.partial(correlate_kernel, scaling),
-        grid=(tiles + 1,),
         in_specs=[pl.BlockSpec(memory_space=pltpu.SMEM)]
-        + [whole(x) for x in (a, *b)]
+        + [pl.BlockSpec(memory_space=pltpu.VMEM)] * (1 + len(b))
         + [pl.BlockSpec(memory_space=pltpu.HBM)],
-        out_specs=pl.BlockSpec(
-            (GROUP, 1, channels, lags), lambda t: (0, jnp.maximum(t - 1, 0), 0, 0)
-        ),
+        out_specs=pl.BlockSpec(memory_space=pltpu.HBM),
         out_shape=jax.ShapeDtypeStruct((GROUP, tiles, channels, lags), jnp.bfloat16),
         scratch_shapes=[
             pltpu.VMEM((2, GROUP * channels, 2 * bins), jnp.bfloat16),
             pltpu.VMEM(table.shape, table.dtype),
+            pltpu.VMEM((2, GROUP, channels, lags), jnp.bfloat16),
             pltpu.SemaphoreType.DMA,
+            pltpu.SemaphoreType.DMA((2,)),
         ],
         compiler_params=pltpu.CompilerParams(vmem_limit_bytes=48 * 2**20),
         name="correlate",

time: 113 us -> 113 us (level)
  no operation moved by 1% of the time
where the time goes in v11:
time: 113 us; the launch traced here: 112 us
  waiting for transfers between devices  37 us (33%)
  starting transfers between devices  36.9 us (33%)
  other arithmetic  19.8 us (18%)
  Pallas kernels  17.9 us (16%)
    all_to_all x3, starting transfers between devices, local(): lax.all_to_all(x, 'pair', split_axis=0, concat_axis=0, tiled=True)  26.4 us
    all_to_all x3, waiting for transfers between devices, local(): lax.all_to_all(x, 'pair', split_axis=0, concat_axis=0, tiled=True)  17.6 us
    another operation x1, other arithmetic  17.4 us
    ppermute x3, waiting for transfers between devices, local(): b.append(lax.ppermute(second, 'win', step))  11.1 us
    pallas_call x1, Pallas kernels, correlate(): pl.pallas_call(functools.partial(correlate_kernel, scaling), in_specs=[pl...  11 us
    ppermute x1, waiting for transfers between devices, local(): first = lax.ppermute(first, ('win', 'pair'), turn)  8.29 us
    ppermute x3, starting transfers between devices, local(): b.append(lax.ppermute(second, 'win', step))  7.27 us
    ppermute x1, starting transfers between devices, local(): first = lax.ppermute(first, ('win', 'pair'), turn)  3.21 us
  transfers between devices with their start and end apart: 7, of which 6 were waited for; matrix products, arithmetic and copies ran while one was open for 18% of the time, Pallas kernels for 1%

profile of v11, /device:TPU:1, one launch (start us, length us, event | category | flops | bytes accessed | tf_op | source)
XLA Modules:
  0.0 111.9 jit_solution(2082008930530955902)
XLA Ops:
  0.0 2.7 %whiten_spread.1 = bf16[2,8,4,9,8,128]{5,4,3,2,1,0:T(8,128)(2,1)} custom-call(s32[1]{0:T(128)} %bitcast.win_ref, bf16[8,1,2,32,1024]{4,3,2,1,0:T(8,128)(2,1)} %x_ref.1, s32[2,64]{1,0:T(2,128)} %bitcast.17, s32[2,4]{1,0:T(2,128)} %bitcast.18), custom_call_target="tpu_custom_call" | custom-call | tf_op jit(solution)/shard_map/whiten_spread/pallas_call | solution.py:65
  2.7 13.0 %all-to-all-start = ((bf16[64,9,8,128]{3,2,1,0:T(8,128)(2,1)}), bf16[64,9,8,128]{3,2,1,0:T(8,128)(2,1)S(1)}, u32[]{:S(2)}, u32[]{:S(2)}) async-start(bf16[64,9,8,128]{3,2,1,0:T(8,128)(2,1)} %bitcast.16), calls=%async_computation | async-start | bytes 2359296 | tf_op jit(solution)/shard_map/all_to_all | solution.py:310
  15.7 17.4 %cosine_convert_fusion = (bf16[1024,1024]{1,0:T(8,128)(2,1)S(1)}, bf16[1024,1024]{1,0:T(8,128)(2,1)S(1)}) fusion(s32[1024]{0:T(1024)S(1)} %get-tuple-element.19, s32[1024]{0:T(1024)S(1)} %get-tuple-element.20), kind=kLoop, calls=%fused_computation.10 | loop fusion | flops 17825792 | bytes 4202496 | tf_op jit(solution)/shard_map/convert
  33.2 2.4 %pad_maximum_fusion.refs_4_ = bf16[2048,1024]{1,0:T(8,128)(2,1)} fusion(bf16[1024,1024]{1,0:T(8,128)(2,1)S(1)} %get-tuple-element.18, bf16[1024,1024]{1,0:T(8,128)(2,1)S(1)} %get-tuple-element.17), kind=kLoop, calls=%fused_computation.8 | loop fusion | flops 8388608 | bytes 8388608 | tf_op jit(solution)/shard_map/concatenate | solution.py:302
  35.6 11.5 %all-to-all-done.x_ref = bf16[64,9,8,128]{3,2,1,0:T(8,128)(2,1)S(1)} async-done(((bf16[64,9,8,128]{3,2,1,0:T(8,128)(2,1)}), bf16[64,9,8,128]{3,2,1,0:T(8,128)(2,1)S(1)}, u32[]{:S(2)}, u32[]{:S(2)}) %all-to-all-start) | async-done | bytes 1179680 | tf_op jit(solution)/shard_map/all_to_all | solution.py:310
  47.1 2.6 %pick_second.1 = (bf16[64,4,8,128]{3,2,1,0:T(8,128)(2,1)}, s32[8,128]{1,0:T(8,128)S(1)}) custom-call(bf16[64,9,8,128]{3,2,1,0:T(8,128)(2,1)S(1)} %all-to-all-done.x_ref), custom_call_target="tpu_custom_call" | custom-call | tf_op jit(solution)/shard_map/pick_second/pallas_call | solution.py:121
  49.8 6.2 %all-to-all-start.1 = ((bf16[64,4,8,128]{3,2,1,0:T(8,128)(2,1)}), bf16[64,4,8,128]{3,2,1,0:T(8,128)(2,1)S(1)}, u32[]{:S(2)}, u32[]{:S(2)}) async-start(bf16[64,4,8,128]{3,2,1,0:T(8,128)(2,1)} %get-tuple-element.12), calls=%async_computation.1 | async-start | bytes 1048576 | tf_op jit(solution)/shard_map/all_to_all | solution.py:310
  56.0 1.0 pick_first.1
  57.0 3.2 %collective-permute-start = (bf16[64,4,8,128]{3,2,1,0:T(8,128)(2,1)S(1)}, bf16[64,4,8,128]{3,2,1,0:T(8,128)(2,1)}, u32[]{:S(2)}, u32[]{:S(2)}) collective-permute-start(bf16[64,4,8,128]{3,2,1,0:T(8,128)(2,1)S(1)} %pick_first.1), channel_id=1, source_target_pairs={{0,0},{1,65},{2,130},{3,195},{4,4},{5,69},{6,134},{7,199},{8,8},{9... | collective-permute-start | bytes 1572872 | tf_op jit(solution)/shard_map/ppermute | solution.py:324
  60.2 8.3 %collective-permute-done = bf16[64,4,8,128]{3,2,1,0:T(8,128)(2,1)} collective-permute-done((bf16[64,4,8,128]{3,2,1,0:T(8,128)(2,1)S(1)}, bf16[64,4,8,128]{3,2,1,0:T(8,128)(2,1)}, u32[]{:S(2)}, u32[]{:S(2)}) %collective-permute-start) | collective-permute-done | bytes 524320 | tf_op jit(solution)/shard_map/ppermute | solution.py:324
  68.5 4.8 %all-to-all-done.1 = bf16[64,4,8,128]{3,2,1,0:T(8,128)(2,1)S(1)} async-done(((bf16[64,4,8,128]{3,2,1,0:T(8,128)(2,1)}), bf16[64,4,8,128]{3,2,1,0:T(8,128)(2,1)S(1)}, u32[]{:S(2)}, u32[]{:S(2)}) %all-to-all-start.1) | async-done | bytes 524320 | tf_op jit(solution)/shard_map/all_to_all | solution.py:310
  73.3 2.9 %collective-permute-start.1 = (bf16[64,4,8,128]{3,2,1,0:T(8,128)(2,1)S(1)}, bf16[64,4,8,128]{3,2,1,0:T(8,128)(2,1)S(1)}, u32[]{:S(2)}, u32[]{:S(2)}) collective-permute-start(bf16[64,4,8,128]{3,2,1,0:T(8,128)(2,1)S(1)} %all-to-all-done.1), channel_id=1, source_target_pairs={{0,128},{64,192},{128,0},{192,64},{1,129},{65,193},{129,1},{193,65... | collective-permute-start | bytes 1572872 | tf_op jit(solution)/shard_map/ppermute | solution.py:330
  76.2 7.2 %all-to-all-start.2 = ((bf16[64,4,8,128]{3,2,1,0:T(8,128)(2,1)}), bf16[64,4,8,128]{3,2,1,0:T(8,128)(2,1)S(1)}, u32[]{:S(2)}, u32[]{:S(2)}) async-start(bf16[64,4,8,128]{3,2,1,0:T(8,128)(2,1)} %collective-permute-done), calls=%async_computation.2 | async-start | bytes 1048576 | tf_op jit(solution)/shard_map/all_to_all | solution.py:310
  83.4 3.0 %collective-permute-start.2 = (bf16[64,4,8,128]{3,2,1,0:T(8,128)(2,1)S(1)}, bf16[64,4,8,128]{3,2,1,0:T(8,128)(2,1)S(1)}, u32[]{:S(2)}, u32[]{:S(2)}) collective-permute-start(bf16[64,4,8,128]{3,2,1,0:T(8,128)(2,1)S(1)} %all-to-all-done.1), channel_id=1, source_target_pairs={{0,64},{64,128},{128,192},{192,0},{1,65},{65,129},{129,193},{193,1... | collective-permute-start | bytes 1572872 | tf_op jit(solution)/shard_map/ppermute | solution.py:330
  86.5 1.3 %collective-permute-start.3 = (bf16[64,4,8,128]{3,2,1,0:T(8,128)(2,1)S(1)}, bf16[64,4,8,128]{3,2,1,0:T(8,128)(2,1)S(1)}, u32[]{:S(2)}, u32[]{:S(2)}) collective-permute-start(bf16[64,4,8,128]{3,2,1,0:T(8,128)(2,1)S(1)} %all-to-all-done.1), channel_id=1, source_target_pairs={{0,192},{64,0},{128,64},{192,128},{1,193},{65,1},{129,65},{193,129... | collective-permute-start | bytes 1572872 | tf_op jit(solution)/shard_map/ppermute | solution.py:330
  87.8 0.2 collective-permute-done.1.refs_0_
  88.0 0.5 settle.1.win_ref
  88.5 10.9 %collective-permute-done.2 = bf16[64,4,8,128]{3,2,1,0:T(8,128)(2,1)S(1)} collective-permute-done((bf16[64,4,8,128]{3,2,1,0:T(8,128)(2,1)S(1)}, bf16[64,4,8,128]{3,2,1,0:T(8,128)(2,1)S(1)}, u32[]{:S(2)}, u32[]{:S(2)}) %collective-permute-start.2) | collective-permute-done | bytes 524320 | tf_op jit(solution)/shard_map/ppermute | solution.py:330
  99.4 0.0 collective-permute-done.3
  99.4 1.3 %all-to-all-done.2 = bf16[64,4,8,128]{3,2,1,0:T(8,128)(2,1)S(1)} async-done(((bf16[64,4,8,128]{3,2,1,0:T(8,128)(2,1)}), bf16[64,4,8,128]{3,2,1,0:T(8,128)(2,1)S(1)}, u32[]{:S(2)}, u32[]{:S(2)}) %all-to-all-start.2) | async-done | bytes 524320 | tf_op jit(solution)/shard_map/all_to_all | solution.py:310
  100.7 11.0 %correlate.1 = bf16[8,4,32,1024]{3,2,1,0:T(8,128)(2,1)} custom-call(s32[1]{0:T(128)} %settle.1.win_ref, bf16[2,8,4,4,8,128]{5,4,3,2,1,0:T(8,128)(2,1)S(1)} %bitcast.12, bf16[2,8,4,4,8,128]{5,4,3,2,1,0:T(8,128)(2,1)S(1)} %bitcast.11, bf16[2,8,4,4,8,128]{5,4,3,2,1,0:T(8,128)(2,1)S(1)} %bitcast.14, bf16[2,8,4,4,8,128]{5,4,3,2,1,0:T(8,128)(2,1)S(1)} %bitcast.13, ...), custom_call_target="tpu_custom_call" | custom-call | tf_op jit(solution)/shard_map/correlate/pallas_call | solution.py:261
  (1 shorter events, 0.0 us)
Async XLA Ops:
  2.7 44.4 %all-to-all-start = ((bf16[64,9,8,128]{3,2,1,0:T(8,128)(2,1)}), bf16[64,9,8,128]{3,2,1,0:T(8,128)(2,1)S(1)}, u32[]{:S(2)}, u32[]{:S(2)}) async-start(bf16[64,9,8,128]{3,2,1,0:T(8,128)(2,1)} %bitcast.16), calls=%async_computation | async-start | bytes 2359296 | tf_op jit(solution)/shard_map/all_to_all | solution.py:310
  49.8 23.5 %all-to-all-start.1 = ((bf16[64,4,8,128]{3,2,1,0:T(8,128)(2,1)}), bf16[64,4,8,128]{3,2,1,0:T(8,128)(2,1)S(1)}, u32[]{:S(2)}, u32[]{:S(2)}) async-start(bf16[64,4,8,128]{3,2,1,0:T(8,128)(2,1)} %get-tuple-element.12), calls=%async_computation.1 | async-start | bytes 1048576 | tf_op jit(solution)/shard_map/all_to_all | solution.py:310
  57.0 11.5 %collective-permute-start = (bf16[64,4,8,128]{3,2,1,0:T(8,128)(2,1)S(1)}, bf16[64,4,8,128]{3,2,1,0:T(8,128)(2,1)}, u32[]{:S(2)}, u32[]{:S(2)}) collective-permute-start(bf16[64,4,8,128]{3,2,1,0:T(8,128)(2,1)S(1)} %pick_first.1), channel_id=1, source_target_pairs={{0,0},{1,65},{2,130},{3,195},{4,4},{5,69},{6,134},{7,199},{8,8},{9... | collective-permute-start | bytes 1572872 | tf_op jit(solution)/shard_map/ppermute | solution.py:324
  73.3 14.7 %collective-permute-start.1 = (bf16[64,4,8,128]{3,2,1,0:T(8,128)(2,1)S(1)}, bf16[64,4,8,128]{3,2,1,0:T(8,128)(2,1)S(1)}, u32[]{:S(2)}, u32[]{:S(2)}) collective-permute-start(bf16[64,4,8,128]{3,2,1,0:T(8,128)(2,1)S(1)} %all-to-all-done.1), channel_id=1, source_target_pairs={{0,128},{64,192},{128,0},{192,64},{1,129},{65,193},{129,1},{193,65... | collective-permute-start | bytes 1572872 | tf_op jit(solution)/shard_map/ppermute | solution.py:330
  76.2 24.5 %all-to-all-start.2 = ((bf16[64,4,8,128]{3,2,1,0:T(8,128)(2,1)}), bf16[64,4,8,128]{3,2,1,0:T(8,128)(2,1)S(1)}, u32[]{:S(2)}, u32[]{:S(2)}) async-start(bf16[64,4,8,128]{3,2,1,0:T(8,128)(2,1)} %collective-permute-done), calls=%async_computation.2 | async-start | bytes 1048576 | tf_op jit(solution)/shard_map/all_to_all | solution.py:310
  83.4 16.0 %collective-permute-start.2 = (bf16[64,4,8,128]{3,2,1,0:T(8,128)(2,1)S(1)}, bf16[64,4,8,128]{3,2,1,0:T(8,128)(2,1)S(1)}, u32[]{:S(2)}, u32[]{:S(2)}) collective-permute-start(bf16[64,4,8,128]{3,2,1,0:T(8,128)(2,1)S(1)} %all-to-all-done.1), channel_id=1, source_target_pairs={{0,64},{64,128},{128,192},{192,0},{1,65},{65,129},{129,193},{193,1... | collective-permute-start | bytes 1572872 | tf_op jit(solution)/shard_map/ppermute | solution.py:330
  86.5 12.9 %collective-permute-start.3 = (bf16[64,4,8,128]{3,2,1,0:T(8,128)(2,1)S(1)}, bf16[64,4,8,128]{3,2,1,0:T(8,128)(2,1)S(1)}, u32[]{:S(2)}, u32[]{:S(2)}) collective-permute-start(bf16[64,4,8,128]{3,2,1,0:T(8,128)(2,1)S(1)} %all-to-all-done.1), channel_id=1, source_target_pairs={{0,192},{64,0},{128,64},{192,128},{1,193},{65,1},{129,65},{193,129... | collective-permute-start | bytes 1572872 | tf_op jit(solution)/shard_map/ppermute | solution.py:330

commit v12 on v9

--- a/solution.py
+++ b/solution.py
@@ -279,11 +279,23 @@
 
 
 def lag_rows_table(bin_total):
-    bin_index = jnp.arange(bin_total, dtype=jnp.int32) + F0
+    fine = 16
     lag_index = jnp.arange(LAGS, dtype=jnp.int32) - LAGS // 2
-    wrapped = bin_index[:, None] * lag_index[None, :] % NS
-    phases = wrapped.astype(jnp.float32) * (2.0 * math.pi / NS)
-    return jnp.concatenate([jnp.cos(phases), -jnp.sin(phases)], axis=0).astype(jnp.bfloat16)
+
+    def turns(bins):
+        wrapped = bins[:, None] * lag_index[None, :] % NS
+        phases = wrapped.astype(jnp.float32) * (2.0 * math.pi / NS)
+        return jnp.cos(phases), jnp.sin(phases)
+
+    coarse_bins = jnp.arange(bin_total // fine, dtype=jnp.int32) * fine + F0
+    pairs = turns(jnp.concatenate([coarse_bins, jnp.arange(fine, dtype=jnp.int32)]))
+    cosine, sine = lax.optimization_barrier(pairs)
+    coarse = [x[:-fine, None, :] for x in (cosine, sine)]
+    small = [x[None, -fine:, :] for x in (cosine, sine)]
+    real = coarse[0] * small[0] - coarse[1] * small[1]
+    imag = coarse[1] * small[0] + coarse[0] * small[1]
+    table = jnp.stack([real, -imag]).astype(jnp.bfloat16)
+    return table.reshape(2 * bin_total, LAGS)
 
 
 def local(spectra, send_blocks, tile_slots):

time: 113 us -> 114 us (level)
  waiting for transfers between devices: 37 us -> 52.1 us
  other arithmetic: 19.8 us -> 5.62 us
    another operation x1 -> x2, other arithmetic: 17.4 us -> 4.19 us  [the longest x1 2.31 us: lag_rows_table(): table = jnp.stack([real, -imag]).astype(jnp.bfloat16)]
    all_to_all x3, waiting for transfers between devices: 17.6 us -> 30.4 us  [local(): lax.all_to_all(x, 'pair', split_axis=0, concat_axis=0, tiled=True)]
    concatenate x1, other arithmetic: 2.39 us -> 0.08 us  [lag_rows_table(): jnp.concatenate([coarse_bins, jnp.arange(fine, dtype=jnp.int32)])]
    ppermute x3, waiting for transfers between devices: 11.1 us -> 13.4 us  [local(): b.append(lax.ppermute(second, 'win', step))]
    sin x0 -> x1, other arithmetic: none -> 1.35 us  [turns(): return (jnp.cos(phases), jnp.sin(phases))]
  transfers between devices with their start and end apart: 7 -> 7, of which waited for: 6 -> 6; matrix products, arithmetic and copies ran while one was open for 18% -> 5% of each run, Pallas kernels for 1% -> 1%
where the time goes in v12:
time: 114 us; the launch traced here: 113 us
  waiting for transfers between devices  52.1 us (46%)
  starting transfers between devices  36.6 us (32%)
  Pallas kernels  18.1 us (16%)
  other arithmetic  5.62 us (5%)
    all_to_all x3, waiting for transfers between devices, local(): lax.all_to_all(x, 'pair', split_axis=0, concat_axis=0, tiled=True)  30.4 us
    all_to_all x3, starting transfers between devices, local(): lax.all_to_all(x, 'pair', split_axis=0, concat_axis=0, tiled=True)  26.4 us
    ppermute x3, waiting for transfers between devices, local(): b.append(lax.ppermute(second, 'win', step))  13.4 us
    pallas_call x1, Pallas kernels, correlate(): pl.pallas_call(functools.partial(correlate_kernel, scaling), grid=(tiles...  11.1 us
    ppermute x1, waiting for transfers between devices, local(): first = lax.ppermute(first, ('win', 'pair'), turn)  8.29 us
    ppermute x3, starting transfers between devices, local(): b.append(lax.ppermute(second, 'win', step))  7 us
    ppermute x1, starting transfers between devices, local(): first = lax.ppermute(first, ('win', 'pair'), turn)  3.21 us
    pallas_call x1, Pallas kernels, whiten_spread(): pl.pallas_call(whiten_kernel, grid=(steps,), in_specs=[pl.BlockSpec(memor...  2.75 us
  transfers between devices with their start and end apart: 7, of which 6 were waited for; matrix products, arithmetic and copies ran while one was open for 5% of the time, Pallas kernels for 1%

profile of v12, /device:TPU:1, one launch (start us, length us, event | category | flops | bytes accessed | tf_op | source)
XLA Modules:
  0.0 112.7 jit_solution(15068904686844067884)
XLA Ops:
  0.0 2.7 %whiten_spread.1 = bf16[2,8,4,9,8,128]{5,4,3,2,1,0:T(8,128)(2,1)} custom-call(s32[1]{0:T(128)} %bitcast.win_ref, bf16[8,1,2,32,1024]{4,3,2,1,0:T(8,128)(2,1)} %x_ref.1, s32[2,64]{1,0:T(2,128)} %bitcast.19, s32[2,4]{1,0:T(2,128)} %bitcast.20), custom_call_target="tpu_custom_call" | custom-call | tf_op jit(solution)/shard_map/whiten_spread/pallas_call | solution.py:65
  2.7 13.0 %all-to-all-start = ((bf16[64,9,8,128]{3,2,1,0:T(8,128)(2,1)}), bf16[64,9,8,128]{3,2,1,0:T(8,128)(2,1)S(1)}, u32[]{:S(2)}, u32[]{:S(2)}) async-start(bf16[64,9,8,128]{3,2,1,0:T(8,128)(2,1)} %bitcast.18), calls=%async_computation | async-start | bytes 2359296 | tf_op jit(solution)/shard_map/all_to_all | solution.py:306
  15.8 0.1 pad_add_fusion
  15.8 1.4 %fusion.3 = (f32[80,1024]{1,0:T(8,128)S(1)}, f32[80,1024]{1,0:T(8,128)S(1)}) fusion(s32[1024]{0:T(1024)S(1)} %iota_add_fusion, s32[80]{0:T(128)S(1)} %pad_add_fusion), kind=kLoop, calls=%fused_computation.11 | loop fusion | flops 1146880 | bytes 659776 | tf_op jit(solution)/shard_map/sin | solution.py:288
  17.3 1.9 %subtract_convert_fusion = (bf16[1,64,16,1024]{3,2,1,0:T(8,128)(2,1)S(1)}, bf16[1,64,16,1024]{3,2,1,0:T(8,128)(2,1)S(1)}) fusion(f32[16,1024]{1,0:T(8,128)S(1)} %slice.15, f32[64,1024]{1,0:T(8,128)S(1)} %slice.14, f32[16,1024]{1,0:T(8,128)S(1)} %slice.13, f32[64,1024]{1,0:T(8,128)S(1)} %slice.12), kind=kLoop, calls=%fused_computation.2 | loop fusion | flops 9437184 | bytes 4849664 | tf_op jit(solution)/shard_map/convert
  19.2 2.3 %pad_maximum_fusion = bf16[2,64,16,1024]{3,2,1,0:T(8,128)(2,1)} fusion(bf16[1,64,16,1024]{3,2,1,0:T(8,128)(2,1)S(1)} %get-tuple-element.22, bf16[1,64,16,1024]{3,2,1,0:T(8,128)(2,1)S(1)} %get-tuple-element.21), kind=kLoop, calls=%fused_computation | loop fusion | flops 2097152 | bytes 8388608 | tf_op jit(solution)/shard_map/stack | solution.py:297
  21.5 25.6 %all-to-all-done.x_ref = bf16[64,9,8,128]{3,2,1,0:T(8,128)(2,1)S(1)} async-done(((bf16[64,9,8,128]{3,2,1,0:T(8,128)(2,1)}), bf16[64,9,8,128]{3,2,1,0:T(8,128)(2,1)S(1)}, u32[]{:S(2)}, u32[]{:S(2)}) %all-to-all-start) | async-done | bytes 1179680 | tf_op jit(solution)/shard_map/all_to_all | solution.py:306
  47.1 2.6 %pick_second.1 = (bf16[64,4,8,128]{3,2,1,0:T(8,128)(2,1)}, s32[8,128]{1,0:T(8,128)S(1)}) custom-call(bf16[64,9,8,128]{3,2,1,0:T(8,128)(2,1)S(1)} %all-to-all-done.x_ref), custom_call_target="tpu_custom_call" | custom-call | tf_op jit(solution)/shard_map/pick_second/pallas_call | solution.py:121
  49.8 6.2 %all-to-all-start.1 = ((bf16[64,4,8,128]{3,2,1,0:T(8,128)(2,1)}), bf16[64,4,8,128]{3,2,1,0:T(8,128)(2,1)S(1)}, u32[]{:S(2)}, u32[]{:S(2)}) async-start(bf16[64,4,8,128]{3,2,1,0:T(8,128)(2,1)} %get-tuple-element.16), calls=%async_computation.1 | async-start | bytes 1048576 | tf_op jit(solution)/shard_map/all_to_all | solution.py:306
  56.0 1.0 pick_first.1
  57.0 3.2 %collective-permute-start = (bf16[64,4,8,128]{3,2,1,0:T(8,128)(2,1)S(1)}, bf16[64,4,8,128]{3,2,1,0:T(8,128)(2,1)}, u32[]{:S(2)}, u32[]{:S(2)}) collective-permute-start(bf16[64,4,8,128]{3,2,1,0:T(8,128)(2,1)S(1)} %pick_first.1), channel_id=1, source_target_pairs={{0,0},{1,65},{2,130},{3,195},{4,4},{5,69},{6,134},{7,199},{8,8},{9... | collective-permute-start | bytes 1572872 | tf_op jit(solution)/shard_map/ppermute | solution.py:320
  60.2 8.3 %collective-permute-done = bf16[64,4,8,128]{3,2,1,0:T(8,128)(2,1)} collective-permute-done((bf16[64,4,8,128]{3,2,1,0:T(8,128)(2,1)S(1)}, bf16[64,4,8,128]{3,2,1,0:T(8,128)(2,1)}, u32[]{:S(2)}, u32[]{:S(2)}) %collective-permute-start) | collective-permute-done | bytes 524320 | tf_op jit(solution)/shard_map/ppermute | solution.py:320
  68.5 4.8 %all-to-all-done.1 = bf16[64,4,8,128]{3,2,1,0:T(8,128)(2,1)S(1)} async-done(((bf16[64,4,8,128]{3,2,1,0:T(8,128)(2,1)}), bf16[64,4,8,128]{3,2,1,0:T(8,128)(2,1)S(1)}, u32[]{:S(2)}, u32[]{:S(2)}) %all-to-all-start.1) | async-done | bytes 524320 | tf_op jit(solution)/shard_map/all_to_all | solution.py:306
  73.3 2.9 %collective-permute-start.1 = (bf16[64,4,8,128]{3,2,1,0:T(8,128)(2,1)S(1)}, bf16[64,4,8,128]{3,2,1,0:T(8,128)(2,1)S(1)}, u32[]{:S(2)}, u32[]{:S(2)}) collective-permute-start(bf16[64,4,8,128]{3,2,1,0:T(8,128)(2,1)S(1)} %all-to-all-done.1), channel_id=1, source_target_pairs={{0,128},{64,192},{128,0},{192,64},{1,129},{65,193},{129,1},{193,65... | collective-permute-start | bytes 1572872 | tf_op jit(solution)/shard_map/ppermute | solution.py:326
  76.2 7.2 %all-to-all-start.2 = ((bf16[64,4,8,128]{3,2,1,0:T(8,128)(2,1)}), bf16[64,4,8,128]{3,2,1,0:T(8,128)(2,1)S(1)}, u32[]{:S(2)}, u32[]{:S(2)}) async-start(bf16[64,4,8,128]{3,2,1,0:T(8,128)(2,1)} %collective-permute-done), calls=%async_computation.2 | async-start | bytes 1048576 | tf_op jit(solution)/shard_map/all_to_all | solution.py:306
  83.4 4.1 %collective-permute-start.3 = (bf16[64,4,8,128]{3,2,1,0:T(8,128)(2,1)S(1)}, bf16[64,4,8,128]{3,2,1,0:T(8,128)(2,1)S(1)}, u32[]{:S(2)}, u32[]{:S(2)}) collective-permute-start(bf16[64,4,8,128]{3,2,1,0:T(8,128)(2,1)S(1)} %all-to-all-done.1), channel_id=1, source_target_pairs={{0,192},{64,0},{128,64},{192,128},{1,193},{65,1},{129,65},{193,129... | collective-permute-start | bytes 1572872 | tf_op jit(solution)/shard_map/ppermute | solution.py:326
  87.5 0.0 collective-permute-start.2
  87.5 0.5 collective-permute-done.1.refs_0_
  88.0 0.5 settle.1.win_ref
  88.5 11.1 %collective-permute-done.3 = bf16[64,4,8,128]{3,2,1,0:T(8,128)(2,1)S(1)} collective-permute-done((bf16[64,4,8,128]{3,2,1,0:T(8,128)(2,1)S(1)}, bf16[64,4,8,128]{3,2,1,0:T(8,128)(2,1)S(1)}, u32[]{:S(2)}, u32[]{:S(2)}) %collective-permute-start.3) | collective-permute-done | bytes 524320 | tf_op jit(solution)/shard_map/ppermute | solution.py:326
  99.6 1.9 %collective-permute-done.2 = bf16[64,4,8,128]{3,2,1,0:T(8,128)(2,1)S(1)} collective-permute-done((bf16[64,4,8,128]{3,2,1,0:T(8,128)(2,1)S(1)}, bf16[64,4,8,128]{3,2,1,0:T(8,128)(2,1)S(1)}, u32[]{:S(2)}, u32[]{:S(2)}) %collective-permute-start.2) | collective-permute-done | bytes 524320 | tf_op jit(solution)/shard_map/ppermute | solution.py:326
  101.4 0.0 all-to-all-done.2
  101.4 11.1 %correlate.1 = bf16[8,4,32,1024]{3,2,1,0:T(8,128)(2,1)} custom-call(s32[1]{0:T(128)} %settle.1.win_ref, bf16[2,8,4,4,8,128]{5,4,3,2,1,0:T(8,128)(2,1)S(1)} %bitcast.13, bf16[2,8,4,4,8,128]{5,4,3,2,1,0:T(8,128)(2,1)S(1)} %bitcast.12, bf16[2,8,4,4,8,128]{5,4,3,2,1,0:T(8,128)(2,1)S(1)} %bitcast.16, bf16[2,8,4,4,8,128]{5,4,3,2,1,0:T(8,128)(2,1)S(1)} %bitcast.14, ...), custom_call_target="tpu_custom_call" | custom-call | tf_op jit(solution)/shard_map/correlate/pallas_call | solution.py:244
  (7 shorter events, 0.1 us)
Async XLA Ops:
  2.7 44.4 %all-to-all-start = ((bf16[64,9,8,128]{3,2,1,0:T(8,128)(2,1)}), bf16[64,9,8,128]{3,2,1,0:T(8,128)(2,1)S(1)}, u32[]{:S(2)}, u32[]{:S(2)}) async-start(bf16[64,9,8,128]{3,2,1,0:T(8,128)(2,1)} %bitcast.18), calls=%async_computation | async-start | bytes 2359296 | tf_op jit(solution)/shard_map/all_to_all | solution.py:306
  49.8 23.5 %all-to-all-start.1 = ((bf16[64,4,8,128]{3,2,1,0:T(8,128)(2,1)}), bf16[64,4,8,128]{3,2,1,0:T(8,128)(2,1)S(1)}, u32[]{:S(2)}, u32[]{:S(2)}) async-start(bf16[64,4,8,128]{3,2,1,0:T(8,128)(2,1)} %get-tuple-element.16), calls=%async_computation.1 | async-start | bytes 1048576 | tf_op jit(solution)/shard_map/all_to_all | solution.py:306
  57.0 11.5 %collective-permute-start = (bf16[64,4,8,128]{3,2,1,0:T(8,128)(2,1)S(1)}, bf16[64,4,8,128]{3,2,1,0:T(8,128)(2,1)}, u32[]{:S(2)}, u32[]{:S(2)}) collective-permute-start(bf16[64,4,8,128]{3,2,1,0:T(8,128)(2,1)S(1)} %pick_first.1), channel_id=1, source_target_pairs={{0,0},{1,65},{2,130},{3,195},{4,4},{5,69},{6,134},{7,199},{8,8},{9... | collective-permute-start | bytes 1572872 | tf_op jit(solution)/shard_map/ppermute | solution.py:320
  73.3 14.7 %collective-permute-start.1 = (bf16[64,4,8,128]{3,2,1,0:T(8,128)(2,1)S(1)}, bf16[64,4,8,128]{3,2,1,0:T(8,128)(2,1)S(1)}, u32[]{:S(2)}, u32[]{:S(2)}) collective-permute-start(bf16[64,4,8,128]{3,2,1,0:T(8,128)(2,1)S(1)} %all-to-all-done.1), channel_id=1, source_target_pairs={{0,128},{64,192},{128,0},{192,64},{1,129},{65,193},{129,1},{193,65... | collective-permute-start | bytes 1572872 | tf_op jit(solution)/shard_map/ppermute | solution.py:326
  76.2 25.2 %all-to-all-start.2 = ((bf16[64,4,8,128]{3,2,1,0:T(8,128)(2,1)}), bf16[64,4,8,128]{3,2,1,0:T(8,128)(2,1)S(1)}, u32[]{:S(2)}, u32[]{:S(2)}) async-start(bf16[64,4,8,128]{3,2,1,0:T(8,128)(2,1)} %collective-permute-done), calls=%async_computation.2 | async-start | bytes 1048576 | tf_op jit(solution)/shard_map/all_to_all | solution.py:306
  83.4 16.1 %collective-permute-start.3 = (bf16[64,4,8,128]{3,2,1,0:T(8,128)(2,1)S(1)}, bf16[64,4,8,128]{3,2,1,0:T(8,128)(2,1)S(1)}, u32[]{:S(2)}, u32[]{:S(2)}) collective-permute-start(bf16[64,4,8,128]{3,2,1,0:T(8,128)(2,1)S(1)} %all-to-all-done.1), channel_id=1, source_target_pairs={{0,192},{64,0},{128,64},{192,128},{1,193},{65,1},{129,65},{193,129... | collective-permute-start | bytes 1572872 | tf_op jit(solution)/shard_map/ppermute | solution.py:326
  87.5 13.9 %collective-permute-start.2 = (bf16[64,4,8,128]{3,2,1,0:T(8,128)(2,1)S(1)}, bf16[64,4,8,128]{3,2,1,0:T(8,128)(2,1)S(1)}, u32[]{:S(2)}, u32[]{:S(2)}) collective-permute-start(bf16[64,4,8,128]{3,2,1,0:T(8,128)(2,1)S(1)} %all-to-all-done.1), channel_id=1, source_target_pairs={{0,64},{64,128},{128,192},{192,0},{1,65},{65,129},{129,193},{193,1... | collective-permute-start | bytes 1572872 | tf_op jit(solution)/shard_map/ppermute | solution.py:326

commit v13 on v9

--- a/solution.py
+++ b/solution.py
@@ -60,7 +60,7 @@
 def whiten_spread(win, spectra, sent, slots):
     blocks, _, parts, channels, bins = spectra.shape
     shape = (parts, bins // LANES, channels // GROUP, blocks + 1, GROUP, LANES)
-    steps = 2
+    steps = 1
     width = bins // steps
     return pl.pallas_call(
         whiten_kernel,

time: 113 us -> 114 us (level)
  no operation moved by 1% of the time
where the time goes in v13:
time: 114 us; the launch traced here: 112 us
  waiting for transfers between devices  37 us (32%)
  starting transfers between devices  36.9 us (32%)
  other arithmetic  19.8 us (17%)
  Pallas kernels  18.3 us (16%)
    all_to_all x3, starting transfers between devices, local(): lax.all_to_all(x, 'pair', split_axis=0, concat_axis=0, tiled=True)  26.4 us
    all_to_all x3, waiting for transfers between devices, local(): lax.all_to_all(x, 'pair', split_axis=0, concat_axis=0, tiled=True)  17.6 us
    another operation x1, other arithmetic  17.4 us
    ppermute x3, waiting for transfers between devices, local(): b.append(lax.ppermute(second, 'win', step))  11.1 us
    pallas_call x1, Pallas kernels, correlate(): pl.pallas_call(functools.partial(correlate_kernel, scaling), grid=(tiles...  11.1 us
    ppermute x1, waiting for transfers between devices, local(): first = lax.ppermute(first, ('win', 'pair'), turn)  8.29 us
    ppermute x3, starting transfers between devices, local(): b.append(lax.ppermute(second, 'win', step))  7.26 us
    ppermute x1, starting transfers between devices, local(): first = lax.ppermute(first, ('win', 'pair'), turn)  3.2 us
  transfers between devices with their start and end apart: 7, of which 6 were waited for; matrix products, arithmetic and copies ran while one was open for 18% of the time, Pallas kernels for 1%

profile of v13, /device:TPU:1, one launch (start us, length us, event | category | flops | bytes accessed | tf_op | source)
XLA Modules:
  0.0 112.2 jit_solution(12809724845078315057)
XLA Ops:
  0.0 3.0 %whiten_spread.1 = bf16[2,8,4,9,8,128]{5,4,3,2,1,0:T(8,128)(2,1)} custom-call(s32[1]{0:T(128)} %bitcast.win_ref, bf16[8,1,2,32,1024]{4,3,2,1,0:T(8,128)(2,1)} %x_ref.1, s32[2,64]{1,0:T(2,128)} %bitcast.17, s32[2,4]{1,0:T(2,128)} %bitcast.18), custom_call_target="tpu_custom_call" | custom-call | tf_op jit(solution)/shard_map/whiten_spread/pallas_call | solution.py:65
  3.0 13.0 %all-to-all-start = ((bf16[64,9,8,128]{3,2,1,0:T(8,128)(2,1)}), bf16[64,9,8,128]{3,2,1,0:T(8,128)(2,1)S(1)}, u32[]{:S(2)}, u32[]{:S(2)}) async-start(bf16[64,9,8,128]{3,2,1,0:T(8,128)(2,1)} %bitcast.16), calls=%async_computation | async-start | bytes 2359296 | tf_op jit(solution)/shard_map/all_to_all | solution.py:294
  16.0 17.4 %cosine_convert_fusion = (bf16[1024,1024]{1,0:T(8,128)(2,1)S(1)}, bf16[1024,1024]{1,0:T(8,128)(2,1)S(1)}) fusion(s32[1024]{0:T(1024)S(1)} %get-tuple-element.19, s32[1024]{0:T(1024)S(1)} %get-tuple-element.20), kind=kLoop, calls=%fused_computation.10 | loop fusion | flops 17825792 | bytes 4202496 | tf_op jit(solution)/shard_map/convert
  33.4 2.4 %pad_maximum_fusion.refs_4_ = bf16[2048,1024]{1,0:T(8,128)(2,1)} fusion(bf16[1024,1024]{1,0:T(8,128)(2,1)S(1)} %get-tuple-element.18, bf16[1024,1024]{1,0:T(8,128)(2,1)S(1)} %get-tuple-element.17), kind=kLoop, calls=%fused_computation.8 | loop fusion | flops 8388608 | bytes 8388608 | tf_op jit(solution)/shard_map/concatenate | solution.py:286
  35.8 11.5 %all-to-all-done.x_ref = bf16[64,9,8,128]{3,2,1,0:T(8,128)(2,1)S(1)} async-done(((bf16[64,9,8,128]{3,2,1,0:T(8,128)(2,1)}), bf16[64,9,8,128]{3,2,1,0:T(8,128)(2,1)S(1)}, u32[]{:S(2)}, u32[]{:S(2)}) %all-to-all-start) | async-done | bytes 1179680 | tf_op jit(solution)/shard_map/all_to_all | solution.py:294
  47.3 2.6 %pick_second.1 = (bf16[64,4,8,128]{3,2,1,0:T(8,128)(2,1)}, s32[8,128]{1,0:T(8,128)S(1)}) custom-call(bf16[64,9,8,128]{3,2,1,0:T(8,128)(2,1)S(1)} %all-to-all-done.x_ref), custom_call_target="tpu_custom_call" | custom-call | tf_op jit(solution)/shard_map/pick_second/pallas_call | solution.py:121
  50.0 6.2 %all-to-all-start.1 = ((bf16[64,4,8,128]{3,2,1,0:T(8,128)(2,1)}), bf16[64,4,8,128]{3,2,1,0:T(8,128)(2,1)S(1)}, u32[]{:S(2)}, u32[]{:S(2)}) async-start(bf16[64,4,8,128]{3,2,1,0:T(8,128)(2,1)} %get-tuple-element.12), calls=%async_computation.1 | async-start | bytes 1048576 | tf_op jit(solution)/shard_map/all_to_all | solution.py:294
  56.2 1.0 pick_first.1
  57.3 3.2 %collective-permute-start = (bf16[64,4,8,128]{3,2,1,0:T(8,128)(2,1)S(1)}, bf16[64,4,8,128]{3,2,1,0:T(8,128)(2,1)}, u32[]{:S(2)}, u32[]{:S(2)}) collective-permute-start(bf16[64,4,8,128]{3,2,1,0:T(8,128)(2,1)S(1)} %pick_first.1), channel_id=1, source_target_pairs={{0,0},{1,65},{2,130},{3,195},{4,4},{5,69},{6,134},{7,199},{8,8},{9... | collective-permute-start | bytes 1572872 | tf_op jit(solution)/shard_map/ppermute | solution.py:308
  60.5 8.3 %collective-permute-done = bf16[64,4,8,128]{3,2,1,0:T(8,128)(2,1)} collective-permute-done((bf16[64,4,8,128]{3,2,1,0:T(8,128)(2,1)S(1)}, bf16[64,4,8,128]{3,2,1,0:T(8,128)(2,1)}, u32[]{:S(2)}, u32[]{:S(2)}) %collective-permute-start) | collective-permute-done | bytes 524320 | tf_op jit(solution)/shard_map/ppermute | solution.py:308
  68.8 4.8 %all-to-all-done.1 = bf16[64,4,8,128]{3,2,1,0:T(8,128)(2,1)S(1)} async-done(((bf16[64,4,8,128]{3,2,1,0:T(8,128)(2,1)}), bf16[64,4,8,128]{3,2,1,0:T(8,128)(2,1)S(1)}, u32[]{:S(2)}, u32[]{:S(2)}) %all-to-all-start.1) | async-done | bytes 524320 | tf_op jit(solution)/shard_map/all_to_all | solution.py:294
  73.5 2.9 %collective-permute-start.1 = (bf16[64,4,8,128]{3,2,1,0:T(8,128)(2,1)S(1)}, bf16[64,4,8,128]{3,2,1,0:T(8,128)(2,1)S(1)}, u32[]{:S(2)}, u32[]{:S(2)}) collective-permute-start(bf16[64,4,8,128]{3,2,1,0:T(8,128)(2,1)S(1)} %all-to-all-done.1), channel_id=1, source_target_pairs={{0,128},{64,192},{128,0},{192,64},{1,129},{65,193},{129,1},{193,65... | collective-permute-start | bytes 1572872 | tf_op jit(solution)/shard_map/ppermute | solution.py:314
  76.4 7.2 %all-to-all-start.2 = ((bf16[64,4,8,128]{3,2,1,0:T(8,128)(2,1)}), bf16[64,4,8,128]{3,2,1,0:T(8,128)(2,1)S(1)}, u32[]{:S(2)}, u32[]{:S(2)}) async-start(bf16[64,4,8,128]{3,2,1,0:T(8,128)(2,1)} %collective-permute-done), calls=%async_computation.2 | async-start | bytes 1048576 | tf_op jit(solution)/shard_map/all_to_all | solution.py:294
  83.7 3.0 %collective-permute-start.2 = (bf16[64,4,8,128]{3,2,1,0:T(8,128)(2,1)S(1)}, bf16[64,4,8,128]{3,2,1,0:T(8,128)(2,1)S(1)}, u32[]{:S(2)}, u32[]{:S(2)}) collective-permute-start(bf16[64,4,8,128]{3,2,1,0:T(8,128)(2,1)S(1)} %all-to-all-done.1), channel_id=1, source_target_pairs={{0,64},{64,128},{128,192},{192,0},{1,65},{65,129},{129,193},{193,1... | collective-permute-start | bytes 1572872 | tf_op jit(solution)/shard_map/ppermute | solution.py:314
  86.7 1.3 %collective-permute-start.3 = (bf16[64,4,8,128]{3,2,1,0:T(8,128)(2,1)S(1)}, bf16[64,4,8,128]{3,2,1,0:T(8,128)(2,1)S(1)}, u32[]{:S(2)}, u32[]{:S(2)}) collective-permute-start(bf16[64,4,8,128]{3,2,1,0:T(8,128)(2,1)S(1)} %all-to-all-done.1), channel_id=1, source_target_pairs={{0,192},{64,0},{128,64},{192,128},{1,193},{65,1},{129,65},{193,129... | collective-permute-start | bytes 1572872 | tf_op jit(solution)/shard_map/ppermute | solution.py:314
  88.0 0.2 collective-permute-done.1.refs_0_
  88.2 0.5 settle.1.win_ref
  88.8 10.9 %collective-permute-done.2 = bf16[64,4,8,128]{3,2,1,0:T(8,128)(2,1)S(1)} collective-permute-done((bf16[64,4,8,128]{3,2,1,0:T(8,128)(2,1)S(1)}, bf16[64,4,8,128]{3,2,1,0:T(8,128)(2,1)S(1)}, u32[]{:S(2)}, u32[]{:S(2)}) %collective-permute-start.2) | collective-permute-done | bytes 524320 | tf_op jit(solution)/shard_map/ppermute | solution.py:314
  99.6 0.0 collective-permute-done.3
  99.6 1.3 %all-to-all-done.2 = bf16[64,4,8,128]{3,2,1,0:T(8,128)(2,1)S(1)} async-done(((bf16[64,4,8,128]{3,2,1,0:T(8,128)(2,1)}), bf16[64,4,8,128]{3,2,1,0:T(8,128)(2,1)S(1)}, u32[]{:S(2)}, u32[]{:S(2)}) %all-to-all-start.2) | async-done | bytes 524320 | tf_op jit(solution)/shard_map/all_to_all | solution.py:294
  101.0 11.1 %correlate.1 = bf16[8,4,32,1024]{3,2,1,0:T(8,128)(2,1)} custom-call(s32[1]{0:T(128)} %settle.1.win_ref, bf16[2,8,4,4,8,128]{5,4,3,2,1,0:T(8,128)(2,1)S(1)} %bitcast.12, bf16[2,8,4,4,8,128]{5,4,3,2,1,0:T(8,128)(2,1)S(1)} %bitcast.11, bf16[2,8,4,4,8,128]{5,4,3,2,1,0:T(8,128)(2,1)S(1)} %bitcast.14, bf16[2,8,4,4,8,128]{5,4,3,2,1,0:T(8,128)(2,1)S(1)} %bitcast.13, ...), custom_call_target="tpu_custom_call" | custom-call | tf_op jit(solution)/shard_map/correlate/pallas_call | solution.py:244
  (1 shorter events, 0.0 us)
Async XLA Ops:
  3.0 44.4 %all-to-all-start = ((bf16[64,9,8,128]{3,2,1,0:T(8,128)(2,1)}), bf16[64,9,8,128]{3,2,1,0:T(8,128)(2,1)S(1)}, u32[]{:S(2)}, u32[]{:S(2)}) async-start(bf16[64,9,8,128]{3,2,1,0:T(8,128)(2,1)} %bitcast.16), calls=%async_computation | async-start | bytes 2359296 | tf_op jit(solution)/shard_map/all_to_all | solution.py:294
  50.0 23.5 %all-to-all-start.1 = ((bf16[64,4,8,128]{3,2,1,0:T(8,128)(2,1)}), bf16[64,4,8,128]{3,2,1,0:T(8,128)(2,1)S(1)}, u32[]{:S(2)}, u32[]{:S(2)}) async-start(bf16[64,4,8,128]{3,2,1,0:T(8,128)(2,1)} %get-tuple-element.12), calls=%async_computation.1 | async-start | bytes 1048576 | tf_op jit(solution)/shard_map/all_to_all | solution.py:294
  57.3 11.5 %collective-permute-start = (bf16[64,4,8,128]{3,2,1,0:T(8,128)(2,1)S(1)}, bf16[64,4,8,128]{3,2,1,0:T(8,128)(2,1)}, u32[]{:S(2)}, u32[]{:S(2)}) collective-permute-start(bf16[64,4,8,128]{3,2,1,0:T(8,128)(2,1)S(1)} %pick_first.1), channel_id=1, source_target_pairs={{0,0},{1,65},{2,130},{3,195},{4,4},{5,69},{6,134},{7,199},{8,8},{9... | collective-permute-start | bytes 1572872 | tf_op jit(solution)/shard_map/ppermute | solution.py:308
  73.5 14.7 %collective-permute-start.1 = (bf16[64,4,8,128]{3,2,1,0:T(8,128)(2,1)S(1)}, bf16[64,4,8,128]{3,2,1,0:T(8,128)(2,1)S(1)}, u32[]{:S(2)}, u32[]{:S(2)}) collective-permute-start(bf16[64,4,8,128]{3,2,1,0:T(8,128)(2,1)S(1)} %all-to-all-done.1), channel_id=1, source_target_pairs={{0,128},{64,192},{128,0},{192,64},{1,129},{65,193},{129,1},{193,65... | collective-permute-start | bytes 1572872 | tf_op jit(solution)/shard_map/ppermute | solution.py:314
  76.4 24.5 %all-to-all-start.2 = ((bf16[64,4,8,128]{3,2,1,0:T(8,128)(2,1)}), bf16[64,4,8,128]{3,2,1,0:T(8,128)(2,1)S(1)}, u32[]{:S(2)}, u32[]{:S(2)}) async-start(bf16[64,4,8,128]{3,2,1,0:T(8,128)(2,1)} %collective-permute-done), calls=%async_computation.2 | async-start | bytes 1048576 | tf_op jit(solution)/shard_map/all_to_all | solution.py:294
  83.7 16.0 %collective-permute-start.2 = (bf16[64,4,8,128]{3,2,1,0:T(8,128)(2,1)S(1)}, bf16[64,4,8,128]{3,2,1,0:T(8,128)(2,1)S(1)}, u32[]{:S(2)}, u32[]{:S(2)}) collective-permute-start(bf16[64,4,8,128]{3,2,1,0:T(8,128)(2,1)S(1)} %all-to-all-done.1), channel_id=1, source_target_pairs={{0,64},{64,128},{128,192},{192,0},{1,65},{65,129},{129,193},{193,1... | collective-permute-start | bytes 1572872 | tf_op jit(solution)/shard_map/ppermute | solution.py:314
  86.7 12.9 %collective-permute-start.3 = (bf16[64,4,8,128]{3,2,1,0:T(8,128)(2,1)S(1)}, bf16[64,4,8,128]{3,2,1,0:T(8,128)(2,1)S(1)}, u32[]{:S(2)}, u32[]{:S(2)}) collective-permute-start(bf16[64,4,8,128]{3,2,1,0:T(8,128)(2,1)S(1)} %all-to-all-done.1), channel_id=1, source_target_pairs={{0,192},{64,0},{128,64},{192,128},{1,193},{65,1},{129,65},{193,129... | collective-permute-start | bytes 1572872 | tf_op jit(solution)/shard_map/ppermute | solution.py:314
